TPU v7x, 256 devices: a whole 4x4x8 slice. The times are simulated.
256 devices in a mesh: sec: 4 (over x_lo, core), dev: 64 (over x_hi, z, y).
Axes of the slice: x: 4 (x_hi: 2, x_lo: 2; x = x_hi * 2 + x_lo), y: 4, z: 8, core: 2. Of those that a mesh axis runs over, the one named last changes fastest.
Arguments:
- queries: bfloat16 [256, 128, 576], P(('sec', 'dev')), may hold values from -56 to 56
- latent_cache: bfloat16 [256, 4096, 576], P(('sec', 'dev')), may hold values from -4 to 4
- cache_lengths: int32 [256], P(('sec', 'dev')), may hold values from 512 to 4096, as said below
- stream: bfloat16 [512, 7168], P('dev'), may hold values from -6 to 6
- norm_gain: float32 [7168], replicated, may hold values from 0.1 to 1.9
- expert_ids: int32 [512, 8], P('dev'), may hold values from 0 to 15, all different within a row; in each aligned block of 8 rows (0 to 7, 8 to 15, ...) at most 5 rows name the same one
- route_weights: float32 [512, 8], P('dev'), may hold values from 0.1 to 1
- w_gate: bfloat16 [64, 7168, 512], P('dev', None, 'sec'), may hold values from -0.0625 to 0.0625
- w_up: bfloat16 [64, 7168, 512], P('dev', None, 'sec'), may hold values from -0.0625 to 0.0625
- w_down: bfloat16 [64, 512, 7168], P('dev', 'sec'), may hold values from -0.125 to 0.125
Outputs:
- context: bfloat16 [256, 128, 512], P(('sec', 'dev'))
- mixed: bfloat16 [512, 7168], P('dev')
Inputs may be any that keep to these rules, and one draw needn't show every extreme that they name: `expert_ids`: each row names 8 distinct experts; within the 8 rows of one group no expert is named more than 5 times, a bound that some block reaches. `cache_lengths`: the longest sequence holds 4096 positions.
All inputs are finite; a program needn't handle non-finite values.
Results may differ from a plain program's by a relative error of at most 0.015.
Values may be sent and summed in bfloat16 or wider, within the bound.
No kernel may reach another device: no remote copies, remote signals or barrier semaphores. Data moves between devices by JAX's collectives and lax.ppermute only.
A program may use at most 128 MiB of HBM per device.

v0:
```python
import jax
import jax.numpy as jnp
from jax import lax
from jax.sharding import PartitionSpec as P

MOE_HIDDEN = 2048
LATENT = 512
HID_DEV = 128


score_scale = 192.0 ** (-0.5)


def slot_table(choices, count, capacity):
    experts = jnp.arange(count, dtype=jnp.int32)
    hit_count = jnp.sum((choices[..., None] == experts).astype(jnp.float32), axis=2)
    before = jnp.cumsum(hit_count, axis=1) - hit_count
    slot_ids = jnp.arange(capacity).astype(jnp.float32)
    picked = hit_count[..., None] * (before[..., None] == slot_ids).astype(jnp.float32)
    return (jnp.transpose(picked, (0, 2, 3, 1)), hit_count)


def local(
    queries,
    latent_cache,
    cache_lengths,
    stream,
    norm_gain,
    expert_ids,
    route_weights,
    w_gate,
    w_up,
    w_down,
):
    scores = (
        jnp.einsum("shk,slk->shl", queries, latent_cache, preferred_element_type=jnp.float32)
        * score_scale
    )
    visible = (
        jnp.arange(latent_cache.shape[1], dtype=jnp.int32)[None, None, :]
        < cache_lengths[:, None, None]
    )
    scores = jnp.where(visible, scores, jnp.float32(-1e30))
    peak = jnp.max(scores, axis=2, keepdims=True)
    powered = jnp.exp(scores - peak)
    probs = (powered / jnp.sum(powered, axis=2, keepdims=True)).astype(jnp.bfloat16)
    context = jnp.einsum(
        "shl,slk->shk", probs, latent_cache[:, :, :LATENT], preferred_element_type=jnp.float32
    ).astype(jnp.bfloat16)
    dev_count = lax.axis_size("dev")
    sec_count = lax.axis_size("sec")
    group_size = MOE_HIDDEN // (HID_DEV * sec_count)
    expert_count = dev_count // group_size
    row_count = stream.shape[0]
    top_count = expert_ids.shape[1]
    capacity = max(2, row_count * top_count * 5 // (4 * expert_count))
    width = stream.shape[1]
    stream_f = stream.astype(jnp.float32)
    scale_rows = lax.rsqrt(jnp.mean(stream_f * stream_f, axis=1, keepdims=True) + 1e-06)
    normed = (stream_f * scale_rows * norm_gain).astype(jnp.bfloat16)
    own_table, hit_count = slot_table(expert_ids[None], expert_count, capacity)
    own_table = own_table[0]
    all_rows, all_ids = (
        lax.all_gather(normed, "dev", axis=0, tiled=True),
        lax.all_gather(expert_ids, "dev", axis=0, tiled=True),
    )
    own_expert = lax.axis_index("dev") // group_size
    grouped_ids = all_ids.reshape(dev_count, row_count, top_count)
    named = jnp.sum((grouped_ids == own_expert).astype(jnp.float32), axis=2)
    before = jnp.cumsum(named, axis=1) - named
    slot_ids = jnp.arange(capacity).astype(jnp.float32)
    picked = named[:, None, :] * (before[:, None, :] == slot_ids[None, :, None]).astype(jnp.float32)
    received = jnp.einsum(
        "gjr,grd->gjd",
        picked.astype(jnp.bfloat16),
        all_rows.reshape(dev_count, row_count, width),
        preferred_element_type=jnp.float32,
    ).astype(jnp.bfloat16)
    slot_flat = received.reshape(dev_count * capacity, width)
    gate_proj = jnp.dot(slot_flat, w_gate[0], preferred_element_type=jnp.float32)
    up_proj = jnp.dot(slot_flat, w_up[0], preferred_element_type=jnp.float32)
    hidden = (jax.nn.silu(gate_proj) * up_proj).astype(jnp.bfloat16)
    partial_value = jnp.dot(hidden, w_down[0], preferred_element_type=jnp.float32).astype(
        jnp.bfloat16
    )
    experts = jnp.arange(expert_count, dtype=jnp.int32)
    weight_table = jnp.sum(
        route_weights[..., None] * (expert_ids[..., None] == experts).astype(jnp.float32), axis=1
    )
    weighted = own_table * jnp.transpose(weight_table)[:, None, :]
    returned = lax.all_to_all(
        partial_value.reshape(dev_count, capacity, width),
        "dev",
        split_axis=0,
        concat_axis=0,
        tiled=True,
    )
    block_sums = jnp.sum(
        returned.reshape(expert_count, group_size, capacity, width), axis=1, dtype=jnp.float32
    )
    section_part = jnp.einsum("ejr,ejd->rd", weighted, block_sums, precision=lax.Precision.HIGHEST)
    section_total = lax.psum(section_part.astype(jnp.bfloat16), "sec").astype(jnp.float32)
    mixed = (stream_f + section_total).astype(jnp.bfloat16)
    return (context, mixed)


def solution(mesh):
    return jax.shard_map(
        local,
        mesh=mesh,
        in_specs=(
            P(("sec", "dev"), None, None),
            P(("sec", "dev"), None, None),
            P(("sec", "dev")),
            P("dev", None),
            P(),
            P("dev", None),
            P("dev", None),
            P("dev", None, "sec"),
            P("dev", None, "sec"),
            P("dev", "sec", None),
        ),
        out_specs=(P(("sec", "dev"), None, None), P("dev", None)),
        check_vma=False,
    )
```

profile of v0, /device:TPU:1, one launch (start us, length us, event | category | flops | bytes accessed | tf_op | source)
XLA Modules:
  0.0 435.7 jit_solution(7749568602587736564)
XLA Ops:
  7.2 0.0 copy-start
  7.2 0.0 all-gather.2.cloned.1.call-start
  7.2 1.2 fusion.30
  8.4 1.6 fusion.32
  10.1 0.0 all-gather.2.cloned.1.call-update
  10.1 160.0 %all_gather.6 = s32[512,8]{1,0:T(8,128)S(1)} all-gather(s32[8,8]{1,0:T(8,128)} %param.15), channel_id=1, replica_groups=mesh['sec'=4,'dev'=64] {'dev'}, dimensions={0}, use_global_device_ids=true | all-gather | bytes 16640 | tf_op jit(solution)/shard_map/all_gather | solution.py:65
  170.1 0.1 convert_reduce_fusion.1
  170.3 0.1 reduce_window_sum.25
  170.4 0.2 reduce_window_sum.26
  170.6 0.0 all-gather.2.cloned.1.call-done
  170.6 8.2 %convolution_convert_fusion = bf16[64,5,7168]{2,1,0:T(8,128)(2,1)} fusion(bf16[512,7168]{1,0:T(8,128)(2,1)} %all-gather.2.cloned.1.call-done, f32[64,8]{1,0:T(8,128)S(1)} %reduce_window_sum.25, f32[64,8]{1,0:T(8,128)S(1)} %sub.33, f32[5]{0:T(128)S(1)} %iota_convert_fusion), kind=kOutput, calls=%fused_computation.1 | convolution fusion | flops 38999040 | bytes 11931668 | tf_op jit(solution)/shard_map/gjr,grd->gjd/dot_general | solution.py:73
  178.7 8.2 %reshape.143 = bf16[320,7168]{1,0:T(8,128)(2,1)} reshape(bf16[64,5,7168]{2,1,0:T(8,128)(2,1)} %convolution_convert_fusion) | data formatting | bytes 9175040 | tf_op jit(solution)/shard_map/reshape | solution.py:79
  187.0 4.2 fusion.12
  191.2 0.0 copy-done
  191.2 9.9 %convolution_convert_fusion.1 = bf16[320,7168]{1,0:T(8,128)(2,1)} fusion(bf16[1,128,7168]{2,1,0:T(8,128)(2,1)S(1)} %copy-done, bf16[320,7168]{1,0:T(8,128)(2,1)} %reshape.143, bf16[1,7168,128]{2,1,0:T(8,128)(2,1)} %param.18, f32[320,128]{1,0:T(8,128)S(1)} %fusion.12), kind=kOutput, calls=%fused_computation.2 | convolution fusion | flops 1176944640 | bytes 13008896 | tf_op jit(solution)/shard_map/dot_general | solution.py:83
  201.1 8.0 %reshape.144 = bf16[64,5,7168]{2,1,0:T(8,128)(2,1)} reshape(bf16[320,7168]{1,0:T(8,128)(2,1)} %convolution_convert_fusion.1) | data formatting | bytes 9175040 | tf_op jit(solution)/shard_map/reshape | solution.py:92
  209.1 0.0 copy-start.4
  209.1 0.0 copy-start.5
  209.1 0.0 copy-start.3
  209.1 5.9 %all-to-all-start = ((bf16[64,5,7168]{2,1,0:T(8,128)(2,1)}), bf16[64,5,7168]{2,1,0:T(8,128)(2,1)}, u32[]{:S(2)}, u32[]{:S(2)}) async-start(bf16[64,5,7168]{2,1,0:T(8,128)(2,1)} %reshape.144), calls=%async_computation | async-start | bytes 14680064 | tf_op jit(solution)/shard_map/all_to_all | solution.py:91
  215.0 0.2 all-reduce.2.cloned.1.call-start
  215.2 0.0 copy-done.4
  215.2 0.1 convert_reduce_fusion.2
  216.0 0.0 copy-done.5
  216.0 0.1 select_reduce_fusion
  216.1 0.0 copy-done.3
  216.1 3.5 fusion.55
  219.6 0.0 copy-start.1
  219.6 1.3 copy-done.1
  220.9 0.4 fusion.8
  221.3 126.4 %all-to-all-done = bf16[64,5,7168]{2,1,0:T(8,128)(2,1)} async-done(((bf16[64,5,7168]{2,1,0:T(8,128)(2,1)}), bf16[64,5,7168]{2,1,0:T(8,128)(2,1)}, u32[]{:S(2)}, u32[]{:S(2)}) %all-to-all-start) | async-done | bytes 4587552 | tf_op jit(solution)/shard_map/all_to_all | solution.py:91
  347.7 5.4 %convert_reduce_fusion = f32[16,5,7168]{2,1,0:T(8,128)S(1)} fusion(bf16[64,5,7168]{2,1,0:T(8,128)(2,1)} %all-to-all-done), kind=kLoop, calls=%fused_computation | loop fusion | flops 4014080 | bytes 6881280 | tf_op jit(solution)/shard_map/reduce_sum | solution.py:98
  353.1 4.2 fusion
  357.3 0.0 all-reduce.2.cloned.1.call-update
  357.4 0.0 copy-start.2
  357.4 5.1 %fusion.20 = bf16[1,128,512]{2,1,0:T(8,128)(2,1)} fusion(bf16[1,4096,576]{1,2,0:T(8,128)(2,1)} %param.11, f32[128,4096]{1,0:T(8,128)} %copy-done.1, f32[128]{0:T(128)S(1)} %fusion.8, f32[128]{0:T(128)S(1)} %get-tuple-element.2), kind=kOutput, calls=%fused_computation.23 | convolution fusion | flops 538509312 | bytes 6423552 | tf_op jit(solution)/shard_map/shl,slk->shk/dot_general | solution.py:47
  362.4 64.9 %all-reduce.2.cloned.1.call-done = bf16[8,7168]{1,0:T(8,128)(2,1)} async-done(((bf16[8,7168]{1,0:T(8,128)(2,1)}), bf16[8,7168]{1,0:T(8,128)(2,1)}) %all-reduce.2.cloned.1.call-update) | async-done | bytes 114704 | tf_op jit(solution)/shard_map/psum | solution.py:102
  427.3 0.0 copy-done.2
  427.3 1.6 fusion.33
  (6 shorter events, 0.1 us)
Async XLA Ops:
  7.2 184.0 %copy-start = (bf16[1,128,7168]{2,1,0:T(8,128)(2,1)S(1)}, bf16[1,128,7168]{2,1,0:T(8,128)(2,1)}, u32[]{:S(2)}) copy-start(bf16[1,128,7168]{2,1,0:T(8,128)(2,1)} %param.19) | copy-start | bytes 5505028
  7.2 163.4 %all-gather.2.cloned.1.call-start = ((), (), s32[]{:S(2)}) async-start(), calls=%async_computation.1 | async-start | bytes 7454720 | tf_op jit(solution)/shard_map/all_gather | solution.py:64
  209.1 6.1 %copy-start.4 = (s32[8,8]{1,0:T(8,128)S(1)}, s32[8,8]{1,0:T(8,128)}, u32[]{:S(2)}) copy-start(s32[8,8]{1,0:T(8,128)} %param.15) | copy-start | bytes 772
  209.1 6.9 %copy-start.5 = (f32[8,8]{1,0:T(8,128)S(1)}, f32[8,8]{1,0:T(8,128)}, u32[]{:S(2)}) copy-start(f32[8,8]{1,0:T(8,128)} %param.16) | copy-start | bytes 772
  209.1 7.0 %copy-start.3 = (bf16[1,128,576]{1,2,0:T(8,128)(2,1)S(1)}, bf16[1,128,576]{1,2,0:T(8,128)(2,1)}, u32[]{:S(2)}) copy-start(bf16[1,128,576]{1,2,0:T(8,128)(2,1)} %param.10) | copy-start | bytes 442372
  209.1 138.6 %all-to-all-start = ((bf16[64,5,7168]{2,1,0:T(8,128)(2,1)}), bf16[64,5,7168]{2,1,0:T(8,128)(2,1)}, u32[]{:S(2)}, u32[]{:S(2)}) async-start(bf16[64,5,7168]{2,1,0:T(8,128)(2,1)} %reshape.144), calls=%async_computation | async-start | bytes 14680064 | tf_op jit(solution)/shard_map/all_to_all | solution.py:91
  215.0 212.3 %all-reduce.2.cloned.1.call-start = ((), (), s32[]{:S(2)}) async-start(), calls=%async_computation.2 | async-start | bytes 229376 | tf_op jit(solution)/shard_map/psum | solution.py:102
  219.6 1.3 copy-start.1
  357.4 69.9 %copy-start.2 = (bf16[8,7168]{1,0:T(8,128)(2,1)S(1)}, bf16[8,7168]{1,0:T(8,128)(2,1)}, u32[]{:S(2)}) copy-start(bf16[8,7168]{1,0:T(8,128)(2,1)} %param.13) | copy-start | bytes 344068
Sparse Core Ops, SparseCore 0:
  12.2 145.7 all-gather.1
  357.5 69.7 all-reduce.1
where the time goes:
time: 436 us
  waiting for transfers between devices  191 us (44%)
  blocking collectives  160 us (37%)
  matrix products  35 us (8%)
  local copies, waits for them, and re-layouts  17.6 us (4%)
  between operations  14.8 us (3%)
  other arithmetic  10.8 us (2%)
  starting transfers between devices  6.12 us (1%)
    all_gather x1, blocking collectives, local(): lax.all_gather(expert_ids, 'dev', axis=0, tiled=True)  160 us
    all_to_all x1, waiting for transfers between devices, local(): lax.all_to_all(partial_value.reshape(dev_count, capacity, width), 'dev',...  126 us
    psum x1, waiting for transfers between devices, local(): lax.psum(section_part.astype(jnp.bfloat16), 'sec').astype(jnp.float32)  64.9 us
    dot_general x1, matrix products, local(): jnp.dot(hidden, w_down[0], preferred_element_type=jnp.float32)  9.9 us
  transfers between devices with their start and end apart: 3, of which 2 were waited for; matrix products, arithmetic and copies ran while one was open for 2% of the time, Pallas kernels for 0%

commit v1 on v0

v1 whole, which is shorter than its diff:
```python
import functools

import jax
import jax.numpy as jnp
from jax import lax
from jax.experimental import pallas as pl
from jax.experimental.pallas import tpu as pltpu
from jax.sharding import PartitionSpec as P

LATENT = 512
CAP = 5
ROWS = 8
WIDTH = 7168
HALF = 3584
SLOTS = 40
score_scale = 192.0 ** (-0.5)

SIZES = (2, 2, 2, 8, 4)


def pairs(move):
    out = []
    for xl in range(2):
        for c in range(2):
            for xh in range(2):
                for z in range(8):
                    for y in range(4):
                        place = (xl, c, xh, z, y)
                        lin = []
                        for spot in (place, move(*place)):
                            at = 0
                            for part, size in zip(spot, SIZES):
                                at = at * size + part % size
                            lin.append(at)
                        out.append(tuple(lin))
    return out


def send(value, move):
    return lax.ppermute(value, ("sec", "dev"), pairs(move))


def swap_core(value):
    return send(value, lambda xl, c, xh, z, y: (xl, 1 - c, xh, z, y))


def z_step(c, k):
    return k if c == 0 else -(k + 1)


def spread(value, k, sign):
    return send(
        value, lambda xl, c, xh, z, y: (xl, c, xh ^ xl, z + sign * z_step(c, k), y)
    )


def across(value, dxl, dy):
    return send(value, lambda xl, c, xh, z, y: (xl ^ dxl, c, xh, z, y + dy))


ORDER = (3, 2, 1, 0)
DELTAS = ((1, 2), (1, 1), (1, 3), (0, 2), (0, 1), (0, 3), (1, 0))


def pick_kernel(at_ref, r0, r1, r2, r3, gain_ref, keep_ref, send_ref, table_ref):
    core = at_ref[0]
    expert = at_ref[1].astype(jnp.float32)
    rows = (r0, r1, r2, r3)
    named = []
    scale = []
    for r in rows:
        ids = r[:, WIDTH:].astype(jnp.float32)
        named.append(jnp.sum((ids == expert).astype(jnp.float32), axis=1, keepdims=True))
        x = r[:, :WIDTH].astype(jnp.float32)
        scale.append(lax.rsqrt(jnp.sum(x * x, axis=1, keepdims=True) / WIDTH + 1e-06))
    named = jnp.concatenate(named, axis=0)
    scale = jnp.concatenate(scale, axis=0)
    count = 4 * ROWS
    row = lax.broadcasted_iota(jnp.int32, (count, count), 0)
    col = lax.broadcasted_iota(jnp.int32, (count, count), 1)
    earlier = ((col < row) & ((col // ROWS) == (row // ROWS))).astype(jnp.float32)
    named = jnp.broadcast_to(named, (count, 128))
    before = jnp.dot(earlier, named, preferred_element_type=jnp.float32)
    group = lax.broadcasted_iota(jnp.int32, (count, 128), 0) // ROWS
    lane = lax.broadcasted_iota(jnp.int32, (count, 128), 1)
    place = (group * CAP + core * (4 * CAP)).astype(jnp.float32) + before
    hit = (named > 0.5) & (before < CAP - 0.5) & (lane.astype(jnp.float32) == place)
    table = hit.astype(jnp.bfloat16)
    table_ref[...] = table
    wide = WIDTH // 4
    for part in range(4):
        cols = pl.ds(part * wide, wide)
        x = jnp.concatenate([r[:, cols].astype(jnp.float32) for r in rows], axis=0)
        normed = (x * scale * gain_ref[:, cols]).astype(jnp.bfloat16)
        slots = lax.dot_general(
            table, normed, (((0,), (0,)), ((), ())), preferred_element_type=jnp.float32
        )[:SLOTS].astype(jnp.bfloat16)
        inner = pl.ds((part % 2) * wide, wide)

        @pl.when(core == part // 2)
        def _():
            keep_ref[:, inner] = slots

        @pl.when(core != part // 2)
        def _():
            send_ref[:, inner] = slots


def pick(at, rows, gain):
    vmem = pl.BlockSpec(memory_space=pltpu.VMEM)
    return pl.pallas_call(
        pick_kernel,
        out_shape=(
            jax.ShapeDtypeStruct((SLOTS, HALF), jnp.bfloat16),
            jax.ShapeDtypeStruct((SLOTS, HALF), jnp.bfloat16),
            jax.ShapeDtypeStruct((4 * ROWS, 128), jnp.bfloat16),
        ),
        in_specs=[pl.BlockSpec(memory_space=pltpu.SMEM)] + [vmem] * 5,
        out_specs=(vmem, vmem, vmem),
        cost_estimate=pl.CostEstimate(
            flops=2 * 128 * 32 * WIDTH, bytes_accessed=2 * 72 * WIDTH, transcendentals=32
        ),
        compiler_params=pltpu.CompilerParams(vmem_limit_bytes=16 * 1024 * 1024),
    )(at, *rows, gain)


def attend(queries, latent_cache, cache_lengths):
    scores = (
        jnp.einsum("shk,slk->shl", queries, latent_cache, preferred_element_type=jnp.float32)
        * score_scale
    )
    visible = (
        jnp.arange(latent_cache.shape[1], dtype=jnp.int32)[None, None, :]
        < cache_lengths[:, None, None]
    )
    scores = jnp.where(visible, scores, jnp.float32(-1e30))
    peak = jnp.max(scores, axis=2, keepdims=True)
    powered = jnp.exp(scores - peak)
    probs = (powered / jnp.sum(powered, axis=2, keepdims=True)).astype(jnp.bfloat16)
    return jnp.einsum(
        "shl,slk->shk", probs, latent_cache[:, :, :LATENT], preferred_element_type=jnp.float32
    ).astype(jnp.bfloat16)


def local(
    queries,
    latent_cache,
    cache_lengths,
    stream,
    norm_gain,
    expert_ids,
    route_weights,
    w_gate,
    w_up,
    w_down,
):
    sec = lax.axis_index("sec")
    dev = lax.axis_index("dev")
    xl, core = sec // 2, sec % 2
    xh, z = dev // 32, (dev // 4) % 8
    expert = xh * 8 + z

    ids_wide = jnp.pad(expert_ids.astype(jnp.bfloat16), ((0, 0), (0, 120)), constant_values=-1)
    block = jnp.concatenate([stream, ids_wide], axis=1)
    arrived = {k: spread(block, k, 1) for k in ORDER}

    gate_halves = w_gate[0].reshape(2, HALF, 128)
    up_halves = w_up[0].reshape(2, HALF, 128)
    down_halves = w_down[0].reshape(128, 2, HALF)

    def half(array, which, axis):
        return lax.dynamic_index_in_dim(array, which, axis, keepdims=False)

    w_own = jnp.concatenate([half(gate_halves, core, 0), half(up_halves, core, 0)], axis=1)
    w_send = jnp.concatenate([half(gate_halves, 1 - core, 0), half(up_halves, 1 - core, 0)], axis=1)
    w_other = swap_core(w_send)
    down_own = half(down_halves, core, 1)
    down_other = swap_core(half(down_halves, 1 - core, 1))

    context = attend(queries, latent_cache, cache_lengths)

    at = jnp.stack([core, expert]).astype(jnp.int32)
    keep, give, table = pick(at, [arrived[k] for k in range(4)], norm_gain[None, :])
    mine = keep + swap_core(give)

    blocks = [mine] + [across(mine, dxl, dy) for dxl, dy in DELTAS]

    def experts(part):
        x = jnp.concatenate(part, axis=0)
        own = jnp.dot(x, w_own, preferred_element_type=jnp.float32)
        other = jnp.dot(x, w_other, preferred_element_type=jnp.float32)
        got = swap_core(jnp.concatenate([own, other], axis=1))
        own = own + got[:, 256:]
        other = other + got[:, :256]
        hidden = jnp.concatenate(
            [
                (jax.nn.silu(v[:, :128]) * v[:, 128:]).astype(jnp.bfloat16)
                for v in (own, other)
            ],
            axis=1,
        )
        down = jnp.concatenate([down_own, down_other], axis=0)
        out = jnp.dot(hidden, down, preferred_element_type=jnp.float32).astype(jnp.bfloat16)
        return [out[i * SLOTS : (i + 1) * SLOTS] for i in range(len(part))]

    sums = experts(blocks[:4]) + experts(blocks[4:])
    total = sums[0].astype(jnp.float32)
    for value, (dxl, dy) in zip(sums[1:], DELTAS):
        total = total + across(value, dxl, -dy).astype(jnp.float32)
    total = total.astype(jnp.bfloat16)
    whole = jnp.concatenate([total, swap_core(total)], axis=1)
    dense = jnp.dot(table[:, :SLOTS], whole, preferred_element_type=jnp.float32).astype(
        jnp.bfloat16
    )
    returned = {k: spread(dense[k * ROWS : (k + 1) * ROWS], k, -1) for k in ORDER}

    moe = jnp.zeros((ROWS, WIDTH), jnp.float32)
    for k in range(4):
        step = jnp.where(core == 0, k, -(k + 1))
        source = (xh ^ xl) * 8 + (z + step) % 8
        weight = jnp.sum(
            route_weights * (expert_ids == source).astype(jnp.float32), axis=1, keepdims=True
        )
        moe = moe + weight * returned[k].astype(jnp.float32)
    part = moe.astype(jnp.bfloat16)
    got = swap_core(part)
    swapped = jnp.concatenate([got[:, HALF:], got[:, :HALF]], axis=1)
    pair = part.astype(jnp.float32) + swapped.astype(jnp.float32)
    pair_sent = pair.astype(jnp.bfloat16)
    far = send(pair_sent, lambda xl, c, xh, z, y: (1 - xl, c, xh, z, y))
    full = pair_sent.astype(jnp.float32) + far.astype(jnp.float32)
    first, second = full[:, :HALF], full[:, HALF:]
    full = jnp.where(
        core == 0,
        jnp.concatenate([first, second], axis=1),
        jnp.concatenate([second, first], axis=1),
    )
    mixed = (stream.astype(jnp.float32) + full).astype(jnp.bfloat16)
    return (context, mixed)


def solution(mesh):
    return jax.shard_map(
        local,
        mesh=mesh,
        in_specs=(
            P(("sec", "dev"), None, None),
            P(("sec", "dev"), None, None),
            P(("sec", "dev")),
            P("dev", None),
            P(),
            P("dev", None),
            P("dev", None),
            P("dev", None, "sec"),
            P("dev", None, "sec"),
            P("dev", "sec", None),
        ),
        out_specs=(P(("sec", "dev"), None, None), P("dev", None)),
        check_vma=False,
    )
```

time: 436 us -> 151 us (0.35)
  waiting for transfers between devices: 191 us -> 27.4 us
  blocking collectives: 160 us -> 0 us
  starting transfers between devices: 6.12 us -> 84.4 us
  matrix products: 35 us -> 15.5 us
  between operations: 14.8 us -> 1.83 us
  local copies, waits for them, and re-layouts: 17.6 us -> 11.8 us
    all_gather x1 -> x0, blocking collectives: 160 us -> none  [local(): lax.all_gather(expert_ids, 'dev', axis=0, tiled=True)]
    all_to_all x1 -> x0, waiting for transfers between devices: 126 us -> none  [local(): lax.all_to_all(partial_value.reshape(dev_count, capacity, width), 'dev',...]
    ppermute x0 -> x30, starting transfers between devices: none -> 84.4 us  [send(): return lax.ppermute(value, ('sec', 'dev'), pairs(move))]
    psum x1 -> x0, waiting for transfers between devices: 64.9 us -> none  [local(): lax.psum(section_part.astype(jnp.bfloat16), 'sec').astype(jnp.float32)]
    ppermute x0 -> x30, waiting for transfers between devices: none -> 27.4 us  [send(): return lax.ppermute(value, ('sec', 'dev'), pairs(move))]
    dot_general x6 -> x9, matrix products: 35 us -> 15.5 us  [the longest x1 4.41 us: attend(): jnp.einsum('shl,slk->shk', probs, latent_cache[:, :, :LATENT], preferred_...]
    reshape x2 -> x0, local copies, waits for them, and re-layouts: 16.2 us -> none  [the longest x1 8.22 us: local(): slot_flat = received.reshape(dev_count * capacity, width)]
    reduce_sum x6 -> x2, other arithmetic: 7.31 us -> 0.58 us  [the longest x1 0.44 us: attend(): jnp.sum(powered, axis=2, keepdims=True)]
  transfers between devices with their start and end apart: 3 -> 30, of which waited for: 2 -> 10; matrix products, arithmetic and copies ran while one was open for 2% -> 20% of each run, Pallas kernels for 0% -> 0%
where the time goes in v1:
time: 151 us; the launch traced here: 150 us
  starting transfers between devices  84.4 us (56%)
  waiting for transfers between devices  27.4 us (18%)
  matrix products  15.5 us (10%)
  local copies, waits for them, and re-layouts  11.8 us (8%)
  other arithmetic  7.37 us (5%)
  Pallas kernels  2.01 us (1%)
  between operations  1.83 us (1%)
    ppermute x30, starting transfers between devices, send(): return lax.ppermute(value, ('sec', 'dev'), pairs(move))  84.4 us
    ppermute x30, waiting for transfers between devices, send(): return lax.ppermute(value, ('sec', 'dev'), pairs(move))  27.4 us
    dot_general x1, matrix products, attend(): jnp.einsum('shl,slk->shk', probs, latent_cache[:, :, :LATENT], preferred_...  4.41 us
    unnamed x24, local copies, waits for them, and re-layouts  4.1 us
    dot_general x2, matrix products, experts(): other = jnp.dot(x, w_other, preferred_element_type=jnp.float32)  3.93 us
    squeeze x1, local copies, waits for them, and re-layouts, half(): return lax.dynamic_index_in_dim(array, which, axis, keepdims=False)  3.52 us
    dot_general x1, matrix products, attend(): jnp.einsum('shk,slk->shl', queries, latent_cache, preferred_element_type=...  3.45 us
    dynamic_slice x3, local copies, waits for them, and re-layouts, half(): return lax.dynamic_index_in_dim(array, which, axis, keepdims=False)  3.04 us
  transfers between devices with their start and end apart: 30, of which 10 were waited for; matrix products, arithmetic and copies ran while one was open for 20% of the time, Pallas kernels for 0%

profile of v1, /device:TPU:1, one launch (start us, length us, event | category | flops | bytes accessed | tf_op | source)
XLA Modules:
  0.0 150.3 jit_solution(10763897768960629568)
XLA Ops:
  0.6 0.7 convert_element_type.107
  1.4 0.9 fusion.24
  2.3 8.3 %collective-permute-start = (bf16[8,7296]{1,0:T(8,128)(2,1)S(1)}, bf16[8,7296]{1,0:T(8,128)(2,1)S(1)}, u32[]{:S(2)}, u32[]{:S(2)}) collective-permute-start(bf16[8,7296]{1,0:T(8,128)(2,1)S(1)} %fusion.24), channel_id=1, source_target_pairs={{0,0},{1,1},{2,2},{3,3},{4,4},{5,5},{6,6},{7,7},{8,8},{9,9},{10,10... | collective-permute-start | bytes 350216 | tf_op jit(solution)/shard_map/ppermute | solution.py:40
  10.6 1.2 collective-permute-start.1
  12.4 4.4 %collective-permute-start.3 = (bf16[8,7296]{1,0:T(8,128)(2,1)S(1)}, bf16[8,7296]{1,0:T(8,128)(2,1)S(1)}, u32[]{:S(2)}, u32[]{:S(2)}) collective-permute-start(bf16[8,7296]{1,0:T(8,128)(2,1)S(1)} %fusion.24), channel_id=1, source_target_pairs={{0,12},{1,13},{2,14},{3,15},{4,16},{5,17},{6,18},{7,19},{8,20},{9,... | collective-permute-start | bytes 350216 | tf_op jit(solution)/shard_map/ppermute | solution.py:40
  16.8 3.5 %dynamic-slice_bitcast_fusion.2 = (bf16[3584,128]{1,0:T(8,128)(2,1)}, bf16[3584,128]{1,0:T(8,128)(2,1)S(1)}, bf16[3584,128]{1,0:T(8,128)(2,1)S(1)}, bf16[3584,128]{1,0:T(8,128)(2,1)}) fusion(bf16[2,3584,128]{2,1,0:T(8,128)(2,1)} %bitcast.43, s32[]{:T(128)S(6)} %select_n.84, s32[]{:T(128)S(6)} %select_n.85, bf16[2,3584,128]{2,1,0:T(8,128)(2,1)} %bitcast.44), kind=kLoop, calls=%fused_computation.24 | loop fusion | bytes 7340040 | tf_op jit(solution)/shard_map/jit(dynamic_index_in_dim)/squeeze | solution.py:172
  20.4 1.5 collective-permute-done.3.r3
  21.9 2.0 %shard_map.113 = (bf16[40,3584]{1,0:T(8,128)(2,1)S(1)}, bf16[40,3584]{1,0:T(8,128)(2,1)S(1)}, bf16[32,128]{1,0:T(8,128)(2,1)S(1)}) custom-call(s32[2]{0:T(128)S(1)} %pad_add_fusion.at_ref, bf16[8,7296]{1,0:T(8,128)(2,1)S(1)} %collective-permute-done.r0, bf16[8,7296]{1,0:T(8,128)(2,1)S(1)} %collective-permute-done.1.r1, ...), custom_call_target="tpu_custom_call" | custom-call | flops 58720256 | bytes 1032192 | tf_op jit(solution)/shard_map/pallas_call | solution.py:111
  23.9 1.5 collective-permute-start.4
  25.4 1.5 pad_maximum_fusion.1
  26.8 3.3 %copy.12 = bf16[1,128,7168]{1,2,0:T(8,128)(2,1)S(1)} copy(bf16[1,128,7168]{2,1,0:T(8,128)(2,1)} %param.19) | data formatting | bytes 3670016 | tf_op args[9]
  30.1 0.7 copy-done.7
  30.9 1.0 add.137
  31.9 3.0 %collective-permute-start.14 = (bf16[40,3584]{1,0:T(8,128)(2,1)S(1)}, bf16[40,3584]{1,0:T(8,128)(2,1)S(1)}, u32[]{:S(2)}, u32[]{:S(2)}) collective-permute-start(bf16[40,3584]{1,0:T(8,128)(2,1)S(1)} %add.137), channel_id=1, source_target_pairs={{0,2},{1,3},{2,0},{3,1},{4,6},{5,7},{6,4},{7,5},{8,10},{9,11},{10,... | collective-permute-start | bytes 860168 | tf_op jit(solution)/shard_map/ppermute | solution.py:40
  34.9 1.1 constant_dynamic-slice_fusion.1
  36.0 1.5 copy.14
  38.4 2.3 %collective-permute-start.16 = (bf16[40,3584]{1,0:T(8,128)(2,1)S(1)}, bf16[40,3584]{1,0:T(8,128)(2,1)S(1)}, u32[]{:S(2)}, u32[]{:S(2)}) collective-permute-start(bf16[40,3584]{1,0:T(8,128)(2,1)S(1)} %add.137), channel_id=1, source_target_pairs={{0,3},{1,0},{2,1},{3,2},{4,7},{5,4},{6,5},{7,6},{8,11},{9,8},{10,9... | collective-permute-start | bytes 860168 | tf_op jit(solution)/shard_map/ppermute | solution.py:40
  40.7 8.8 %collective-permute-start.17 = (bf16[40,3584]{1,0:T(8,128)(2,1)S(1)}, bf16[40,3584]{1,0:T(8,128)(2,1)S(1)}, u32[]{:S(2)}, u32[]{:S(2)}) collective-permute-start(bf16[40,3584]{1,0:T(8,128)(2,1)S(1)} %add.137), channel_id=1, source_target_pairs={{0,128},{1,129},{2,130},{3,131},{4,132},{5,133},{6,134},{7,135},{8... | collective-permute-start | bytes 860168 | tf_op jit(solution)/shard_map/ppermute | solution.py:40
  49.5 3.7 %collective-permute-start.7 = (bf16[40,3584]{1,0:T(8,128)(2,1)S(1)}, bf16[40,3584]{1,0:T(8,128)(2,1)S(1)}, u32[]{:S(2)}, u32[]{:S(2)}) collective-permute-start(bf16[40,3584]{1,0:T(8,128)(2,1)S(1)} %add.137), channel_id=1, source_target_pairs={{0,131},{1,128},{2,129},{3,130},{4,135},{5,132},{6,133},{7,134},{8... | collective-permute-start | bytes 860168 | tf_op jit(solution)/shard_map/ppermute | solution.py:40
  53.2 4.8 %collective-permute-start.6 = (bf16[40,3584]{1,0:T(8,128)(2,1)S(1)}, bf16[40,3584]{1,0:T(8,128)(2,1)S(1)}, u32[]{:S(2)}, u32[]{:S(2)}) collective-permute-start(bf16[40,3584]{1,0:T(8,128)(2,1)S(1)} %add.137), channel_id=1, source_target_pairs={{0,129},{1,130},{2,131},{3,128},{4,133},{5,134},{6,135},{7,132},{8... | collective-permute-start | bytes 860168 | tf_op jit(solution)/shard_map/ppermute | solution.py:40
  58.1 5.4 %collective-permute-start.5 = (bf16[40,3584]{1,0:T(8,128)(2,1)S(1)}, bf16[40,3584]{1,0:T(8,128)(2,1)S(1)}, u32[]{:S(2)}, u32[]{:S(2)}) collective-permute-start(bf16[40,3584]{1,0:T(8,128)(2,1)S(1)} %add.137), channel_id=1, source_target_pairs={{0,130},{1,131},{2,128},{3,129},{4,134},{5,135},{6,132},{7,133},{8... | collective-permute-start | bytes 860168 | tf_op jit(solution)/shard_map/ppermute | solution.py:40
  63.6 1.4 collective-permute-start.10
  65.0 3.2 %collective-permute-done.6 = bf16[40,3584]{1,0:T(8,128)(2,1)S(1)} collective-permute-done((bf16[40,3584]{1,0:T(8,128)(2,1)S(1)}, bf16[40,3584]{1,0:T(8,128)(2,1)S(1)}, u32[]{:S(2)}, u32[]{:S(2)}) %collective-permute-start.6) | collective-permute-done | bytes 286752 | tf_op jit(solution)/shard_map/ppermute | solution.py:40
  68.2 6.0 %collective-permute-done.5 = bf16[40,3584]{1,0:T(8,128)(2,1)S(1)} collective-permute-done((bf16[40,3584]{1,0:T(8,128)(2,1)S(1)}, bf16[40,3584]{1,0:T(8,128)(2,1)S(1)}, u32[]{:S(2)}, u32[]{:S(2)}) %collective-permute-start.5) | collective-permute-done | bytes 286752 | tf_op jit(solution)/shard_map/ppermute | solution.py:40
  74.3 2.1 %fusion.7 = f32[160,256]{1,0:T(8,128)S(1)} fusion(bf16[3584,128]{1,0:T(8,128)(2,1)} %get-tuple-element.14, bf16[3584,128]{1,0:T(8,128)(2,1)} %get-tuple-element.40, bf16[40,3584]{1,0:T(8,128)(2,1)S(1)} %collective-permute-done.7, bf16[40,3584]{1,0:T(8,128)(2,1)S(1)} %collective-permute-done.6, bf16[40,3584]{1,0:T(8,128)(2,1)S(1)} %collective-permute-done.5, ...), kind=kOutput, calls=%fused_computation.16 | convolution fusion | flops 301858816 | bytes 3145728 | tf_op jit(solution)/shard_map/dot_general | solution.py:190
  76.9 2.0 %fusion.48 = f32[160,256]{1,0:T(8,128)S(1)} fusion(bf16[160,3584]{1,0:T(8,128)(2,1)S(1)} %constant_dynamic-update-slice_fusion, bf16[3584,256]{1,0:T(8,128)(2,1)} %collective-permute-done.8), kind=kOutput, calls=%fused_computation.86 | convolution fusion | flops 293601280 | bytes 3145728 | tf_op jit(solution)/shard_map/dot_general | solution.py:191
  78.9 1.3 collective-permute-start.18
  80.2 2.0 %fusion.22 = f32[160,256]{1,0:T(8,128)S(1)} fusion(bf16[3584,256]{1,0:T(8,128)(2,1)} %collective-permute-done.8, bf16[40,3584]{1,0:T(8,128)(2,1)S(1)} %collective-permute-done.7, bf16[40,3584]{1,0:T(8,128)(2,1)S(1)} %collective-permute-done.6, bf16[40,3584]{1,0:T(8,128)(2,1)S(1)} %collective-permute-done.5, bf16[40,3584]{1,0:T(8,128)(2,1)S(1)} %add.137), kind=kOutput, calls=%fused_computation.40 | convolution fusion | flops 298188800 | bytes 3145728 | tf_op jit(solution)/shard_map/dot_general | solution.py:191
  83.0 1.6 %collective-permute-start.22 = (bf16[40,3584]{1,0:T(8,128)(2,1)S(1)}, bf16[40,3584]{1,0:T(8,128)(2,1)S(1)}, u32[]{:S(2)}, u32[]{:S(2)}) collective-permute-start(bf16[40,3584]{1,0:T(8,128)(2,1)S(1)} %get-tuple-element.22), channel_id=1, source_target_pairs={{0,128},{1,129},{2,130},{3,131},{4,132},{5,133},{6,134},{7,135},{8... | collective-permute-start | bytes 860168 | tf_op jit(solution)/shard_map/ppermute | solution.py:40
  85.2 2.1 %collective-permute-start.20 = (bf16[40,3584]{1,0:T(8,128)(2,1)S(1)}, bf16[40,3584]{1,0:T(8,128)(2,1)S(1)}, u32[]{:S(2)}, u32[]{:S(2)}) collective-permute-start(bf16[40,3584]{1,0:T(8,128)(2,1)S(1)} %get-tuple-element.24), channel_id=1, source_target_pairs={{0,3},{1,0},{2,1},{3,2},{4,7},{5,4},{6,5},{7,6},{8,11},{9,8},{10,9... | collective-permute-start | bytes 860168 | tf_op jit(solution)/shard_map/ppermute | solution.py:40
  87.3 1.8 %collective-permute-start.19 = (bf16[40,3584]{1,0:T(8,128)(2,1)S(1)}, bf16[40,3584]{1,0:T(8,128)(2,1)S(1)}, u32[]{:S(2)}, u32[]{:S(2)}) collective-permute-start(bf16[40,3584]{1,0:T(8,128)(2,1)S(1)} %get-tuple-element.21), channel_id=1, source_target_pairs={{0,2},{1,3},{2,0},{3,1},{4,6},{5,7},{6,4},{7,5},{8,10},{9,11},{10,... | collective-permute-start | bytes 860168 | tf_op jit(solution)/shard_map/ppermute | solution.py:40
  89.6 0.9 fusion.42
  91.0 3.1 %collective-permute-start.12 = (bf16[40,3584]{1,0:T(8,128)(2,1)}, bf16[40,3584]{1,0:T(8,128)(2,1)}, u32[]{:S(2)}, u32[]{:S(2)}) collective-permute-start(bf16[40,3584]{1,0:T(8,128)(2,1)} %get-tuple-element.20), channel_id=1, source_target_pairs={{0,131},{1,128},{2,129},{3,130},{4,135},{5,132},{6,133},{7,134},{8... | collective-permute-start | bytes 860168 | tf_op jit(solution)/shard_map/ppermute | solution.py:40
  94.2 6.7 %collective-permute-start.11 = (bf16[40,3584]{1,0:T(8,128)(2,1)}, bf16[40,3584]{1,0:T(8,128)(2,1)}, u32[]{:S(2)}, u32[]{:S(2)}) collective-permute-start(bf16[40,3584]{1,0:T(8,128)(2,1)} %get-tuple-element.18), channel_id=1, source_target_pairs={{0,130},{1,131},{2,128},{3,129},{4,134},{5,135},{6,132},{7,133},{8... | collective-permute-start | bytes 860168 | tf_op jit(solution)/shard_map/ppermute | solution.py:40
  101.5 5.2 %collective-permute-done.19 = bf16[40,3584]{1,0:T(8,128)(2,1)S(1)} collective-permute-done((bf16[40,3584]{1,0:T(8,128)(2,1)S(1)}, bf16[40,3584]{1,0:T(8,128)(2,1)S(1)}, u32[]{:S(2)}, u32[]{:S(2)}) %collective-permute-start.19) | collective-permute-done | bytes 286752 | tf_op jit(solution)/shard_map/ppermute | solution.py:40
  106.7 4.6 %collective-permute-done.11 = bf16[40,3584]{1,0:T(8,128)(2,1)} collective-permute-done((bf16[40,3584]{1,0:T(8,128)(2,1)}, bf16[40,3584]{1,0:T(8,128)(2,1)}, u32[]{:S(2)}, u32[]{:S(2)}) %collective-permute-start.11) | collective-permute-done | bytes 286752 | tf_op jit(solution)/shard_map/ppermute | solution.py:40
  111.3 1.4 add_convert_fusion
  112.7 4.1 %collective-permute-start.23 = (bf16[40,3584]{1,0:T(8,128)(2,1)S(1)}, bf16[40,3584]{1,0:T(8,128)(2,1)S(1)}, u32[]{:S(2)}, u32[]{:S(2)}) collective-permute-start(bf16[40,3584]{1,0:T(8,128)(2,1)S(1)} %add_convert_fusion), channel_id=1, source_target_pairs={{0,64},{1,65},{2,66},{3,67},{4,68},{5,69},{6,70},{7,71},{8,72},{9,... | collective-permute-start | bytes 860168 | tf_op jit(solution)/shard_map/ppermute | solution.py:40
  116.8 3.5 %fusion.47 = (f32[128]{0:T(128)S(1)}, f32[128,4096]{1,0:T(8,128)S(1)}) fusion(bf16[1,4096,576]{1,2,0:T(8,128)(2,1)} %param.11, bf16[1,128,576]{1,2,0:T(8,128)(2,1)S(1)} %copy-done, pred[4096]{0:T(1024)(128)(4,1)S(1)} %iota_compare_fusion.1), kind=kOutput, calls=%fused_computation.85 | convolution fusion | flops 605552512 | bytes 6967808 | tf_op jit(solution)/shard_map/shk,slk->shl/dot_general | solution.py:129
  120.6 2.7 %collective-permute-start.27 = (bf16[8,7168]{1,0:T(8,128)(2,1)S(1)}, bf16[8,7168]{1,0:T(8,128)(2,1)S(1)}, u32[]{:S(2)}, u32[]{:S(2)}) collective-permute-start(bf16[8,7168]{1,0:T(8,128)(2,1)S(1)} %get-tuple-element.26), channel_id=1, source_target_pairs={{0,20},{1,21},{2,22},{3,23},{4,24},{5,25},{6,26},{7,27},{8,28},{9,... | collective-permute-start | bytes 344072 | tf_op jit(solution)/shard_map/ppermute | solution.py:40
  123.8 3.8 %collective-permute-start.25 = (bf16[8,7168]{1,0:T(8,128)(2,1)S(1)}, bf16[8,7168]{1,0:T(8,128)(2,1)S(1)}, u32[]{:S(2)}, u32[]{:S(2)}) collective-permute-start(bf16[8,7168]{1,0:T(8,128)(2,1)S(1)} %get-tuple-element.28), channel_id=1, source_target_pairs={{0,28},{1,29},{2,30},{3,31},{4,0},{5,1},{6,2},{7,3},{8,4},{9,5},{1... | collective-permute-start | bytes 344072 | tf_op jit(solution)/shard_map/ppermute | solution.py:40
  127.6 3.3 %collective-permute-start.24 = (bf16[8,7168]{1,0:T(8,128)(2,1)S(1)}, bf16[8,7168]{1,0:T(8,128)(2,1)S(1)}, u32[]{:S(2)}, u32[]{:S(2)}) collective-permute-start(bf16[8,7168]{1,0:T(8,128)(2,1)S(1)} %get-tuple-element.25), channel_id=1, source_target_pairs={{0,0},{1,1},{2,2},{3,3},{4,4},{5,5},{6,6},{7,7},{8,8},{9,9},{10,10... | collective-permute-start | bytes 344072 | tf_op jit(solution)/shard_map/ppermute | solution.py:40
  131.2 2.1 %collective-permute-done.26 = bf16[8,7168]{1,0:T(8,128)(2,1)S(1)} collective-permute-done((bf16[8,7168]{1,0:T(8,128)(2,1)S(1)}, bf16[8,7168]{1,0:T(8,128)(2,1)S(1)}, u32[]{:S(2)}, u32[]{:S(2)}) %collective-permute-start.26) | collective-permute-done | bytes 114720 | tf_op jit(solution)/shard_map/ppermute | solution.py:40
  133.3 2.7 %collective-permute-done.25 = bf16[8,7168]{1,0:T(8,128)(2,1)S(1)} collective-permute-done((bf16[8,7168]{1,0:T(8,128)(2,1)S(1)}, bf16[8,7168]{1,0:T(8,128)(2,1)S(1)}, u32[]{:S(2)}, u32[]{:S(2)}) %collective-permute-start.25) | collective-permute-done | bytes 114720 | tf_op jit(solution)/shard_map/ppermute | solution.py:40
  137.4 0.9 collective-permute-done.28
  138.3 6.8 %collective-permute-start.29 = (bf16[8,7168]{1,0:T(8,128)(2,1)S(1)}, bf16[8,7168]{1,0:T(8,128)(2,1)S(1)}, u32[]{:S(2)}, u32[]{:S(2)}) collective-permute-start(bf16[8,7168]{1,0:T(8,128)(2,1)S(1)} %add_convert_fusion.1), channel_id=1, source_target_pairs={{0,128},{1,129},{2,130},{3,131},{4,132},{5,133},{6,134},{7,135},{8... | collective-permute-start | bytes 344072 | tf_op jit(solution)/shard_map/ppermute | solution.py:40
  145.1 4.4 %fusion.11 = bf16[1,128,512]{2,1,0:T(8,128)(2,1)} fusion(bf16[1,4096,576]{1,2,0:T(8,128)(2,1)} %param.11, f32[128,4096]{1,0:T(8,128)S(1)} %get-tuple-element.38, f32[128]{0:T(128)S(1)} %fusion.5, f32[128]{0:T(128)S(1)} %get-tuple-element.37), kind=kOutput, calls=%fused_computation.19 | convolution fusion | flops 538509312 | bytes 6423552 | tf_op jit(solution)/shard_map/shl,slk->shk/dot_general | solution.py:140
  149.6 0.7 fusion.21
  (77 shorter events, 7.1 us)
Async XLA Ops:
  0.6 116.2 %copy-start = (bf16[1,128,576]{1,2,0:T(8,128)(2,1)S(1)}, bf16[1,128,576]{1,2,0:T(8,128)(2,1)}, u32[]{:S(2)}) copy-start(bf16[1,128,576]{1,2,0:T(8,128)(2,1)} %param.10) | copy-start | bytes 442372
  2.3 18.1 %collective-permute-start = (bf16[8,7296]{1,0:T(8,128)(2,1)S(1)}, bf16[8,7296]{1,0:T(8,128)(2,1)S(1)}, u32[]{:S(2)}, u32[]{:S(2)}) collective-permute-start(bf16[8,7296]{1,0:T(8,128)(2,1)S(1)} %fusion.24), channel_id=1, source_target_pairs={{0,0},{1,1},{2,2},{3,3},{4,4},{5,5},{6,6},{7,7},{8,8},{9,9},{10,10... | collective-permute-start | bytes 350216 | tf_op jit(solution)/shard_map/ppermute | solution.py:40
  10.6 9.8 %collective-permute-start.1 = (bf16[8,7296]{1,0:T(8,128)(2,1)S(1)}, bf16[8,7296]{1,0:T(8,128)(2,1)S(1)}, u32[]{:S(2)}, u32[]{:S(2)}) collective-permute-start(bf16[8,7296]{1,0:T(8,128)(2,1)S(1)} %fusion.24), channel_id=1, source_target_pairs={{0,4},{1,5},{2,6},{3,7},{4,8},{5,9},{6,10},{7,11},{8,12},{9,13},{1... | collective-permute-start | bytes 350216 | tf_op jit(solution)/shard_map/ppermute | solution.py:40
  11.8 8.5 %collective-permute-start.2 = (bf16[8,7296]{1,0:T(8,128)(2,1)S(1)}, bf16[8,7296]{1,0:T(8,128)(2,1)S(1)}, u32[]{:S(2)}, u32[]{:S(2)}) collective-permute-start(bf16[8,7296]{1,0:T(8,128)(2,1)S(1)} %fusion.24), channel_id=1, source_target_pairs={{0,8},{1,9},{2,10},{3,11},{4,12},{5,13},{6,14},{7,15},{8,16},{9,17... | collective-permute-start | bytes 350216 | tf_op jit(solution)/shard_map/ppermute | solution.py:40
  12.4 9.5 %collective-permute-start.3 = (bf16[8,7296]{1,0:T(8,128)(2,1)S(1)}, bf16[8,7296]{1,0:T(8,128)(2,1)S(1)}, u32[]{:S(2)}, u32[]{:S(2)}) collective-permute-start(bf16[8,7296]{1,0:T(8,128)(2,1)S(1)} %fusion.24), channel_id=1, source_target_pairs={{0,12},{1,13},{2,14},{3,15},{4,16},{5,17},{6,18},{7,19},{8,20},{9,... | collective-permute-start | bytes 350216 | tf_op jit(solution)/shard_map/ppermute | solution.py:40
  16.8 5.1 %copy-start.1 = (f32[7168]{0:T(1024)S(1)}, f32[7168]{0:T(1024)}, u32[]{:S(2)}) copy-start(f32[7168]{0:T(1024)} %param.14) | copy-start | bytes 86020
  23.9 6.2 %collective-permute-start.4 = (bf16[40,3584]{1,0:T(8,128)(2,1)S(1)}, bf16[40,3584]{1,0:T(8,128)(2,1)S(1)}, u32[]{:S(2)}, u32[]{:S(2)}) collective-permute-start(bf16[40,3584]{1,0:T(8,128)(2,1)S(1)} %get-tuple-element.7), channel_id=1, source_target_pairs={{0,64},{1,65},{2,66},{3,67},{4,68},{5,69},{6,70},{7,71},{8,72},{9,... | collective-permute-start | bytes 860168 | tf_op jit(solution)/shard_map/ppermute | solution.py:40
  26.8 50.0 %collective-permute-start.8 = (bf16[3584,256]{1,0:T(8,128)(2,1)}, bf16[3584,256]{1,0:T(8,128)(2,1)}, u32[]{:S(2)}, u32[]{:S(2)}) collective-permute-start(bf16[3584,256]{1,0:T(8,128)(2,1)} %pad_maximum_fusion.1), channel_id=1, source_target_pairs={{0,64},{1,65},{2,66},{3,67},{4,68},{5,69},{6,70},{7,71},{8,72},{9,... | collective-permute-start | bytes 5505032 | tf_op jit(solution)/shard_map/ppermute | solution.py:40
  30.1 0.7 copy-start.7
  31.9 17.6 %collective-permute-start.14 = (bf16[40,3584]{1,0:T(8,128)(2,1)S(1)}, bf16[40,3584]{1,0:T(8,128)(2,1)S(1)}, u32[]{:S(2)}, u32[]{:S(2)}) collective-permute-start(bf16[40,3584]{1,0:T(8,128)(2,1)S(1)} %add.137), channel_id=1, source_target_pairs={{0,2},{1,3},{2,0},{3,1},{4,6},{5,7},{6,4},{7,5},{8,10},{9,11},{10,... | collective-permute-start | bytes 860168 | tf_op jit(solution)/shard_map/ppermute | solution.py:40
  38.0 44.5 %copy-start.2 = (bf16[128,1,3584]{2,0,1:T(8,128)(2,1)}, bf16[128,1,3584]{2,0,1:T(8,128)(2,1)S(1)}, u32[]{:S(2)}) copy-start(bf16[128,1,3584]{2,0,1:T(8,128)(2,1)S(1)} %copy.13) | copy-start | bytes 2752516
  38.0 15.3 %collective-permute-start.15 = (bf16[40,3584]{1,0:T(8,128)(2,1)S(1)}, bf16[40,3584]{1,0:T(8,128)(2,1)S(1)}, u32[]{:S(2)}, u32[]{:S(2)}) collective-permute-start(bf16[40,3584]{1,0:T(8,128)(2,1)S(1)} %add.137), channel_id=1, source_target_pairs={{0,1},{1,2},{2,3},{3,0},{4,5},{5,6},{6,7},{7,4},{8,9},{9,10},{10,1... | collective-permute-start | bytes 860168 | tf_op jit(solution)/shard_map/ppermute | solution.py:40
  38.4 19.7 %collective-permute-start.16 = (bf16[40,3584]{1,0:T(8,128)(2,1)S(1)}, bf16[40,3584]{1,0:T(8,128)(2,1)S(1)}, u32[]{:S(2)}, u32[]{:S(2)}) collective-permute-start(bf16[40,3584]{1,0:T(8,128)(2,1)S(1)} %add.137), channel_id=1, source_target_pairs={{0,3},{1,0},{2,1},{3,2},{4,7},{5,4},{6,5},{7,6},{8,11},{9,8},{10,9... | collective-permute-start | bytes 860168 | tf_op jit(solution)/shard_map/ppermute | solution.py:40
  40.7 35.6 %collective-permute-start.17 = (bf16[40,3584]{1,0:T(8,128)(2,1)S(1)}, bf16[40,3584]{1,0:T(8,128)(2,1)S(1)}, u32[]{:S(2)}, u32[]{:S(2)}) collective-permute-start(bf16[40,3584]{1,0:T(8,128)(2,1)S(1)} %add.137), channel_id=1, source_target_pairs={{0,128},{1,129},{2,130},{3,131},{4,132},{5,133},{6,134},{7,135},{8... | collective-permute-start | bytes 860168 | tf_op jit(solution)/shard_map/ppermute | solution.py:40
  49.5 14.0 %collective-permute-start.7 = (bf16[40,3584]{1,0:T(8,128)(2,1)S(1)}, bf16[40,3584]{1,0:T(8,128)(2,1)S(1)}, u32[]{:S(2)}, u32[]{:S(2)}) collective-permute-start(bf16[40,3584]{1,0:T(8,128)(2,1)S(1)} %add.137), channel_id=1, source_target_pairs={{0,131},{1,128},{2,129},{3,130},{4,135},{5,132},{6,133},{7,134},{8... | collective-permute-start | bytes 860168 | tf_op jit(solution)/shard_map/ppermute | solution.py:40
  53.2 15.0 %collective-permute-start.6 = (bf16[40,3584]{1,0:T(8,128)(2,1)S(1)}, bf16[40,3584]{1,0:T(8,128)(2,1)S(1)}, u32[]{:S(2)}, u32[]{:S(2)}) collective-permute-start(bf16[40,3584]{1,0:T(8,128)(2,1)S(1)} %add.137), channel_id=1, source_target_pairs={{0,129},{1,130},{2,131},{3,128},{4,133},{5,134},{6,135},{7,132},{8... | collective-permute-start | bytes 860168 | tf_op jit(solution)/shard_map/ppermute | solution.py:40
  58.1 16.1 %collective-permute-start.5 = (bf16[40,3584]{1,0:T(8,128)(2,1)S(1)}, bf16[40,3584]{1,0:T(8,128)(2,1)S(1)}, u32[]{:S(2)}, u32[]{:S(2)}) collective-permute-start(bf16[40,3584]{1,0:T(8,128)(2,1)S(1)} %add.137), channel_id=1, source_target_pairs={{0,130},{1,131},{2,128},{3,129},{4,134},{5,135},{6,132},{7,133},{8... | collective-permute-start | bytes 860168 | tf_op jit(solution)/shard_map/ppermute | solution.py:40
  63.6 18.9 %collective-permute-start.10 = (bf16[128,3584]{1,0:T(8,128)(2,1)S(1)}, bf16[128,3584]{1,0:T(8,128)(2,1)S(1)}, u32[]{:S(2)}, u32[]{:S(2)}) collective-permute-start(bf16[128,3584]{1,0:T(8,128)(2,1)S(1)} %bitcast.47), channel_id=1, source_target_pairs={{0,64},{1,65},{2,66},{3,67},{4,68},{5,69},{6,70},{7,71},{8,72},{9,... | collective-permute-start | bytes 2752520 | tf_op jit(solution)/shard_map/ppermute | solution.py:40
  74.2 2.1 %copy-start.4 = (bf16[3584,128]{1,0:T(8,128)(2,1)S(1)}, bf16[3584,128]{1,0:T(8,128)(2,1)}, u32[]{:S(2)}) copy-start(bf16[3584,128]{1,0:T(8,128)(2,1)} %get-tuple-element.14) | copy-start | bytes 2752516
  74.3 2.1 %copy-start.5 = (bf16[3584,128]{1,0:T(8,128)(2,1)S(1)}, bf16[3584,128]{1,0:T(8,128)(2,1)}, u32[]{:S(2)}) copy-start(bf16[3584,128]{1,0:T(8,128)(2,1)} %get-tuple-element.40) | copy-start | bytes 2752516
  78.9 3.4 %collective-permute-start.18 = (f32[160,512]{1,0:T(8,128)S(1)}, f32[160,512]{1,0:T(8,128)S(1)}, u32[]{:S(2)}, u32[]{:S(2)}) collective-permute-start(f32[160,512]{1,0:T(8,128)S(1)} %pad_maximum_fusion.9), channel_id=1, source_target_pairs={{0,64},{1,65},{2,66},{3,67},{4,68},{5,69},{6,70},{7,71},{8,72},{9,... | collective-permute-start | bytes 983048 | tf_op jit(solution)/shard_map/ppermute | solution.py:40
  82.2 6.8 %collective-permute-start.9 = (f32[160,512]{1,0:T(8,128)S(1)}, f32[160,512]{1,0:T(8,128)S(1)}, u32[]{:S(2)}, u32[]{:S(2)}) collective-permute-start(f32[160,512]{1,0:T(8,128)S(1)} %pad_maximum_fusion.8), channel_id=1, source_target_pairs={{0,64},{1,65},{2,66},{3,67},{4,68},{5,69},{6,70},{7,71},{8,72},{9,... | collective-permute-start | bytes 983048 | tf_op jit(solution)/shard_map/ppermute | solution.py:40
  82.9 6.2 %copy-start.3 = (bf16[128,1,3584]{2,0,1:T(8,128)(2,1)S(1)}, bf16[128,1,3584]{2,0,1:T(8,128)(2,1)}, u32[]{:S(2)}) copy-start(bf16[128,1,3584]{2,0,1:T(8,128)(2,1)} %copy-done.2) | copy-start | bytes 2752516
  83.0 8.0 %collective-permute-start.22 = (bf16[40,3584]{1,0:T(8,128)(2,1)S(1)}, bf16[40,3584]{1,0:T(8,128)(2,1)S(1)}, u32[]{:S(2)}, u32[]{:S(2)}) collective-permute-start(bf16[40,3584]{1,0:T(8,128)(2,1)S(1)} %get-tuple-element.22), channel_id=1, source_target_pairs={{0,128},{1,129},{2,130},{3,131},{4,132},{5,133},{6,134},{7,135},{8... | collective-permute-start | bytes 860168 | tf_op jit(solution)/shard_map/ppermute | solution.py:40
  84.6 9.6 %collective-permute-start.21 = (bf16[40,3584]{1,0:T(8,128)(2,1)S(1)}, bf16[40,3584]{1,0:T(8,128)(2,1)S(1)}, u32[]{:S(2)}, u32[]{:S(2)}) collective-permute-start(bf16[40,3584]{1,0:T(8,128)(2,1)S(1)} %get-tuple-element.23), channel_id=1, source_target_pairs={{0,1},{1,2},{2,3},{3,0},{4,5},{5,6},{6,7},{7,4},{8,9},{9,10},{10,1... | collective-permute-start | bytes 860168 | tf_op jit(solution)/shard_map/ppermute | solution.py:40
  85.2 16.3 %collective-permute-start.20 = (bf16[40,3584]{1,0:T(8,128)(2,1)S(1)}, bf16[40,3584]{1,0:T(8,128)(2,1)S(1)}, u32[]{:S(2)}, u32[]{:S(2)}) collective-permute-start(bf16[40,3584]{1,0:T(8,128)(2,1)S(1)} %get-tuple-element.24), channel_id=1, source_target_pairs={{0,3},{1,0},{2,1},{3,2},{4,7},{5,4},{6,5},{7,6},{8,11},{9,8},{10,9... | collective-permute-start | bytes 860168 | tf_op jit(solution)/shard_map/ppermute | solution.py:40
  87.3 19.4 %collective-permute-start.19 = (bf16[40,3584]{1,0:T(8,128)(2,1)S(1)}, bf16[40,3584]{1,0:T(8,128)(2,1)S(1)}, u32[]{:S(2)}, u32[]{:S(2)}) collective-permute-start(bf16[40,3584]{1,0:T(8,128)(2,1)S(1)} %get-tuple-element.21), channel_id=1, source_target_pairs={{0,2},{1,3},{2,0},{3,1},{4,6},{5,7},{6,4},{7,5},{8,10},{9,11},{10,... | collective-permute-start | bytes 860168 | tf_op jit(solution)/shard_map/ppermute | solution.py:40
  90.6 16.1 %collective-permute-start.13 = (bf16[40,3584]{1,0:T(8,128)(2,1)}, bf16[40,3584]{1,0:T(8,128)(2,1)S(1)}, u32[]{:S(2)}, u32[]{:S(2)}) collective-permute-start(bf16[40,3584]{1,0:T(8,128)(2,1)} %get-tuple-element.19), channel_id=1, source_target_pairs={{0,129},{1,130},{2,131},{3,128},{4,133},{5,134},{6,135},{7,132},{8... | collective-permute-start | bytes 860168 | tf_op jit(solution)/shard_map/ppermute | solution.py:40
  91.0 15.7 %collective-permute-start.12 = (bf16[40,3584]{1,0:T(8,128)(2,1)}, bf16[40,3584]{1,0:T(8,128)(2,1)}, u32[]{:S(2)}, u32[]{:S(2)}) collective-permute-start(bf16[40,3584]{1,0:T(8,128)(2,1)} %get-tuple-element.20), channel_id=1, source_target_pairs={{0,131},{1,128},{2,129},{3,130},{4,135},{5,132},{6,133},{7,134},{8... | collective-permute-start | bytes 860168 | tf_op jit(solution)/shard_map/ppermute | solution.py:40
  94.2 17.2 %collective-permute-start.11 = (bf16[40,3584]{1,0:T(8,128)(2,1)}, bf16[40,3584]{1,0:T(8,128)(2,1)}, u32[]{:S(2)}, u32[]{:S(2)}) collective-permute-start(bf16[40,3584]{1,0:T(8,128)(2,1)} %get-tuple-element.18), channel_id=1, source_target_pairs={{0,130},{1,131},{2,128},{3,129},{4,134},{5,135},{6,132},{7,133},{8... | collective-permute-start | bytes 860168 | tf_op jit(solution)/shard_map/ppermute | solution.py:40
  112.7 7.6 %collective-permute-start.23 = (bf16[40,3584]{1,0:T(8,128)(2,1)S(1)}, bf16[40,3584]{1,0:T(8,128)(2,1)S(1)}, u32[]{:S(2)}, u32[]{:S(2)}) collective-permute-start(bf16[40,3584]{1,0:T(8,128)(2,1)S(1)} %add_convert_fusion), channel_id=1, source_target_pairs={{0,64},{1,65},{2,66},{3,67},{4,68},{5,69},{6,70},{7,71},{8,72},{9,... | collective-permute-start | bytes 860168 | tf_op jit(solution)/shard_map/ppermute | solution.py:40
  120.3 10.7 %copy-start.8 = (s32[8,8]{1,0:T(8,128)S(1)}, s32[8,8]{1,0:T(8,128)}, u32[]{:S(2)}) copy-start(s32[8,8]{1,0:T(8,128)} %param.15) | copy-start | bytes 772
  120.3 10.7 %copy-start.9 = (f32[8,8]{1,0:T(8,128)S(1)}, f32[8,8]{1,0:T(8,128)}, u32[]{:S(2)}) copy-start(f32[8,8]{1,0:T(8,128)} %param.16) | copy-start | bytes 772
  120.6 10.5 %collective-permute-start.27 = (bf16[8,7168]{1,0:T(8,128)(2,1)S(1)}, bf16[8,7168]{1,0:T(8,128)(2,1)S(1)}, u32[]{:S(2)}, u32[]{:S(2)}) collective-permute-start(bf16[8,7168]{1,0:T(8,128)(2,1)S(1)} %get-tuple-element.26), channel_id=1, source_target_pairs={{0,20},{1,21},{2,22},{3,23},{4,24},{5,25},{6,26},{7,27},{8,28},{9,... | collective-permute-start | bytes 344072 | tf_op jit(solution)/shard_map/ppermute | solution.py:40
  123.3 10.0 %collective-permute-start.26 = (bf16[8,7168]{1,0:T(8,128)(2,1)S(1)}, bf16[8,7168]{1,0:T(8,128)(2,1)S(1)}, u32[]{:S(2)}, u32[]{:S(2)}) collective-permute-start(bf16[8,7168]{1,0:T(8,128)(2,1)S(1)} %get-tuple-element.27), channel_id=1, source_target_pairs={{0,24},{1,25},{2,26},{3,27},{4,28},{5,29},{6,30},{7,31},{8,0},{9,1... | collective-permute-start | bytes 344072 | tf_op jit(solution)/shard_map/ppermute | solution.py:40
  123.8 12.2 %collective-permute-start.25 = (bf16[8,7168]{1,0:T(8,128)(2,1)S(1)}, bf16[8,7168]{1,0:T(8,128)(2,1)S(1)}, u32[]{:S(2)}, u32[]{:S(2)}) collective-permute-start(bf16[8,7168]{1,0:T(8,128)(2,1)S(1)} %get-tuple-element.28), channel_id=1, source_target_pairs={{0,28},{1,29},{2,30},{3,31},{4,0},{5,1},{6,2},{7,3},{8,4},{9,5},{1... | collective-permute-start | bytes 344072 | tf_op jit(solution)/shard_map/ppermute | solution.py:40
  127.6 9.0 %collective-permute-start.24 = (bf16[8,7168]{1,0:T(8,128)(2,1)S(1)}, bf16[8,7168]{1,0:T(8,128)(2,1)S(1)}, u32[]{:S(2)}, u32[]{:S(2)}) collective-permute-start(bf16[8,7168]{1,0:T(8,128)(2,1)S(1)} %get-tuple-element.25), channel_id=1, source_target_pairs={{0,0},{1,1},{2,2},{3,3},{4,4},{5,5},{6,6},{7,7},{8,8},{9,9},{10,10... | collective-permute-start | bytes 344072 | tf_op jit(solution)/shard_map/ppermute | solution.py:40
  136.8 1.4 collective-permute-start.28
  138.3 11.3 %copy-start.6 = (bf16[8,7168]{1,0:T(8,128)(2,1)S(1)}, bf16[8,7168]{1,0:T(8,128)(2,1)}, u32[]{:S(2)}) copy-start(bf16[8,7168]{1,0:T(8,128)(2,1)} %param.13) | copy-start | bytes 344068
  138.3 11.2 %collective-permute-start.29 = (bf16[8,7168]{1,0:T(8,128)(2,1)S(1)}, bf16[8,7168]{1,0:T(8,128)(2,1)S(1)}, u32[]{:S(2)}, u32[]{:S(2)}) collective-permute-start(bf16[8,7168]{1,0:T(8,128)(2,1)S(1)} %add_convert_fusion.1), channel_id=1, source_target_pairs={{0,128},{1,129},{2,130},{3,131},{4,132},{5,133},{6,134},{7,135},{8... | collective-permute-start | bytes 344072 | tf_op jit(solution)/shard_map/ppermute | solution.py:40

commit v2 on v1

v2 whole, which is shorter than its diff:
```python
import functools

import jax
import jax.numpy as jnp
from jax import lax
from jax.experimental import pallas as pl
from jax.experimental.pallas import tpu as pltpu
from jax.sharding import PartitionSpec as P

LATENT = 512
CAP = 5
ROWS = 8
WIDTH = 7168
SLOTS = 24
score_scale = 192.0 ** (-0.5)

SIZES = (2, 2, 2, 8, 4)


def pairs(move):
    out = []
    for xl in range(2):
        for c in range(2):
            for xh in range(2):
                for z in range(8):
                    for y in range(4):
                        place = (xl, c, xh, z, y)
                        lin = []
                        for spot in (place, move(*place)):
                            at = 0
                            for part, size in zip(spot, SIZES):
                                at = at * size + part % size
                            lin.append(at)
                        out.append(tuple(lin))
    return out


def send(value, move):
    return lax.ppermute(value, ("sec", "dev"), pairs(move))


def swap_core(value):
    return send(value, lambda xl, c, xh, z, y: (xl, 1 - c, xh, z, y))


STEPS = ((0, 1, -2, 3), (-1, 2, -3, 4))


def spread(value, k, sign):
    def move(xl, c, xh, z, y):
        if xl == c:
            return (xl, c, xh, z + sign * STEPS[c][k], y)
        return (1 - xl, 1 - c, 1 - xh, z + (STEPS[c][k] if sign > 0 else -STEPS[1 - c][k]), y)

    return send(value, move)


ORDER = (0, 1, 2, 3)


def pick_kernel(at_ref, r0, r1, r2, r3, gain_ref, slots_ref, table_ref):
    expert = at_ref[0].astype(jnp.float32)
    rows = (r0, r1, r2, r3)
    named = []
    scale = []
    for r in rows:
        ids = r[:, WIDTH:].astype(jnp.float32)
        named.append(jnp.sum((ids == expert).astype(jnp.float32), axis=1, keepdims=True))
        x = r[:, :WIDTH].astype(jnp.float32)
        scale.append(lax.rsqrt(jnp.sum(x * x, axis=1, keepdims=True) / WIDTH + 1e-06))
    named = jnp.concatenate(named, axis=0)
    scale = jnp.concatenate(scale, axis=0)
    count = 4 * ROWS
    row = lax.broadcasted_iota(jnp.int32, (count, count), 0)
    col = lax.broadcasted_iota(jnp.int32, (count, count), 1)
    earlier = ((col < row) & ((col // ROWS) == (row // ROWS))).astype(jnp.float32)
    named = jnp.broadcast_to(named, (count, 128))
    before = jnp.dot(earlier, named, preferred_element_type=jnp.float32)
    group = lax.broadcasted_iota(jnp.int32, (count, 128), 0) // ROWS
    lane = lax.broadcasted_iota(jnp.int32, (count, 128), 1)
    place = (group * CAP).astype(jnp.float32) + before
    hit = (named > 0.5) & (before < CAP - 0.5) & (lane.astype(jnp.float32) == place)
    table = hit.astype(jnp.bfloat16)
    table_ref[...] = table
    wide = WIDTH // 4
    for part in range(4):
        cols = pl.ds(part * wide, wide)
        x = jnp.concatenate([r[:, cols].astype(jnp.float32) for r in rows], axis=0)
        normed = (x * scale * gain_ref[:, cols]).astype(jnp.bfloat16)
        slots_ref[:, cols] = lax.dot_general(
            table, normed, (((0,), (0,)), ((), ())), preferred_element_type=jnp.float32
        )[:SLOTS].astype(jnp.bfloat16)


def pick(at, rows, gain):
    vmem = pl.BlockSpec(memory_space=pltpu.VMEM)
    return pl.pallas_call(
        pick_kernel,
        out_shape=(
            jax.ShapeDtypeStruct((SLOTS, WIDTH), jnp.bfloat16),
            jax.ShapeDtypeStruct((4 * ROWS, 128), jnp.bfloat16),
        ),
        in_specs=[pl.BlockSpec(memory_space=pltpu.SMEM)] + [vmem] * 5,
        out_specs=(vmem, vmem),
        cost_estimate=pl.CostEstimate(
            flops=2 * 128 * 32 * WIDTH, bytes_accessed=2 * 72 * WIDTH, transcendentals=32
        ),
        compiler_params=pltpu.CompilerParams(vmem_limit_bytes=16 * 1024 * 1024),
    )(at, *rows, gain)


def widen_kernel(stream_ref, ids_ref, out_ref):
    out_ref[:, :WIDTH] = stream_ref[...]
    out_ref[:, WIDTH:] = jnp.full((ROWS, 128), -1, jnp.bfloat16)
    out_ref[:, WIDTH : WIDTH + 8] = ids_ref[...].astype(jnp.float32).astype(jnp.bfloat16)


def widen(stream, ids):
    vmem = pl.BlockSpec(memory_space=pltpu.VMEM)
    return pl.pallas_call(
        widen_kernel,
        out_shape=jax.ShapeDtypeStruct((ROWS, WIDTH + 128), jnp.bfloat16),
        in_specs=[vmem, vmem],
        out_specs=vmem,
    )(stream, ids)


def expert_kernel(count, *refs):
    blocks = refs[:count]
    gates = refs[count : count + 2]
    ups = refs[count + 2 : count + 4]
    downs = refs[count + 4 : count + 6]
    outs = refs[count + 6 :]
    step = 1024
    acc = jnp.zeros((count * SLOTS, 512), jnp.float32)
    for at in range(0, WIDTH, step):
        ks = pl.ds(at, step)
        x = jnp.concatenate([b[:, ks].astype(jnp.float32) for b in blocks], axis=0)
        w = jnp.concatenate([r[ks, :] for r in gates + ups], axis=1)
        acc = acc + jnp.dot(x.astype(jnp.bfloat16), w, preferred_element_type=jnp.float32)
    gate_proj, up_proj = acc[:, :256], acc[:, 256:]
    hidden = (gate_proj / (1.0 + jnp.exp(-gate_proj)) * up_proj).astype(jnp.bfloat16)
    for at in range(0, WIDTH, step):
        ks = pl.ds(at, step)
        w = jnp.concatenate([r[:, ks] for r in downs], axis=0)
        out = jnp.dot(hidden, w, preferred_element_type=jnp.float32)
        for i, ref in enumerate(outs):
            ref[:, ks] = out[i * SLOTS : (i + 1) * SLOTS].astype(jnp.bfloat16)


def experts(blocks, gates, ups, downs):
    vmem = pl.BlockSpec(memory_space=pltpu.VMEM)
    count = len(blocks)
    rows = count * SLOTS
    return pl.pallas_call(
        functools.partial(expert_kernel, count),
        out_shape=tuple(jax.ShapeDtypeStruct((SLOTS, WIDTH), jnp.bfloat16) for _ in blocks),
        in_specs=[vmem] * (count + 6),
        out_specs=tuple(vmem for _ in blocks),
        cost_estimate=pl.CostEstimate(
            flops=2 * rows * WIDTH * 768,
            bytes_accessed=2 * WIDTH * (768 + 2 * rows),
            transcendentals=rows * 256,
        ),
        compiler_params=pltpu.CompilerParams(vmem_limit_bytes=32 * 1024 * 1024),
    )(*blocks, *gates, *ups, *downs)


def scatter_kernel(table_ref, b0, b1, b2, b3, o0, o1, o2, o3):
    table = table_ref[...][:, :SLOTS]
    wide = WIDTH // 4
    for part in range(4):
        cols = pl.ds(part * wide, wide)
        total = b0[:, cols].astype(jnp.float32)
        for b in (b1, b2, b3):
            total = total + b[:, cols].astype(jnp.float32)
        dense = jnp.dot(table, total.astype(jnp.bfloat16), preferred_element_type=jnp.float32)
        for i, out in enumerate((o0, o1, o2, o3)):
            out[:, cols] = dense[i * ROWS : (i + 1) * ROWS].astype(jnp.bfloat16)


def scatter(table, blocks):
    vmem = pl.BlockSpec(memory_space=pltpu.VMEM)
    return pl.pallas_call(
        scatter_kernel,
        out_shape=tuple(jax.ShapeDtypeStruct((ROWS, WIDTH), jnp.bfloat16) for _ in range(4)),
        in_specs=[vmem] * 5,
        out_specs=(vmem,) * 4,
        cost_estimate=pl.CostEstimate(
            flops=2 * 32 * 32 * WIDTH, bytes_accessed=2 * 152 * WIDTH, transcendentals=0
        ),
        compiler_params=pltpu.CompilerParams(vmem_limit_bytes=16 * 1024 * 1024),
    )(table, *blocks)


def attend_kernel(length_ref, q_hbm, cache_hbm, out_ref, q_ref, cache_ref, sems):
    parts, _, size = cache_ref.shape
    heads = q_ref.shape[1]
    copies = [pltpu.make_async_copy(q_hbm.at[0], q_ref, sems.at[parts])]
    for part in range(parts):
        copies.append(
            pltpu.make_async_copy(
                cache_hbm.at[0, :, pl.ds(part * size, size)], cache_ref.at[part], sems.at[part]
            )
        )
    for copy in copies:
        copy.start()
    copies[0].wait()
    peak = jnp.full((heads, 1), -1e30, jnp.float32)
    total = jnp.zeros((heads, 1), jnp.float32)
    acc = jnp.zeros((heads, LATENT), jnp.float32)
    query = q_ref[...]
    for part in range(parts):
        copies[part + 1].wait()
        scores = (
            lax.dot_general(
                query,
                cache_ref[part],
                (((0,), (0,)), ((), ())),
                preferred_element_type=jnp.float32,
            )
            * score_scale
        )
        at = part * size + lax.broadcasted_iota(jnp.int32, scores.shape, 1)
        scores = jnp.where(at < length_ref[0], scores, jnp.float32(-1e30))
        new = jnp.maximum(peak, jnp.max(scores, axis=1, keepdims=True))
        powered = jnp.exp(scores - new)
        fade = jnp.exp(peak - new)
        total = total * fade + jnp.sum(powered, axis=1, keepdims=True)
        peak = new
        acc = acc * fade + lax.dot_general(
            powered.astype(jnp.bfloat16),
            cache_ref[part, :LATENT],
            (((1,), (1,)), ((), ())),
            preferred_element_type=jnp.float32,
        )
    out_ref[0] = (acc / total).astype(jnp.bfloat16)


def attend(queries, latent_cache, cache_lengths):
    heads, width = queries.shape[1:]
    length = latent_cache.shape[1]
    parts = 4
    return pl.pallas_call(
        attend_kernel,
        out_shape=jax.ShapeDtypeStruct((1, heads, LATENT), jnp.bfloat16),
        in_specs=[
            pl.BlockSpec(memory_space=pltpu.SMEM),
            pl.BlockSpec(memory_space=pltpu.HBM),
            pl.BlockSpec(memory_space=pltpu.HBM),
        ],
        out_specs=pl.BlockSpec(memory_space=pltpu.VMEM),
        scratch_shapes=[
            pltpu.VMEM((width, heads), jnp.bfloat16),
            pltpu.VMEM((parts, width, length // parts), jnp.bfloat16),
            pltpu.SemaphoreType.DMA((parts + 1,)),
        ],
        cost_estimate=pl.CostEstimate(
            flops=2 * heads * length * (width + LATENT),
            bytes_accessed=2 * length * width,
            transcendentals=heads * length,
        ),
        compiler_params=pltpu.CompilerParams(vmem_limit_bytes=16 * 1024 * 1024),
    )(cache_lengths, jnp.swapaxes(queries, 1, 2), jnp.swapaxes(latent_cache, 1, 2))


def local(
    queries,
    latent_cache,
    cache_lengths,
    stream,
    norm_gain,
    expert_ids,
    route_weights,
    w_gate,
    w_up,
    w_down,
):
    sec = lax.axis_index("sec")
    dev = lax.axis_index("dev")
    xl, core = sec // 2, sec % 2
    xh, z = dev // 32, (dev // 4) % 8
    expert = xh * 8 + z

    block = widen(stream, expert_ids)
    arrived = {k: spread(block, k, 1) for k in ORDER}

    gate_own, up_own, down_own = w_gate[0], w_up[0], w_down[0]
    block, gate_own = lax.optimization_barrier((block, gate_own))
    gate_other = swap_core(gate_own)
    context = attend(queries, latent_cache, cache_lengths)
    rows = [arrived[k] for k in range(4)]
    rows[1], context = lax.optimization_barrier((rows[1], context))
    at = expert.astype(jnp.int32)[None]
    mine, table = pick(at, rows, norm_gain[None, :])

    def over(value):
        return send(value, lambda xl, c, xh, z, y: (1 - xl, c, xh, z, y))

    def along(value, sign, flip=0):
        return send(
            value,
            lambda xl, c, xh, z, y: (xl ^ flip, c, xh, z, y + (sign if c == 0 else -sign)),
        )

    mine, up_own, gate_other = lax.optimization_barrier((mine, up_own, gate_other))
    up_other = swap_core(up_own)
    x_in = over(mine)
    p_in = along(mine, 1)
    m_in = along(mine, -1)
    x_in, p_in, m_in, up_other, down_own = lax.optimization_barrier(
        (x_in, p_in, m_in, up_other, down_own)
    )
    down_other = swap_core(down_own)
    weights = ((gate_own, gate_other), (up_own, up_other), (down_own, down_other))
    pxp_in = along(p_in, 1, 1)
    pp_in = along(p_in, 1)
    xp_in = along(x_in, 1)
    mx_in = over(m_in)
    own, x_out, p_out, m_out = experts([mine, x_in, p_in, m_in], *weights)
    pxp_in, own = lax.optimization_barrier((pxp_in, own))
    pxp_out, pp_out, xp_out, mx_out = experts([pxp_in, pp_in, xp_in, mx_in], *weights)
    pxp_back = along(pxp_out, -1, 1)
    pp_back = along(pp_out, -1)
    xp_back = along(xp_out, -1)
    mx_back = over(mx_out)

    def add(*values):
        return sum(v.astype(jnp.float32) for v in values).astype(jnp.bfloat16)

    p_back = along(add(p_out, pp_back, pxp_back), -1)
    m_back = along(add(m_out, mx_back), 1)
    x_back = over(add(x_out, xp_back))
    dense = scatter(table, (own, p_back, m_back, x_back))
    returned = {k: spread(dense[k], k, -1) for k in ORDER}

    moe = jnp.zeros((ROWS, WIDTH), jnp.float32)
    for k in range(4):
        step = jnp.where(core == 0, STEPS[0][k], STEPS[1][k])
        source = jnp.where(xl == core, xh, 1 - xh) * 8 + (z + step) % 8
        weight = jnp.sum(
            route_weights * (expert_ids == source).astype(jnp.float32), axis=1, keepdims=True
        )
        moe = moe + weight * returned[k].astype(jnp.float32)
    part = moe.astype(jnp.bfloat16)
    pair = part.astype(jnp.float32) + swap_core(part).astype(jnp.float32)
    pair = pair.astype(jnp.bfloat16)
    far = over(pair)
    full = pair.astype(jnp.float32) + far.astype(jnp.float32)
    mixed = (stream.astype(jnp.float32) + full).astype(jnp.bfloat16)
    return (context, mixed)


def solution(mesh):
    return jax.shard_map(
        local,
        mesh=mesh,
        in_specs=(
            P(("sec", "dev"), None, None),
            P(("sec", "dev"), None, None),
            P(("sec", "dev")),
            P("dev", None),
            P(),
            P("dev", None),
            P("dev", None),
            P("dev", None, "sec"),
            P("dev", None, "sec"),
            P("dev", "sec", None),
        ),
        out_specs=(P(("sec", "dev"), None, None), P("dev", None)),
        check_vma=False,
    )
```

time: 151 us -> 122 us (0.81)
  starting transfers between devices: 84.4 us -> 48.1 us
  waiting for transfers between devices: 27.4 us -> 52.7 us
  matrix products: 15.5 us -> 0 us
  Pallas kernels: 2.01 us -> 15 us
  local copies, waits for them, and re-layouts: 11.8 us -> 3.28 us
  other arithmetic: 7.37 us -> 1.31 us
    ppermute x30 -> x27, starting transfers between devices: 84.4 us -> 48.1 us  [send(): return lax.ppermute(value, ('sec', 'dev'), pairs(move))]
    ppermute x30 -> x27, waiting for transfers between devices: 27.4 us -> 52.7 us  [send(): return lax.ppermute(value, ('sec', 'dev'), pairs(move))]
    dot_general x9 -> x0, matrix products: 15.5 us -> none  [the longest x1 4.41 us: attend(): jnp.einsum('shl,slk->shk', probs, latent_cache[:, :, :LATENT], preferred_...]
    pallas_call x1 -> x6, Pallas kernels: 2.01 us -> 15 us  [the longest x2 6.95 us: experts(): pl.pallas_call(functools.partial(expert_kernel, count), out_shape=tuple((...]
    squeeze x1 -> x0, local copies, waits for them, and re-layouts: 3.52 us -> none  [half(): return lax.dynamic_index_in_dim(array, which, axis, keepdims=False)]
    dynamic_slice x3 -> x0, local copies, waits for them, and re-layouts: 3.04 us -> none  [half(): return lax.dynamic_index_in_dim(array, which, axis, keepdims=False)]
    concatenate x4 -> x0, other arithmetic: 2.42 us -> none  [the longest x1 1.46 us: local(): jnp.concatenate([half(gate_halves, 1 - core, 0), half(up_halves, 1 - core...]
    convert_element_type x7 -> x4, other arithmetic: 2.29 us -> 0.32 us  [the longest x3 0.29 us: add(): return sum((v.astype(jnp.float32) for v in values)).astype(jnp.bfloat16)]
  transfers between devices with their start and end apart: 30 -> 27, of which waited for: 10 -> 16; matrix products, arithmetic and copies ran while one was open for 20% -> 0% of each run, Pallas kernels for 0% -> 8%
where the time goes in v2:
time: 122 us
  waiting for transfers between devices  52.7 us (43%)
  starting transfers between devices  48.1 us (39%)
  Pallas kernels  15 us (12%)
  local copies, waits for them, and re-layouts  3.28 us (3%)
  between operations  1.77 us (1%)
  other arithmetic  1.31 us (1%)
    ppermute x27, waiting for transfers between devices, send(): return lax.ppermute(value, ('sec', 'dev'), pairs(move))  52.7 us
    ppermute x27, starting transfers between devices, send(): return lax.ppermute(value, ('sec', 'dev'), pairs(move))  48.1 us
    pallas_call x2, Pallas kernels, experts(): pl.pallas_call(functools.partial(expert_kernel, count), out_shape=tuple((...  6.95 us
    pallas_call x1, Pallas kernels, attend(): pl.pallas_call(attend_kernel, out_shape=jax.ShapeDtypeStruct((1, heads, L...  5.24 us
    unnamed x18, local copies, waits for them, and re-layouts  3.28 us
  transfers between devices with their start and end apart: 27, of which 16 were waited for; matrix products, arithmetic and copies ran while one was open for 0% of the time, Pallas kernels for 8%

profile of v2, /device:TPU:1, one launch (start us, length us, event | category | flops | bytes accessed | tf_op | source)
XLA Modules:
  0.0 122.1 jit_solution(6065821860158186417)
XLA Ops:
  0.6 1.6 %shard_map.113 = bf16[8,7296]{1,0:T(8,128)(2,1)} custom-call(bf16[8,7168]{1,0:T(8,128)(2,1)} %stream_ref.1, s32[8,8]{1,0:T(8,128)} %ids_ref.1), custom_call_target="tpu_custom_call" | custom-call | tf_op jit(solution)/shard_map/pallas_call | solution.py:120
  2.2 3.2 %collective-permute-start.4 = (bf16[7168,128]{1,0:T(8,128)(2,1)}, bf16[7168,128]{1,0:T(8,128)(2,1)}, u32[]{:S(2)}, u32[]{:S(2)}) collective-permute-start(bf16[7168,128]{1,0:T(8,128)(2,1)} %bitcast.7), channel_id=1, source_target_pairs={{0,64},{1,65},{2,66},{3,67},{4,68},{5,69},{6,70},{7,71},{8,72},{9,... | collective-permute-start | bytes 5505032 | tf_op jit(solution)/shard_map/ppermute | solution.py:39
  5.4 3.3 %collective-permute-start = (bf16[8,7296]{1,0:T(8,128)(2,1)}, bf16[8,7296]{1,0:T(8,128)(2,1)S(1)}, u32[]{:S(2)}, u32[]{:S(2)}) collective-permute-start(bf16[8,7296]{1,0:T(8,128)(2,1)} %shard_map.113), channel_id=1, source_target_pairs={{0,4},{1,5},{2,6},{3,7},{4,8},{5,9},{6,10},{7,11},{8,12},{9,13},{1... | collective-permute-start | bytes 350216 | tf_op jit(solution)/shard_map/ppermute | solution.py:39
  8.8 4.5 %collective-permute-start.1 = (bf16[8,7296]{1,0:T(8,128)(2,1)}, bf16[8,7296]{1,0:T(8,128)(2,1)S(1)}, u32[]{:S(2)}, u32[]{:S(2)}) collective-permute-start(bf16[8,7296]{1,0:T(8,128)(2,1)} %shard_map.113), channel_id=1, source_target_pairs={{0,0},{1,1},{2,2},{3,3},{4,4},{5,5},{6,6},{7,7},{8,8},{9,9},{10,10... | collective-permute-start | bytes 350216 | tf_op jit(solution)/shard_map/ppermute | solution.py:39
  13.3 4.8 %collective-permute-start.2 = (bf16[8,7296]{1,0:T(8,128)(2,1)}, bf16[8,7296]{1,0:T(8,128)(2,1)S(1)}, u32[]{:S(2)}, u32[]{:S(2)}) collective-permute-start(bf16[8,7296]{1,0:T(8,128)(2,1)} %shard_map.113), channel_id=1, source_target_pairs={{0,24},{1,25},{2,26},{3,27},{4,28},{5,29},{6,30},{7,31},{8,0},{9,1... | collective-permute-start | bytes 350216 | tf_op jit(solution)/shard_map/ppermute | solution.py:39
  18.1 2.6 %collective-permute-start.3 = (bf16[8,7296]{1,0:T(8,128)(2,1)}, bf16[8,7296]{1,0:T(8,128)(2,1)S(1)}, u32[]{:S(2)}, u32[]{:S(2)}) collective-permute-start(bf16[8,7296]{1,0:T(8,128)(2,1)} %shard_map.113), channel_id=1, source_target_pairs={{0,12},{1,13},{2,14},{3,15},{4,16},{5,17},{6,18},{7,19},{8,20},{9,... | collective-permute-start | bytes 350216 | tf_op jit(solution)/shard_map/ppermute | solution.py:39
  21.5 2.3 %copy-done.3 = bf16[1,4096,576]{1,2,0:T(8,128)(2,1)S(1)} copy-done((bf16[1,4096,576]{1,2,0:T(8,128)(2,1)S(1)}, bf16[1,4096,576]{1,2,0:T(8,128)(2,1)}, u32[]{:S(2)}) %copy-start.3) | copy-done | bytes 4718616
  23.8 0.9 copy-done.4
  24.7 5.2 %shard_map.114 = bf16[1,128,512]{2,1,0:T(8,128)(2,1)} custom-call(s32[1]{0:T(128)S(6)} %copy.12.length_ref, bf16[1,576,128]{2,1,0:T(8,128)(2,1)S(1)} %bitcast.17, bf16[1,576,4096]{2,1,0:T(8,128)(2,1)S(1)} %bitcast.16), custom_call_target="tpu_custom_call" | custom-call | flops 1140850688 | bytes 4718592 | tf_op jit(solution)/shard_map/pallas_call | solution.py:244
  30.0 0.9 shard_map.115
  31.0 0.1 collective-permute-start.8
  31.1 0.1 collective-permute-start.5
  31.2 2.8 %collective-permute-start.6 = (bf16[24,7168]{1,0:T(8,128)(2,1)S(1)}, bf16[24,7168]{1,0:T(8,128)(2,1)S(1)}, u32[]{:S(2)}, u32[]{:S(2)}) collective-permute-start(bf16[24,7168]{1,0:T(8,128)(2,1)S(1)} %get-tuple-element.34.refs_0_), channel_id=1, source_target_pairs={{0,1},{1,2},{2,3},{3,0},{4,5},{5,6},{6,7},{7,4},{8,9},{9,10},{10,1... | collective-permute-start | bytes 1032200 | tf_op jit(solution)/shard_map/ppermute | solution.py:39
  34.0 6.4 %collective-permute-done.5.refs_1_ = bf16[24,7168]{1,0:T(8,128)(2,1)S(1)} collective-permute-done((bf16[24,7168]{1,0:T(8,128)(2,1)S(1)}, bf16[24,7168]{1,0:T(8,128)(2,1)S(1)}, u32[]{:S(2)}, u32[]{:S(2)}) %collective-permute-start.5) | collective-permute-done | bytes 344096 | tf_op jit(solution)/shard_map/ppermute | solution.py:39
  40.4 0.5 collective-permute-done.6.refs_2_
  40.8 2.2 %collective-permute-done.7.refs_3_ = bf16[24,7168]{1,0:T(8,128)(2,1)S(1)} collective-permute-done((bf16[24,7168]{1,0:T(8,128)(2,1)S(1)}, bf16[24,7168]{1,0:T(8,128)(2,1)S(1)}, u32[]{:S(2)}, u32[]{:S(2)}) %collective-permute-start.7) | collective-permute-done | bytes 344096 | tf_op jit(solution)/shard_map/ppermute | solution.py:39
  43.0 3.7 %collective-permute-start.9 = (bf16[24,7168]{1,0:T(8,128)(2,1)S(1)}, bf16[24,7168]{1,0:T(8,128)(2,1)S(1)}, u32[]{:S(2)}, u32[]{:S(2)}) collective-permute-start(bf16[24,7168]{1,0:T(8,128)(2,1)S(1)} %collective-permute-done.6.refs_2_), channel_id=1, source_target_pairs={{0,129},{1,130},{2,131},{3,128},{4,133},{5,134},{6,135},{7,132},{8... | collective-permute-start | bytes 1032200 | tf_op jit(solution)/shard_map/ppermute | solution.py:39
  46.8 0.4 collective-permute-start.12
  47.1 3.5 %shard_map.116 = (bf16[24,7168]{1,0:T(8,128)(2,1)S(1)}, bf16[24,7168]{1,0:T(8,128)(2,1)S(1)}, bf16[24,7168]{1,0:T(8,128)(2,1)S(1)}, bf16[24,7168]{1,0:T(8,128)(2,1)S(1)}) custom-call(bf16[24,7168]{1,0:T(8,128)(2,1)S(1)} %get-tuple-element.34.refs_0_, bf16[24,7168]{1,0:T(8,128)(2,1)S(1)} %collective-permute-done.5.refs_1_, ...), custom_call_target="tpu_custom_call" | custom-call | flops 1056964608 | bytes 13762560 | tf_op jit(solution)/shard_map/pallas_call | solution.py:155
  50.6 4.0 %collective-permute-done.9.refs_0_ = bf16[24,7168]{1,0:T(8,128)(2,1)S(1)} collective-permute-done((bf16[24,7168]{1,0:T(8,128)(2,1)S(1)}, bf16[24,7168]{1,0:T(8,128)(2,1)S(1)}, u32[]{:S(2)}, u32[]{:S(2)}) %collective-permute-start.9) | collective-permute-done | bytes 344096 | tf_op jit(solution)/shard_map/ppermute | solution.py:39
  54.7 0.6 collective-permute-done.11.refs_1_
  55.2 3.7 %collective-permute-done.12.refs_2_ = bf16[24,7168]{1,0:T(8,128)(2,1)S(1)} collective-permute-done((bf16[24,7168]{1,0:T(8,128)(2,1)S(1)}, bf16[24,7168]{1,0:T(8,128)(2,1)S(1)}, u32[]{:S(2)}, u32[]{:S(2)}) %collective-permute-start.12) | collective-permute-done | bytes 344096 | tf_op jit(solution)/shard_map/ppermute | solution.py:39
  58.9 2.2 %collective-permute-done.13.refs_3_ = bf16[24,7168]{1,0:T(8,128)(2,1)S(1)} collective-permute-done((bf16[24,7168]{1,0:T(8,128)(2,1)S(1)}, bf16[24,7168]{1,0:T(8,128)(2,1)S(1)}, u32[]{:S(2)}, u32[]{:S(2)}) %collective-permute-start.13) | collective-permute-done | bytes 344096 | tf_op jit(solution)/shard_map/ppermute | solution.py:39
  61.2 3.5 %shard_map.117 = (bf16[24,7168]{1,0:T(8,128)(2,1)S(1)}, bf16[24,7168]{1,0:T(8,128)(2,1)S(1)}, bf16[24,7168]{1,0:T(8,128)(2,1)S(1)}, bf16[24,7168]{1,0:T(8,128)(2,1)S(1)}) custom-call(bf16[24,7168]{1,0:T(8,128)(2,1)S(1)} %collective-permute-done.9.refs_0_, bf16[24,7168]{1,0:T(8,128)(2,1)S(1)} %collective-permute-done.11.refs_1_, ...), custom_call_target="tpu_custom_call" | custom-call | flops 1056964608 | bytes 13762560 | tf_op jit(solution)/shard_map/pallas_call | solution.py:155
  64.7 2.0 %collective-permute-start.15 = (bf16[24,7168]{1,0:T(8,128)(2,1)S(1)}, bf16[24,7168]{1,0:T(8,128)(2,1)S(1)}, u32[]{:S(2)}, u32[]{:S(2)}) collective-permute-start(bf16[24,7168]{1,0:T(8,128)(2,1)S(1)} %get-tuple-element.47), channel_id=1, source_target_pairs={{0,131},{1,128},{2,129},{3,130},{4,135},{5,132},{6,133},{7,134},{8... | collective-permute-start | bytes 1032200 | tf_op jit(solution)/shard_map/ppermute | solution.py:39
  66.6 0.4 collective-permute-start.17
  67.0 0.9 collective-permute-start.19
  67.9 8.7 %collective-permute-done.15 = bf16[24,7168]{1,0:T(8,128)(2,1)S(1)} collective-permute-done((bf16[24,7168]{1,0:T(8,128)(2,1)S(1)}, bf16[24,7168]{1,0:T(8,128)(2,1)S(1)}, u32[]{:S(2)}, u32[]{:S(2)}) %collective-permute-start.15) | collective-permute-done | bytes 344096 | tf_op jit(solution)/shard_map/ppermute | solution.py:39
  76.5 0.5 collective-permute-done.14
  77.1 0.1 add_convert_fusion.2
  77.3 3.3 %collective-permute-done.17 = bf16[24,7168]{1,0:T(8,128)(2,1)S(1)} collective-permute-done((bf16[24,7168]{1,0:T(8,128)(2,1)S(1)}, bf16[24,7168]{1,0:T(8,128)(2,1)S(1)}, u32[]{:S(2)}, u32[]{:S(2)}) %collective-permute-start.17) | collective-permute-done | bytes 344096 | tf_op jit(solution)/shard_map/ppermute | solution.py:39
  80.7 3.5 %collective-permute-start.18 = (bf16[24,7168]{1,0:T(8,128)(2,1)S(1)}, bf16[24,7168]{1,0:T(8,128)(2,1)S(1)}, u32[]{:S(2)}, u32[]{:S(2)}) collective-permute-start(bf16[24,7168]{1,0:T(8,128)(2,1)S(1)} %add_convert_fusion.1), channel_id=1, source_target_pairs={{0,1},{1,2},{2,3},{3,0},{4,5},{5,6},{6,7},{7,4},{8,9},{9,10},{10,1... | collective-permute-start | bytes 1032200 | tf_op jit(solution)/shard_map/ppermute | solution.py:39
  84.3 2.3 %collective-permute-start.20 = (bf16[24,7168]{1,0:T(8,128)(2,1)S(1)}, bf16[24,7168]{1,0:T(8,128)(2,1)S(1)}, u32[]{:S(2)}, u32[]{:S(2)}) collective-permute-start(bf16[24,7168]{1,0:T(8,128)(2,1)S(1)} %add_convert_fusion), channel_id=1, source_target_pairs={{0,128},{1,129},{2,130},{3,131},{4,132},{5,133},{6,134},{7,135},{8... | collective-permute-start | bytes 1032200 | tf_op jit(solution)/shard_map/ppermute | solution.py:39
  86.6 2.4 %collective-permute-done.18.b2 = bf16[24,7168]{1,0:T(8,128)(2,1)S(1)} collective-permute-done((bf16[24,7168]{1,0:T(8,128)(2,1)S(1)}, bf16[24,7168]{1,0:T(8,128)(2,1)S(1)}, u32[]{:S(2)}, u32[]{:S(2)}) %collective-permute-start.18) | collective-permute-done | bytes 344096 | tf_op jit(solution)/shard_map/ppermute | solution.py:39
  89.0 5.2 %collective-permute-done.20.b3 = bf16[24,7168]{1,0:T(8,128)(2,1)S(1)} collective-permute-done((bf16[24,7168]{1,0:T(8,128)(2,1)S(1)}, bf16[24,7168]{1,0:T(8,128)(2,1)S(1)}, u32[]{:S(2)}, u32[]{:S(2)}) %collective-permute-start.20) | collective-permute-done | bytes 344096 | tf_op jit(solution)/shard_map/ppermute | solution.py:39
  94.2 0.3 shard_map.118
  94.5 3.7 %collective-permute-start.24 = (bf16[8,7168]{1,0:T(8,128)(2,1)S(1)}, bf16[8,7168]{1,0:T(8,128)(2,1)S(1)}, u32[]{:S(2)}, u32[]{:S(2)}) collective-permute-start(bf16[8,7168]{1,0:T(8,128)(2,1)S(1)} %get-tuple-element.55), channel_id=1, source_target_pairs={{0,20},{1,21},{2,22},{3,23},{4,24},{5,25},{6,26},{7,27},{8,28},{9,... | collective-permute-start | bytes 344072 | tf_op jit(solution)/shard_map/ppermute | solution.py:39
  98.2 3.0 %collective-permute-start.23 = (bf16[8,7168]{1,0:T(8,128)(2,1)S(1)}, bf16[8,7168]{1,0:T(8,128)(2,1)S(1)}, u32[]{:S(2)}, u32[]{:S(2)}) collective-permute-start(bf16[8,7168]{1,0:T(8,128)(2,1)S(1)} %get-tuple-element.54), channel_id=1, source_target_pairs={{0,8},{1,9},{2,10},{3,11},{4,12},{5,13},{6,14},{7,15},{8,16},{9,17... | collective-permute-start | bytes 344072 | tf_op jit(solution)/shard_map/ppermute | solution.py:39
  101.2 0.2 collective-permute-start.22
  101.4 6.4 %collective-permute-start.21 = (bf16[8,7168]{1,0:T(8,128)(2,1)S(1)}, bf16[8,7168]{1,0:T(8,128)(2,1)S(1)}, u32[]{:S(2)}, u32[]{:S(2)}) collective-permute-start(bf16[8,7168]{1,0:T(8,128)(2,1)S(1)} %get-tuple-element.52), channel_id=1, source_target_pairs={{0,0},{1,1},{2,2},{3,3},{4,4},{5,5},{6,6},{7,7},{8,8},{9,9},{10,10... | collective-permute-start | bytes 344072 | tf_op jit(solution)/shard_map/ppermute | solution.py:39
  107.9 0.1 select_reduce_fusion.3
  108.0 4.8 %collective-permute-done.23 = bf16[8,7168]{1,0:T(8,128)(2,1)S(1)} collective-permute-done((bf16[8,7168]{1,0:T(8,128)(2,1)S(1)}, bf16[8,7168]{1,0:T(8,128)(2,1)S(1)}, u32[]{:S(2)}, u32[]{:S(2)}) %collective-permute-start.23) | collective-permute-done | bytes 114720 | tf_op jit(solution)/shard_map/ppermute | solution.py:39
  112.8 2.4 %collective-permute-done.21 = bf16[8,7168]{1,0:T(8,128)(2,1)S(1)} collective-permute-done((bf16[8,7168]{1,0:T(8,128)(2,1)S(1)}, bf16[8,7168]{1,0:T(8,128)(2,1)S(1)}, u32[]{:S(2)}, u32[]{:S(2)}) %collective-permute-start.21) | collective-permute-done | bytes 114720 | tf_op jit(solution)/shard_map/ppermute | solution.py:39
  115.2 0.2 add_convert_fusion.5
  115.3 0.1 collective-permute-start.25
  115.4 1.3 %collective-permute-done.25 = bf16[8,7168]{1,0:T(8,128)(2,1)S(1)} collective-permute-done((bf16[8,7168]{1,0:T(8,128)(2,1)S(1)}, bf16[8,7168]{1,0:T(8,128)(2,1)S(1)}, u32[]{:S(2)}, u32[]{:S(2)}) %collective-permute-start.25) | collective-permute-done | bytes 114720 | tf_op jit(solution)/shard_map/ppermute | solution.py:39
  116.9 4.6 %collective-permute-done.26 = bf16[8,7168]{1,0:T(8,128)(2,1)S(1)} collective-permute-done((bf16[8,7168]{1,0:T(8,128)(2,1)S(1)}, bf16[8,7168]{1,0:T(8,128)(2,1)S(1)}, u32[]{:S(2)}, u32[]{:S(2)}) %collective-permute-start.26) | collective-permute-done | bytes 114720 | tf_op jit(solution)/shard_map/ppermute | solution.py:39
  121.4 0.7 add_convert_fusion.3
  (37 shorter events, 0.5 us)
Async XLA Ops:
  0.6 29.4 %copy-start.5 = (f32[7168]{0:T(1024)S(1)}, f32[7168]{0:T(1024)}, u32[]{:S(2)}) copy-start(f32[7168]{0:T(1024)} %param.14) | copy-start | bytes 86020
  2.2 28.8 %collective-permute-start.4 = (bf16[7168,128]{1,0:T(8,128)(2,1)}, bf16[7168,128]{1,0:T(8,128)(2,1)}, u32[]{:S(2)}, u32[]{:S(2)}) collective-permute-start(bf16[7168,128]{1,0:T(8,128)(2,1)} %bitcast.7), channel_id=1, source_target_pairs={{0,64},{1,65},{2,66},{3,67},{4,68},{5,69},{6,70},{7,71},{8,72},{9,... | collective-permute-start | bytes 5505032 | tf_op jit(solution)/shard_map/ppermute | solution.py:39
  5.4 24.5 %collective-permute-start = (bf16[8,7296]{1,0:T(8,128)(2,1)}, bf16[8,7296]{1,0:T(8,128)(2,1)S(1)}, u32[]{:S(2)}, u32[]{:S(2)}) collective-permute-start(bf16[8,7296]{1,0:T(8,128)(2,1)} %shard_map.113), channel_id=1, source_target_pairs={{0,4},{1,5},{2,6},{3,7},{4,8},{5,9},{6,10},{7,11},{8,12},{9,13},{1... | collective-permute-start | bytes 350216 | tf_op jit(solution)/shard_map/ppermute | solution.py:39
  8.8 21.2 %collective-permute-start.1 = (bf16[8,7296]{1,0:T(8,128)(2,1)}, bf16[8,7296]{1,0:T(8,128)(2,1)S(1)}, u32[]{:S(2)}, u32[]{:S(2)}) collective-permute-start(bf16[8,7296]{1,0:T(8,128)(2,1)} %shard_map.113), channel_id=1, source_target_pairs={{0,0},{1,1},{2,2},{3,3},{4,4},{5,5},{6,6},{7,7},{8,8},{9,9},{10,10... | collective-permute-start | bytes 350216 | tf_op jit(solution)/shard_map/ppermute | solution.py:39
  13.3 16.7 %collective-permute-start.2 = (bf16[8,7296]{1,0:T(8,128)(2,1)}, bf16[8,7296]{1,0:T(8,128)(2,1)S(1)}, u32[]{:S(2)}, u32[]{:S(2)}) collective-permute-start(bf16[8,7296]{1,0:T(8,128)(2,1)} %shard_map.113), channel_id=1, source_target_pairs={{0,24},{1,25},{2,26},{3,27},{4,28},{5,29},{6,30},{7,31},{8,0},{9,1... | collective-permute-start | bytes 350216 | tf_op jit(solution)/shard_map/ppermute | solution.py:39
  18.1 11.9 %collective-permute-start.3 = (bf16[8,7296]{1,0:T(8,128)(2,1)}, bf16[8,7296]{1,0:T(8,128)(2,1)S(1)}, u32[]{:S(2)}, u32[]{:S(2)}) collective-permute-start(bf16[8,7296]{1,0:T(8,128)(2,1)} %shard_map.113), channel_id=1, source_target_pairs={{0,12},{1,13},{2,14},{3,15},{4,16},{5,17},{6,18},{7,19},{8,20},{9,... | collective-permute-start | bytes 350216 | tf_op jit(solution)/shard_map/ppermute | solution.py:39
  20.6 22.4 %copy-start.2 = (bf16[1,128,7168]{2,1,0:T(8,128)(2,1)S(1)}, bf16[1,128,7168]{2,1,0:T(8,128)(2,1)}, u32[]{:S(2)}) copy-start(bf16[1,128,7168]{2,1,0:T(8,128)(2,1)} %param.19) | copy-start | bytes 5505028
  21.5 2.3 %copy-start.3 = (bf16[1,4096,576]{1,2,0:T(8,128)(2,1)S(1)}, bf16[1,4096,576]{1,2,0:T(8,128)(2,1)}, u32[]{:S(2)}) copy-start(bf16[1,4096,576]{1,2,0:T(8,128)(2,1)} %param.11) | copy-start | bytes 14155780
  23.8 0.9 copy-start.4
  24.7 6.3 %copy-start.1 = (bf16[1,7168,128]{2,1,0:T(8,128)(2,1)S(1)}, bf16[1,7168,128]{2,1,0:T(8,128)(2,1)}, u32[]{:S(2)}) copy-start(bf16[1,7168,128]{2,1,0:T(8,128)(2,1)} %param.18) | copy-start | bytes 5505028
  24.7 22.4 %copy-start = (bf16[1,7168,128]{2,1,0:T(8,128)(2,1)S(1)}, bf16[1,7168,128]{2,1,0:T(8,128)(2,1)}, u32[]{:S(2)}) copy-start(bf16[1,7168,128]{2,1,0:T(8,128)(2,1)} %param.17) | copy-start | bytes 5505028
  31.0 12.1 %collective-permute-start.8 = (bf16[7168,128]{1,0:T(8,128)(2,1)S(1)}, bf16[7168,128]{1,0:T(8,128)(2,1)S(1)}, u32[]{:S(2)}, u32[]{:S(2)}) collective-permute-start(bf16[7168,128]{1,0:T(8,128)(2,1)S(1)} %bitcast.10), channel_id=1, source_target_pairs={{0,64},{1,65},{2,66},{3,67},{4,68},{5,69},{6,70},{7,71},{8,72},{9,... | collective-permute-start | bytes 5505032 | tf_op jit(solution)/shard_map/ppermute | solution.py:39
  31.1 9.3 %collective-permute-start.5 = (bf16[24,7168]{1,0:T(8,128)(2,1)S(1)}, bf16[24,7168]{1,0:T(8,128)(2,1)S(1)}, u32[]{:S(2)}, u32[]{:S(2)}) collective-permute-start(bf16[24,7168]{1,0:T(8,128)(2,1)S(1)} %get-tuple-element.34.refs_0_), channel_id=1, source_target_pairs={{0,128},{1,129},{2,130},{3,131},{4,132},{5,133},{6,134},{7,135},{8... | collective-permute-start | bytes 1032200 | tf_op jit(solution)/shard_map/ppermute | solution.py:39
  31.2 9.7 %collective-permute-start.6 = (bf16[24,7168]{1,0:T(8,128)(2,1)S(1)}, bf16[24,7168]{1,0:T(8,128)(2,1)S(1)}, u32[]{:S(2)}, u32[]{:S(2)}) collective-permute-start(bf16[24,7168]{1,0:T(8,128)(2,1)S(1)} %get-tuple-element.34.refs_0_), channel_id=1, source_target_pairs={{0,1},{1,2},{2,3},{3,0},{4,5},{5,6},{6,7},{7,4},{8,9},{9,10},{10,1... | collective-permute-start | bytes 1032200 | tf_op jit(solution)/shard_map/ppermute | solution.py:39
  34.0 9.1 %collective-permute-start.7 = (bf16[24,7168]{1,0:T(8,128)(2,1)S(1)}, bf16[24,7168]{1,0:T(8,128)(2,1)S(1)}, u32[]{:S(2)}, u32[]{:S(2)}) collective-permute-start(bf16[24,7168]{1,0:T(8,128)(2,1)S(1)} %get-tuple-element.34.refs_0_), channel_id=1, source_target_pairs={{0,3},{1,0},{2,1},{3,2},{4,7},{5,4},{6,5},{7,6},{8,11},{9,8},{10,9... | collective-permute-start | bytes 1032200 | tf_op jit(solution)/shard_map/ppermute | solution.py:39
  43.0 4.1 %collective-permute-start.10 = (bf16[128,7168]{1,0:T(8,128)(2,1)S(1)}, bf16[128,7168]{1,0:T(8,128)(2,1)S(1)}, u32[]{:S(2)}, u32[]{:S(2)}) collective-permute-start(bf16[128,7168]{1,0:T(8,128)(2,1)S(1)} %bitcast.13), channel_id=1, source_target_pairs={{0,64},{1,65},{2,66},{3,67},{4,68},{5,69},{6,70},{7,71},{8,72},{9,... | collective-permute-start | bytes 5505032 | tf_op jit(solution)/shard_map/ppermute | solution.py:39
  43.0 11.6 %collective-permute-start.9 = (bf16[24,7168]{1,0:T(8,128)(2,1)S(1)}, bf16[24,7168]{1,0:T(8,128)(2,1)S(1)}, u32[]{:S(2)}, u32[]{:S(2)}) collective-permute-start(bf16[24,7168]{1,0:T(8,128)(2,1)S(1)} %collective-permute-done.6.refs_2_), channel_id=1, source_target_pairs={{0,129},{1,130},{2,131},{3,128},{4,133},{5,134},{6,135},{7,132},{8... | collective-permute-start | bytes 1032200 | tf_op jit(solution)/shard_map/ppermute | solution.py:39
  46.8 8.5 %collective-permute-start.11 = (bf16[24,7168]{1,0:T(8,128)(2,1)S(1)}, bf16[24,7168]{1,0:T(8,128)(2,1)S(1)}, u32[]{:S(2)}, u32[]{:S(2)}) collective-permute-start(bf16[24,7168]{1,0:T(8,128)(2,1)S(1)} %collective-permute-done.6.refs_2_), channel_id=1, source_target_pairs={{0,1},{1,2},{2,3},{3,0},{4,5},{5,6},{6,7},{7,4},{8,9},{9,10},{10,1... | collective-permute-start | bytes 1032200 | tf_op jit(solution)/shard_map/ppermute | solution.py:39
  46.8 12.2 %collective-permute-start.12 = (bf16[24,7168]{1,0:T(8,128)(2,1)S(1)}, bf16[24,7168]{1,0:T(8,128)(2,1)S(1)}, u32[]{:S(2)}, u32[]{:S(2)}) collective-permute-start(bf16[24,7168]{1,0:T(8,128)(2,1)S(1)} %collective-permute-done.5.refs_1_), channel_id=1, source_target_pairs={{0,1},{1,2},{2,3},{3,0},{4,5},{5,6},{6,7},{7,4},{8,9},{9,10},{10,1... | collective-permute-start | bytes 1032200 | tf_op jit(solution)/shard_map/ppermute | solution.py:39
  47.1 14.0 %collective-permute-start.13 = (bf16[24,7168]{1,0:T(8,128)(2,1)S(1)}, bf16[24,7168]{1,0:T(8,128)(2,1)S(1)}, u32[]{:S(2)}, u32[]{:S(2)}) collective-permute-start(bf16[24,7168]{1,0:T(8,128)(2,1)S(1)} %collective-permute-done.7.refs_3_), channel_id=1, source_target_pairs={{0,128},{1,129},{2,130},{3,131},{4,132},{5,133},{6,134},{7,135},{8... | collective-permute-start | bytes 1032200 | tf_op jit(solution)/shard_map/ppermute | solution.py:39
  64.7 11.9 %collective-permute-start.15 = (bf16[24,7168]{1,0:T(8,128)(2,1)S(1)}, bf16[24,7168]{1,0:T(8,128)(2,1)S(1)}, u32[]{:S(2)}, u32[]{:S(2)}) collective-permute-start(bf16[24,7168]{1,0:T(8,128)(2,1)S(1)} %get-tuple-element.47), channel_id=1, source_target_pairs={{0,131},{1,128},{2,129},{3,130},{4,135},{5,132},{6,133},{7,134},{8... | collective-permute-start | bytes 1032200 | tf_op jit(solution)/shard_map/ppermute | solution.py:39
  66.6 10.5 %collective-permute-start.14 = (bf16[24,7168]{1,0:T(8,128)(2,1)S(1)}, bf16[24,7168]{1,0:T(8,128)(2,1)S(1)}, u32[]{:S(2)}, u32[]{:S(2)}) collective-permute-start(bf16[24,7168]{1,0:T(8,128)(2,1)S(1)} %get-tuple-element.46), channel_id=1, source_target_pairs={{0,3},{1,0},{2,1},{3,2},{4,7},{5,4},{6,5},{7,6},{8,11},{9,8},{10,9... | collective-permute-start | bytes 1032200 | tf_op jit(solution)/shard_map/ppermute | solution.py:39
  66.6 14.0 %collective-permute-start.17 = (bf16[24,7168]{1,0:T(8,128)(2,1)S(1)}, bf16[24,7168]{1,0:T(8,128)(2,1)S(1)}, u32[]{:S(2)}, u32[]{:S(2)}) collective-permute-start(bf16[24,7168]{1,0:T(8,128)(2,1)S(1)} %get-tuple-element.49), channel_id=1, source_target_pairs={{0,128},{1,129},{2,130},{3,131},{4,132},{5,133},{6,134},{7,135},{8... | collective-permute-start | bytes 1032200 | tf_op jit(solution)/shard_map/ppermute | solution.py:39
  67.0 17.2 %collective-permute-start.19 = (bf16[24,7168]{1,0:T(8,128)(2,1)S(1)}, bf16[24,7168]{1,0:T(8,128)(2,1)S(1)}, u32[]{:S(2)}, u32[]{:S(2)}) collective-permute-start(bf16[24,7168]{1,0:T(8,128)(2,1)S(1)} %get-tuple-element.51), channel_id=1, source_target_pairs={{0,3},{1,0},{2,1},{3,2},{4,7},{5,4},{6,5},{7,6},{8,11},{9,8},{10,9... | collective-permute-start | bytes 1032200 | tf_op jit(solution)/shard_map/ppermute | solution.py:39
  77.2 30.7 %copy-start.7 = (s32[8,8]{1,0:T(8,128)S(1)}, s32[8,8]{1,0:T(8,128)}, u32[]{:S(2)}) copy-start(s32[8,8]{1,0:T(8,128)} %ids_ref.1) | copy-start | bytes 772
  77.2 30.7 %copy-start.8 = (f32[8,8]{1,0:T(8,128)S(1)}, f32[8,8]{1,0:T(8,128)}, u32[]{:S(2)}) copy-start(f32[8,8]{1,0:T(8,128)} %param.16) | copy-start | bytes 772
  77.2 9.3 %collective-permute-start.16 = (bf16[24,7168]{1,0:T(8,128)(2,1)S(1)}, bf16[24,7168]{1,0:T(8,128)(2,1)S(1)}, u32[]{:S(2)}, u32[]{:S(2)}) collective-permute-start(bf16[24,7168]{1,0:T(8,128)(2,1)S(1)} %add_convert_fusion.2), channel_id=1, source_target_pairs={{0,3},{1,0},{2,1},{3,2},{4,7},{5,4},{6,5},{7,6},{8,11},{9,8},{10,9... | collective-permute-start | bytes 1032200 | tf_op jit(solution)/shard_map/ppermute | solution.py:39
  80.7 40.7 %copy-start.6 = (bf16[8,7168]{1,0:T(8,128)(2,1)S(1)}, bf16[8,7168]{1,0:T(8,128)(2,1)}, u32[]{:S(2)}) copy-start(bf16[8,7168]{1,0:T(8,128)(2,1)} %stream_ref.1) | copy-start | bytes 344068
  80.7 8.3 %collective-permute-start.18 = (bf16[24,7168]{1,0:T(8,128)(2,1)S(1)}, bf16[24,7168]{1,0:T(8,128)(2,1)S(1)}, u32[]{:S(2)}, u32[]{:S(2)}) collective-permute-start(bf16[24,7168]{1,0:T(8,128)(2,1)S(1)} %add_convert_fusion.1), channel_id=1, source_target_pairs={{0,1},{1,2},{2,3},{3,0},{4,5},{5,6},{6,7},{7,4},{8,9},{9,10},{10,1... | collective-permute-start | bytes 1032200 | tf_op jit(solution)/shard_map/ppermute | solution.py:39
  84.3 9.9 %collective-permute-start.20 = (bf16[24,7168]{1,0:T(8,128)(2,1)S(1)}, bf16[24,7168]{1,0:T(8,128)(2,1)S(1)}, u32[]{:S(2)}, u32[]{:S(2)}) collective-permute-start(bf16[24,7168]{1,0:T(8,128)(2,1)S(1)} %add_convert_fusion), channel_id=1, source_target_pairs={{0,128},{1,129},{2,130},{3,131},{4,132},{5,133},{6,134},{7,135},{8... | collective-permute-start | bytes 1032200 | tf_op jit(solution)/shard_map/ppermute | solution.py:39
  94.5 13.5 %collective-permute-start.24 = (bf16[8,7168]{1,0:T(8,128)(2,1)S(1)}, bf16[8,7168]{1,0:T(8,128)(2,1)S(1)}, u32[]{:S(2)}, u32[]{:S(2)}) collective-permute-start(bf16[8,7168]{1,0:T(8,128)(2,1)S(1)} %get-tuple-element.55), channel_id=1, source_target_pairs={{0,20},{1,21},{2,22},{3,23},{4,24},{5,25},{6,26},{7,27},{8,28},{9,... | collective-permute-start | bytes 344072 | tf_op jit(solution)/shard_map/ppermute | solution.py:39
  98.2 14.6 %collective-permute-start.23 = (bf16[8,7168]{1,0:T(8,128)(2,1)S(1)}, bf16[8,7168]{1,0:T(8,128)(2,1)S(1)}, u32[]{:S(2)}, u32[]{:S(2)}) collective-permute-start(bf16[8,7168]{1,0:T(8,128)(2,1)S(1)} %get-tuple-element.54), channel_id=1, source_target_pairs={{0,8},{1,9},{2,10},{3,11},{4,12},{5,13},{6,14},{7,15},{8,16},{9,17... | collective-permute-start | bytes 344072 | tf_op jit(solution)/shard_map/ppermute | solution.py:39
  101.2 11.6 %collective-permute-start.22 = (bf16[8,7168]{1,0:T(8,128)(2,1)S(1)}, bf16[8,7168]{1,0:T(8,128)(2,1)S(1)}, u32[]{:S(2)}, u32[]{:S(2)}) collective-permute-start(bf16[8,7168]{1,0:T(8,128)(2,1)S(1)} %get-tuple-element.53), channel_id=1, source_target_pairs={{0,28},{1,29},{2,30},{3,31},{4,0},{5,1},{6,2},{7,3},{8,4},{9,5},{1... | collective-permute-start | bytes 344072 | tf_op jit(solution)/shard_map/ppermute | solution.py:39
  101.4 13.8 %collective-permute-start.21 = (bf16[8,7168]{1,0:T(8,128)(2,1)S(1)}, bf16[8,7168]{1,0:T(8,128)(2,1)S(1)}, u32[]{:S(2)}, u32[]{:S(2)}) collective-permute-start(bf16[8,7168]{1,0:T(8,128)(2,1)S(1)} %get-tuple-element.52), channel_id=1, source_target_pairs={{0,0},{1,1},{2,2},{3,3},{4,4},{5,5},{6,6},{7,7},{8,8},{9,9},{10,10... | collective-permute-start | bytes 344072 | tf_op jit(solution)/shard_map/ppermute | solution.py:39
  115.3 1.4 %collective-permute-start.25 = (bf16[8,7168]{1,0:T(8,128)(2,1)S(1)}, bf16[8,7168]{1,0:T(8,128)(2,1)S(1)}, u32[]{:S(2)}, u32[]{:S(2)}) collective-permute-start(bf16[8,7168]{1,0:T(8,128)(2,1)S(1)} %add_convert_fusion.5), channel_id=1, source_target_pairs={{0,64},{1,65},{2,66},{3,67},{4,68},{5,69},{6,70},{7,71},{8,72},{9,... | collective-permute-start | bytes 344072 | tf_op jit(solution)/shard_map/ppermute | solution.py:39
  116.8 4.7 %collective-permute-start.26 = (bf16[8,7168]{1,0:T(8,128)(2,1)S(1)}, bf16[8,7168]{1,0:T(8,128)(2,1)S(1)}, u32[]{:S(2)}, u32[]{:S(2)}) collective-permute-start(bf16[8,7168]{1,0:T(8,128)(2,1)S(1)} %add_convert_fusion.4), channel_id=1, source_target_pairs={{0,128},{1,129},{2,130},{3,131},{4,132},{5,133},{6,134},{7,135},{8... | collective-permute-start | bytes 344072 | tf_op jit(solution)/shard_map/ppermute | solution.py:39

commit v3 on v2

v3 whole, which is shorter than its diff:
```python
import functools

import jax
import jax.numpy as jnp
from jax import lax
from jax.experimental import pallas as pl
from jax.experimental.pallas import tpu as pltpu
from jax.sharding import PartitionSpec as P

LATENT = 512
CAP = 5
ROWS = 8
WIDTH = 7168
PIECES = 8
PIECE = 896
score_scale = 192.0 ** (-0.5)

SIZES = (2, 2, 2, 8, 4)


def pairs(move):
    out = []
    for xl in range(2):
        for c in range(2):
            for xh in range(2):
                for z in range(8):
                    for y in range(4):
                        place = (xl, c, xh, z, y)
                        lin = []
                        for spot in (place, move(*place)):
                            at = 0
                            for part, size in zip(spot, SIZES):
                                at = at * size + part % size
                            lin.append(at)
                        out.append(tuple(lin))
    return out


def send(value, move):
    return lax.ppermute(value, ("sec", "dev"), pairs(move))


def swap_core(value):
    return send(value, lambda xl, c, xh, z, y: (xl, 1 - c, xh, z, y))


STEPS = ((0, 1, -2, 3), (-1, 2, -3, 4))


def spread(value, k, sign):
    def move(xl, c, xh, z, y):
        if xl == c:
            return (xl, c, xh, z + sign * STEPS[c][k], y)
        return (1 - xl, 1 - c, 1 - xh, z + (STEPS[c][k] if sign > 0 else -STEPS[1 - c][k]), y)

    return send(value, move)


ORDER = (0, 1, 2, 3)


VMEM = pl.BlockSpec(memory_space=pltpu.VMEM)
PACKED = jax.ShapeDtypeStruct((CAP * PIECES, PIECE), jnp.bfloat16)
BLOCK = jax.ShapeDtypeStruct((4 * CAP * PIECES, PIECE), jnp.bfloat16)


def limit(mib):
    return pltpu.CompilerParams(vmem_limit_bytes=mib * 1024 * 1024)


def pack_kernel(at_ref, *refs):
    sources, (o0, o1, o2, o3, table_ref) = refs[:4], refs[4:9]
    scratch, sems = refs[9:13], refs[13]
    copies = [
        pltpu.make_async_copy(a, b, sems.at[i]) for i, (a, b) in enumerate(zip(sources, scratch))
    ]
    for copy in copies:
        copy.start()
    for copy in copies:
        copy.wait()
    stream_ref, gain_ref, ids_ref, route_ref = scratch
    lane = lax.broadcasted_iota(jnp.int32, (ROWS, 256), 1)
    target, slot, piece = lane // (CAP * PIECES), (lane // PIECES) % CAP, lane % PIECES
    wanted = jnp.full((ROWS, 256), -1, jnp.int32)
    for k in range(4):
        wanted = jnp.where(target == k, at_ref[k], wanted)
    named = jnp.zeros((ROWS, 256), jnp.float32)
    weight = jnp.zeros((ROWS, 256), jnp.float32)
    ids, route = ids_ref[...], route_ref[...]
    for t in range(ids.shape[1]):
        same = (ids[:, t : t + 1] == wanted).astype(jnp.float32)
        named = named + same
        weight = weight + same * route[:, t : t + 1]
    row = lax.broadcasted_iota(jnp.int32, (ROWS, ROWS), 0)
    col = lax.broadcasted_iota(jnp.int32, (ROWS, ROWS), 1)
    before = jnp.dot((col < row).astype(jnp.float32), named, preferred_element_type=jnp.float32)
    hit = jnp.where(jnp.abs(before - slot.astype(jnp.float32)) < 0.5, named, 0.0)
    table_ref[...] = hit * weight
    picked = jnp.concatenate([jnp.where(piece == p, hit, 0.0) for p in range(PIECES)], axis=0)
    x = stream_ref[...].astype(jnp.float32)
    scale = lax.rsqrt(jnp.sum(x * x, axis=1, keepdims=True) / WIDTH + 1e-06)
    normed = x * scale * gain_ref[...]
    normed = jnp.concatenate(
        [normed[:, p * PIECE : (p + 1) * PIECE] for p in range(PIECES)], axis=0
    )
    out = lax.dot_general(
        picked.astype(jnp.bfloat16),
        normed.astype(jnp.bfloat16),
        (((0,), (0,)), ((), ())),
        preferred_element_type=jnp.float32,
    )
    for k, ref in enumerate((o0, o1, o2, o3)):
        ref[...] = out[k * CAP * PIECES : (k + 1) * CAP * PIECES].astype(jnp.bfloat16)


def pack(at, stream, gain, ids, route):
    return pl.pallas_call(
        pack_kernel,
        out_shape=(PACKED,) * 4 + (jax.ShapeDtypeStruct((ROWS, 256), jnp.float32),),
        in_specs=[pl.BlockSpec(memory_space=pltpu.SMEM)] + [pl.BlockSpec(memory_space=pl.ANY)] * 4,
        out_specs=(VMEM,) * 5,
        scratch_shapes=[pltpu.VMEM(v.shape, v.dtype) for v in (stream, gain, ids, route)]
        + [pltpu.SemaphoreType.DMA((4,))],
        compiler_params=limit(60),
    )(at, stream, gain, ids, route)


def join_kernel(a, b, c, d, out):
    rows = [ref[...].astype(jnp.float32) for ref in (a, b, c, d)]
    out[...] = jnp.concatenate(rows, axis=0).astype(jnp.bfloat16)


def join(parts):
    return pl.pallas_call(
        join_kernel, out_shape=BLOCK, in_specs=[VMEM] * 4, out_specs=VMEM, compiler_params=limit(8)
    )(*parts)


def split_kernel(b0, b1, b2, b3, b4, o0, o1, o2, o3):
    total = b0[...].astype(jnp.float32)
    for ref in (b1, b2, b3, b4):
        total = total + ref[...].astype(jnp.float32)
    for k, ref in enumerate((o0, o1, o2, o3)):
        ref[...] = total[k * CAP * PIECES : (k + 1) * CAP * PIECES].astype(jnp.bfloat16)


def split(blocks):
    return pl.pallas_call(
        split_kernel,
        out_shape=(PACKED,) * 4,
        in_specs=[VMEM] * 5,
        out_specs=(VMEM,) * 4,
        compiler_params=limit(8),
    )(*blocks)


def weigh_kernel(table_ref, a, b, c, d, out):
    rows = [ref[...].astype(jnp.float32) for ref in (a, b, c, d)]
    rows.append(jnp.zeros((256 - 4 * CAP * PIECES, PIECE), jnp.float32))
    rows = jnp.concatenate(rows, axis=0).astype(jnp.bfloat16)
    left = table_ref[...]
    parts = []
    for _ in range(3):
        part = left.astype(jnp.bfloat16).astype(jnp.float32)
        parts.append(part)
        left = left - part
    parts = jnp.concatenate(parts, axis=0)
    piece = lax.broadcasted_iota(jnp.int32, parts.shape, 1) % PIECES
    lhs = jnp.concatenate([jnp.where(piece == p, parts, 0.0) for p in range(PIECES)], axis=0)
    sums = jnp.dot(lhs.astype(jnp.bfloat16), rows, preferred_element_type=jnp.float32)
    for p in range(PIECES):
        at = p * 3 * ROWS
        total = sums[at : at + ROWS]
        total = total + sums[at + ROWS : at + 2 * ROWS] + sums[at + 2 * ROWS : at + 3 * ROWS]
        out[:, p * PIECE : (p + 1) * PIECE] = total.astype(jnp.bfloat16)


def weigh(table, parts):
    return pl.pallas_call(
        weigh_kernel,
        out_shape=jax.ShapeDtypeStruct((ROWS, WIDTH), jnp.bfloat16),
        in_specs=[VMEM] * 5,
        out_specs=VMEM,
        compiler_params=limit(8),
    )(table, *parts)


def expert_kernel(count, rows, *refs):
    blocks = refs[:count]
    wide = refs[count : count + 3]
    down = refs[count + 3]
    outs = refs[count + 4 : -1]
    work = refs[-1]
    size = 4 * CAP * PIECES
    lanes = work.shape[0]
    for i, ref in enumerate(blocks):
        block = ref[...].astype(jnp.float32)
        for t in range(lanes):
            work[t, i * size : (i + 1) * size] = block[:, t * 128 : (t + 1) * 128]
    rest = rows * PIECES - count * size
    for t in range(lanes):
        work[t, count * size :] = jnp.zeros((rest, 128), jnp.float32)
    acc = jnp.zeros((rows, 512), jnp.float32)
    for p in range(PIECES):
        ks = pl.ds(p * PIECE, PIECE)
        x = jnp.concatenate(
            [work[t, pl.ds(p, rows, stride=PIECES), :] for t in range(lanes)], axis=1
        ).astype(jnp.bfloat16)
        w = jnp.concatenate([r[ks, :] for r in wide], axis=1)
        acc = acc + jnp.dot(x, w, preferred_element_type=jnp.float32)
    gate_proj = jnp.concatenate([acc[:, :128], acc[:, 256:384]], axis=1)
    up_proj = jnp.concatenate([acc[:, 128:256], acc[:, 384:]], axis=1)
    hidden = (gate_proj / (1.0 + jnp.exp(-gate_proj)) * up_proj).astype(jnp.bfloat16)
    for p in range(PIECES):
        ks = pl.ds(p * PIECE, PIECE)
        out = jnp.dot(hidden, down[:, ks], preferred_element_type=jnp.float32)
        for t in range(lanes):
            work[t, pl.ds(p, rows, stride=PIECES), :] = out[:, t * 128 : (t + 1) * 128]
    for i, ref in enumerate(outs):
        for t in range(lanes):
            part = work[t, i * size : (i + 1) * size]
            ref[:, t * 128 : (t + 1) * 128] = part.astype(jnp.bfloat16)


def experts(blocks, *weights):
    count = len(blocks)
    rows = -(-count * 4 * CAP // 16) * 16
    return pl.pallas_call(
        functools.partial(expert_kernel, count, rows),
        out_shape=(BLOCK,) * count,
        in_specs=[VMEM] * (count + 4),
        out_specs=(VMEM,) * count,
        scratch_shapes=[pltpu.VMEM((PIECE // 128, rows * PIECES, 128), jnp.float32)],
        cost_estimate=pl.CostEstimate(
            flops=2 * rows * WIDTH * 768,
            bytes_accessed=2 * WIDTH * (768 + 2 * rows),
            transcendentals=rows * 256,
        ),
        compiler_params=limit(32),
    )(*blocks, *weights)


def attend_kernel(length_ref, q_hbm, cache_hbm, out_ref, q_ref, cache_ref, sems):
    parts, _, size = cache_ref.shape
    heads = q_ref.shape[1]
    copies = [pltpu.make_async_copy(q_hbm.at[0], q_ref, sems.at[parts])]
    for part in range(parts):
        copies.append(
            pltpu.make_async_copy(
                cache_hbm.at[0, :, pl.ds(part * size, size)], cache_ref.at[part], sems.at[part]
            )
        )
    for copy in copies:
        copy.start()
    copies[0].wait()
    peak = jnp.full((heads, 1), -1e30, jnp.float32)
    total = jnp.zeros((heads, 1), jnp.float32)
    acc = jnp.zeros((heads, LATENT), jnp.float32)
    query = q_ref[...]
    for part in range(parts):
        copies[part + 1].wait()
        scores = (
            lax.dot_general(
                query,
                cache_ref[part],
                (((0,), (0,)), ((), ())),
                preferred_element_type=jnp.float32,
            )
            * score_scale
        )
        at = part * size + lax.broadcasted_iota(jnp.int32, scores.shape, 1)
        scores = jnp.where(at < length_ref[0], scores, jnp.float32(-1e30))
        new = jnp.maximum(peak, jnp.max(scores, axis=1, keepdims=True))
        powered = jnp.exp(scores - new)
        fade = jnp.exp(peak - new)
        total = total * fade + jnp.sum(powered, axis=1, keepdims=True)
        peak = new
        acc = acc * fade + lax.dot_general(
            powered.astype(jnp.bfloat16),
            cache_ref[part, :LATENT],
            (((1,), (1,)), ((), ())),
            preferred_element_type=jnp.float32,
        )
    out_ref[0] = (acc / total).astype(jnp.bfloat16)


def attend(queries, latent_cache, cache_lengths):
    heads, width = queries.shape[1:]
    length = latent_cache.shape[1]
    parts = 4
    return pl.pallas_call(
        attend_kernel,
        out_shape=jax.ShapeDtypeStruct((1, heads, LATENT), jnp.bfloat16),
        in_specs=[
            pl.BlockSpec(memory_space=pltpu.SMEM),
            pl.BlockSpec(memory_space=pltpu.HBM),
            pl.BlockSpec(memory_space=pltpu.HBM),
        ],
        out_specs=pl.BlockSpec(memory_space=pltpu.VMEM),
        scratch_shapes=[
            pltpu.VMEM((width, heads), jnp.bfloat16),
            pltpu.VMEM((parts, width, length // parts), jnp.bfloat16),
            pltpu.SemaphoreType.DMA((parts + 1,)),
        ],
        cost_estimate=pl.CostEstimate(
            flops=2 * heads * length * (width + LATENT),
            bytes_accessed=2 * length * width,
            transcendentals=heads * length,
        ),
        compiler_params=limit(60),
    )(cache_lengths, jnp.swapaxes(queries, 1, 2), jnp.swapaxes(latent_cache, 1, 2))


def local(
    queries,
    latent_cache,
    cache_lengths,
    stream,
    norm_gain,
    expert_ids,
    route_weights,
    w_gate,
    w_up,
    w_down,
):
    sec = lax.axis_index("sec")
    dev = lax.axis_index("dev")
    xl, core = sec // 2, sec % 2
    xh, z = dev // 32, (dev // 4) % 8

    half = jnp.where(xl == core, xh, 1 - xh) * 8
    at = [half + (z + jnp.where(core == 0, STEPS[0][k], STEPS[1][k])) % 8 for k in range(4)]
    at = jnp.stack(at).astype(jnp.int32)
    *packed, table = pack(at, stream, norm_gain[None, :], expert_ids, route_weights)
    gate_own, up_own, down_own = w_gate[0], w_up[0], w_down[0]
    gate_other = swap_core(gate_own)
    packed[1], up_own, gate_other = lax.optimization_barrier((packed[1], up_own, gate_other))
    arrived = [spread(packed[k], k, 1) for k in range(4)]

    up_other = swap_core(up_own)
    wide_own = jnp.concatenate([gate_own, up_own], axis=1)
    mine = join(arrived)

    def over(value):
        return send(value, lambda xl, c, xh, z, y: (1 - xl, c, xh, z, y))

    def along(value, dy):
        return send(value, lambda xl, c, xh, z, y: (xl, c, xh, z, y + dy))

    mine, down_own, up_other, wide_own = lax.optimization_barrier(
        (mine, down_own, up_other, wide_own)
    )
    down_other = swap_core(down_own)
    x_in = over(mine)
    up_in = along(mine, 1)
    dn_in = along(mine, -1)
    y2_in = along(mine, 2)
    x_in, y2_in, down_other = lax.optimization_barrier((x_in, y2_in, down_other))
    down = jnp.concatenate([down_own, down_other], axis=0)
    weights = (wide_own, gate_other, up_other, down)
    x_up_in = along(x_in, 1)
    x_dn_in = along(x_in, -1)
    x_y2_in = over(y2_in)
    own, x_out, y2_out, up_out, dn_out = experts([mine, x_in, y2_in, up_in, dn_in], *weights)
    x_up_in, own = lax.optimization_barrier((x_up_in, own))
    x_up_out, x_dn_out, x_y2_out = experts([x_up_in, x_dn_in, x_y2_in], *weights)
    up_back = along(up_out, -1)
    dn_back = along(dn_out, 1)
    x_up_back = along(x_up_out, -1)
    x_dn_back = along(x_dn_out, 1)
    x_y2_back = over(x_y2_out)

    def add(*values):
        return sum(v.astype(jnp.float32) for v in values).astype(jnp.bfloat16)

    x_sum = add(x_out, x_up_back, x_dn_back)
    y2_sum = add(y2_out, x_y2_back)
    x_sum, y2_sum, queries = lax.optimization_barrier((x_sum, y2_sum, queries))
    x_back = over(x_sum)
    y2_back = along(y2_sum, 2)
    context = attend(queries, latent_cache, cache_lengths)
    up_back, context = lax.optimization_barrier((up_back, context))
    back = split((own, up_back, dn_back, y2_back, x_back))
    returned = [spread(back[k], k, -1) for k in range(4)]
    part = weigh(table, returned)
    pair = part.astype(jnp.float32) + swap_core(part).astype(jnp.float32)
    pair = pair.astype(jnp.bfloat16)
    far = over(pair)
    full = pair.astype(jnp.float32) + far.astype(jnp.float32)
    mixed = (stream.astype(jnp.float32) + full).astype(jnp.bfloat16)
    return (context, mixed)


def solution(mesh):
    return jax.shard_map(
        local,
        mesh=mesh,
        in_specs=(
            P(("sec", "dev"), None, None),
            P(("sec", "dev"), None, None),
            P(("sec", "dev")),
            P("dev", None),
            P(),
            P("dev", None),
            P("dev", None),
            P("dev", None, "sec"),
            P("dev", None, "sec"),
            P("dev", "sec", None),
        ),
        out_specs=(P(("sec", "dev"), None, None), P("dev", None)),
        check_vma=False,
    )
```

time: 122 us -> 107 us (0.88)
  waiting for transfers between devices: 52.7 us -> 39.5 us
  local copies, waits for them, and re-layouts: 3.28 us -> 0.25 us
  other arithmetic: 1.31 us -> 3.94 us
  Pallas kernels: 15 us -> 13.6 us
    ppermute x27, waiting for transfers between devices: 52.7 us -> 39.5 us  [send(): return lax.ppermute(value, ('sec', 'dev'), pairs(move))]
    unnamed x18 -> x7, local copies, waits for them, and re-layouts: 3.28 us -> 0.13 us
    concatenate x0 -> x1, other arithmetic: none -> 2.45 us  [local(): wide_own = jnp.concatenate([gate_own, up_own], axis=1)]
    pallas_call x5 -> x6, Pallas kernels: 9.76 us -> 8.07 us  [the longest x2 4.84 us: experts(): pl.pallas_call(functools.partial(expert_kernel, count, rows), out_shape=(...]
  transfers between devices with their start and end apart: 27 -> 27, of which waited for: 16 -> 17; matrix products, arithmetic and copies ran while one was open for 0% -> 3% of each run, Pallas kernels for 8% -> 10%
where the time goes in v3:
time: 107 us
  starting transfers between devices  48 us (45%)
  waiting for transfers between devices  39.5 us (37%)
  Pallas kernels  13.6 us (13%)
  other arithmetic  3.94 us (4%)
  between operations  1.48 us (1%)
    ppermute x27, starting transfers between devices, send(): return lax.ppermute(value, ('sec', 'dev'), pairs(move))  48 us
    ppermute x27, waiting for transfers between devices, send(): return lax.ppermute(value, ('sec', 'dev'), pairs(move))  39.5 us
    pallas_call x1, Pallas kernels, attend(): pl.pallas_call(attend_kernel, out_shape=jax.ShapeDtypeStruct((1, heads, L...  5.53 us
    pallas_call x2, Pallas kernels, experts(): pl.pallas_call(functools.partial(expert_kernel, count, rows), out_shape=(...  4.84 us
    pallas_call x1, Pallas kernels, pack(): pl.pallas_call(pack_kernel, out_shape=(PACKED,) * 4 + (jax.ShapeDtypeStru...  2.77 us
    concatenate x1, other arithmetic, local(): wide_own = jnp.concatenate([gate_own, up_own], axis=1)  2.45 us
  transfers between devices with their start and end apart: 27, of which 17 were waited for; matrix products, arithmetic and copies ran while one was open for 3% of the time, Pallas kernels for 10%

profile of v3, /device:TPU:1, one launch (start us, length us, event | category | flops | bytes accessed | tf_op | source)
XLA Modules:
  0.0 106.8 jit_solution(1107036163600176049)
XLA Ops:
  0.6 3.3 %collective-permute-start.1 = (bf16[7168,128]{1,0:T(8,128)(2,1)}, bf16[7168,128]{1,0:T(8,128)(2,1)S(1)}, u32[]{:S(2)}, u32[]{:S(2)}) collective-permute-start(bf16[7168,128]{1,0:T(8,128)(2,1)} %bitcast.11), channel_id=1, source_target_pairs={{0,64},{1,65},{2,66},{3,67},{4,68},{5,69},{6,70},{7,71},{8,72},{9,... | collective-permute-start | bytes 5505032 | tf_op jit(solution)/shard_map/ppermute | solution.py:40
  4.0 0.6 pad_add_fusion.at_ref
  4.6 2.8 %shard_map.113 = (bf16[40,896]{1,0:T(8,128)(2,1)}, bf16[40,896]{1,0:T(8,128)(2,1)}, bf16[40,896]{1,0:T(8,128)(2,1)}, bf16[40,896]{1,0:T(8,128)(2,1)}, f32[8,256]{1,0:T(8,128)}) custom-call(s32[4]{0:T(128)} %pad_add_fusion.at_ref, bf16[8,7168]{1,0:T(8,128)(2,1)} %refs_0_.1, f32[1,7168]{1,0:T(1,128)} %bitcast.18, s32[8,8]{1,0:T(8,128)} %refs_2_.1, f32[8,8]{1,0:T(8,128)} %refs_3_.1), custom_call_target="tpu_custom_call" | custom-call | tf_op jit(solution)/shard_map/pallas_call | solution.py:117
  7.3 0.2 collective-permute-done.1.refs_6_.refs_4_
  7.6 0.4 collective-permute-start.5
  8.0 8.0 %collective-permute-start = (bf16[40,896]{1,0:T(8,128)(2,1)}, bf16[40,896]{1,0:T(8,128)(2,1)S(1)}, u32[]{:S(2)}, u32[]{:S(2)}) collective-permute-start(bf16[40,896]{1,0:T(8,128)(2,1)} %get-tuple-element.36), channel_id=1, source_target_pairs={{0,0},{1,1},{2,2},{3,3},{4,4},{5,5},{6,6},{7,7},{8,8},{9,9},{10,10... | collective-permute-start | bytes 215048 | tf_op jit(solution)/shard_map/ppermute | solution.py:40
  15.9 1.4 %collective-permute-start.3 = (bf16[40,896]{1,0:T(8,128)(2,1)}, bf16[40,896]{1,0:T(8,128)(2,1)S(1)}, u32[]{:S(2)}, u32[]{:S(2)}) collective-permute-start(bf16[40,896]{1,0:T(8,128)(2,1)} %get-tuple-element.39), channel_id=1, source_target_pairs={{0,24},{1,25},{2,26},{3,27},{4,28},{5,29},{6,30},{7,31},{8,0},{9,1... | collective-permute-start | bytes 215048 | tf_op jit(solution)/shard_map/ppermute | solution.py:40
  17.3 1.6 %collective-permute-start.4 = (bf16[40,896]{1,0:T(8,128)(2,1)}, bf16[40,896]{1,0:T(8,128)(2,1)S(1)}, u32[]{:S(2)}, u32[]{:S(2)}) collective-permute-start(bf16[40,896]{1,0:T(8,128)(2,1)} %get-tuple-element.40), channel_id=1, source_target_pairs={{0,12},{1,13},{2,14},{3,15},{4,16},{5,17},{6,18},{7,19},{8,20},{9,... | collective-permute-start | bytes 215048 | tf_op jit(solution)/shard_map/ppermute | solution.py:40
  18.9 2.4 %collective-permute-start.2 = (bf16[40,896]{1,0:T(8,128)(2,1)}, bf16[40,896]{1,0:T(8,128)(2,1)S(1)}, u32[]{:S(2)}, u32[]{:S(2)}) collective-permute-start(bf16[40,896]{1,0:T(8,128)(2,1)} %get-tuple-element.38), channel_id=1, source_target_pairs={{0,4},{1,5},{2,6},{3,7},{4,8},{5,9},{6,10},{7,11},{8,12},{9,13},{1... | collective-permute-start | bytes 215048 | tf_op jit(solution)/shard_map/ppermute | solution.py:40
  21.3 2.4 %pad_maximum_fusion.refs_5_.refs_3_ = bf16[7168,256]{1,0:T(8,128)(2,1)S(1)} fusion(bf16[7168,128]{1,0:T(8,128)(2,1)} %bitcast.14, bf16[7168,128]{1,0:T(8,128)(2,1)} %bitcast.12), kind=kLoop, calls=%fused_computation | loop fusion | flops 7340032 | bytes 7340032 | tf_op jit(solution)/shard_map/concatenate | solution.py:341
  23.8 5.2 %collective-permute-done.4.d = bf16[40,896]{1,0:T(8,128)(2,1)S(1)} collective-permute-done((bf16[40,896]{1,0:T(8,128)(2,1)}, bf16[40,896]{1,0:T(8,128)(2,1)S(1)}, u32[]{:S(2)}, u32[]{:S(2)}) %collective-permute-start.4) | collective-permute-done | bytes 71712 | tf_op jit(solution)/shard_map/ppermute | solution.py:40
  29.3 3.0 %collective-permute-start.7 = (bf16[160,896]{1,0:T(8,128)(2,1)S(1)}, bf16[160,896]{1,0:T(8,128)(2,1)S(1)}, u32[]{:S(2)}, u32[]{:S(2)}) collective-permute-start(bf16[160,896]{1,0:T(8,128)(2,1)S(1)} %shard_map.114.refs_0_), channel_id=1, source_target_pairs={{0,2},{1,3},{2,0},{3,1},{4,6},{5,7},{6,4},{7,5},{8,10},{9,11},{10,... | collective-permute-start | bytes 860168 | tf_op jit(solution)/shard_map/ppermute | solution.py:40
  32.3 0.1 constant_dynamic-update-slice_fusion.1
  32.4 0.9 collective-permute-start.10
  33.3 0.7 collective-permute-start.9
  34.0 3.3 %collective-permute-done.6.refs_1_ = bf16[160,896]{1,0:T(8,128)(2,1)S(1)} collective-permute-done((bf16[160,896]{1,0:T(8,128)(2,1)S(1)}, bf16[160,896]{1,0:T(8,128)(2,1)S(1)}, u32[]{:S(2)}, u32[]{:S(2)}) %collective-permute-start.6) | collective-permute-done | bytes 286752 | tf_op jit(solution)/shard_map/ppermute | solution.py:40
  37.3 1.7 %collective-permute-done.7.refs_2_ = bf16[160,896]{1,0:T(8,128)(2,1)S(1)} collective-permute-done((bf16[160,896]{1,0:T(8,128)(2,1)S(1)}, bf16[160,896]{1,0:T(8,128)(2,1)S(1)}, u32[]{:S(2)}, u32[]{:S(2)}) %collective-permute-start.7) | collective-permute-done | bytes 286752 | tf_op jit(solution)/shard_map/ppermute | solution.py:40
  39.0 1.3 %collective-permute-start.12 = (bf16[160,896]{1,0:T(8,128)(2,1)S(1)}, bf16[160,896]{1,0:T(8,128)(2,1)S(1)}, u32[]{:S(2)}, u32[]{:S(2)}) collective-permute-start(bf16[160,896]{1,0:T(8,128)(2,1)S(1)} %collective-permute-done.6.refs_1_), channel_id=1, source_target_pairs={{0,1},{1,2},{2,3},{3,0},{4,5},{5,6},{6,7},{7,4},{8,9},{9,10},{10,1... | collective-permute-start | bytes 860168 | tf_op jit(solution)/shard_map/ppermute | solution.py:40
  40.3 1.4 %collective-permute-start.13 = (bf16[160,896]{1,0:T(8,128)(2,1)S(1)}, bf16[160,896]{1,0:T(8,128)(2,1)S(1)}, u32[]{:S(2)}, u32[]{:S(2)}) collective-permute-start(bf16[160,896]{1,0:T(8,128)(2,1)S(1)} %collective-permute-done.6.refs_1_), channel_id=1, source_target_pairs={{0,3},{1,0},{2,1},{3,2},{4,7},{5,4},{6,5},{7,6},{8,11},{9,8},{10,9... | collective-permute-start | bytes 860168 | tf_op jit(solution)/shard_map/ppermute | solution.py:40
  41.8 0.9 collective-permute-start.14
  42.7 0.1 constant_dynamic-update-slice_fusion.refs_8_.refs_6_
  42.9 2.7 %collective-permute-done.10.refs_4_ = bf16[160,896]{1,0:T(8,128)(2,1)S(1)} collective-permute-done((bf16[160,896]{1,0:T(8,128)(2,1)S(1)}, bf16[160,896]{1,0:T(8,128)(2,1)S(1)}, u32[]{:S(2)}, u32[]{:S(2)}) %collective-permute-start.10) | collective-permute-done | bytes 286752 | tf_op jit(solution)/shard_map/ppermute | solution.py:40
  45.5 0.3 collective-permute-done.9.refs_3_
  45.8 2.6 %shard_map.115 = (bf16[160,896]{1,0:T(8,128)(2,1)S(1)}, bf16[160,896]{1,0:T(8,128)(2,1)S(1)}, bf16[160,896]{1,0:T(8,128)(2,1)S(1)}, bf16[160,896]{1,0:T(8,128)(2,1)S(1)}, bf16[160,896]{1,0:T(8,128)(2,1)S(1)}) custom-call(bf16[160,896]{1,0:T(8,128)(2,1)S(1)} %shard_map.114.refs_0_, bf16[160,896]{1,0:T(8,128)(2,1)S(1)} %collective-permute-done.6.refs_1_, ...), custom_call_target="tpu_custom_call" | custom-call | flops 1233125376 | bytes 14221312 | tf_op jit(solution)/shard_map/pallas_call | solution.py:228
  48.4 3.5 %collective-permute-done.12.refs_0_ = bf16[160,896]{1,0:T(8,128)(2,1)S(1)} collective-permute-done((bf16[160,896]{1,0:T(8,128)(2,1)S(1)}, bf16[160,896]{1,0:T(8,128)(2,1)S(1)}, u32[]{:S(2)}, u32[]{:S(2)}) %collective-permute-start.12) | collective-permute-done | bytes 286752 | tf_op jit(solution)/shard_map/ppermute | solution.py:40
  51.9 2.2 %shard_map.116 = (bf16[160,896]{1,0:T(8,128)(2,1)S(1)}, bf16[160,896]{1,0:T(8,128)(2,1)S(1)}, bf16[160,896]{1,0:T(8,128)(2,1)S(1)}) custom-call(bf16[160,896]{1,0:T(8,128)(2,1)S(1)} %collective-permute-done.12.refs_0_, bf16[160,896]{1,0:T(8,128)(2,1)S(1)} %collective-permute-done.13.refs_1_, bf16[160,896]{1,0:T(8,128)(2,1)S(1)} %collective-permute-done.14.refs_2_, ...), custom_call_target="tpu_custom_call" | custom-call | flops 704643072 | bytes 12845056 | tf_op jit(solution)/shard_map/pallas_call | solution.py:228
  54.2 1.4 %collective-permute-start.17 = (bf16[160,896]{1,0:T(8,128)(2,1)S(1)}, bf16[160,896]{1,0:T(8,128)(2,1)S(1)}, u32[]{:S(2)}, u32[]{:S(2)}) collective-permute-start(bf16[160,896]{1,0:T(8,128)(2,1)S(1)} %get-tuple-element.57), channel_id=1, source_target_pairs={{0,128},{1,129},{2,130},{3,131},{4,132},{5,133},{6,134},{7,135},{8... | collective-permute-start | bytes 860168 | tf_op jit(solution)/shard_map/ppermute | solution.py:40
  55.5 2.8 %collective-permute-start.15 = (bf16[160,896]{1,0:T(8,128)(2,1)S(1)}, bf16[160,896]{1,0:T(8,128)(2,1)S(1)}, u32[]{:S(2)}, u32[]{:S(2)}) collective-permute-start(bf16[160,896]{1,0:T(8,128)(2,1)S(1)} %get-tuple-element.54), channel_id=1, source_target_pairs={{0,3},{1,0},{2,1},{3,2},{4,7},{5,4},{6,5},{7,6},{8,11},{9,8},{10,9... | collective-permute-start | bytes 860168 | tf_op jit(solution)/shard_map/ppermute | solution.py:40
  58.3 2.7 %collective-permute-start.11 = (bf16[160,896]{1,0:T(8,128)(2,1)S(1)}, bf16[160,896]{1,0:T(8,128)(2,1)S(1)}, u32[]{:S(2)}, u32[]{:S(2)}) collective-permute-start(bf16[160,896]{1,0:T(8,128)(2,1)S(1)} %get-tuple-element.50), channel_id=1, source_target_pairs={{0,3},{1,0},{2,1},{3,2},{4,7},{5,4},{6,5},{7,6},{8,11},{9,8},{10,9... | collective-permute-start | bytes 860168 | tf_op jit(solution)/shard_map/ppermute | solution.py:40
  61.0 0.7 collective-permute-done.17
  61.8 1.9 %collective-permute-done.15 = bf16[160,896]{1,0:T(8,128)(2,1)S(1)} collective-permute-done((bf16[160,896]{1,0:T(8,128)(2,1)S(1)}, bf16[160,896]{1,0:T(8,128)(2,1)S(1)}, u32[]{:S(2)}, u32[]{:S(2)}) %collective-permute-start.15) | collective-permute-done | bytes 286752 | tf_op jit(solution)/shard_map/ppermute | solution.py:40
  63.7 3.1 %collective-permute-done.16 = bf16[160,896]{1,0:T(8,128)(2,1)S(1)} collective-permute-done((bf16[160,896]{1,0:T(8,128)(2,1)S(1)}, bf16[160,896]{1,0:T(8,128)(2,1)S(1)}, u32[]{:S(2)}, u32[]{:S(2)}) %collective-permute-start.16) | collective-permute-done | bytes 286752 | tf_op jit(solution)/shard_map/ppermute | solution.py:40
  66.8 0.1 add_convert_fusion.1
  67.0 0.2 collective-permute-start.20
  67.9 5.5 %shard_map.117 = bf16[1,128,512]{2,1,0:T(8,128)(2,1)} custom-call(s32[1]{0:T(128)S(6)} %copy.13.length_ref, bf16[1,576,128]{2,1,0:T(8,128)(2,1)} %bitcast.17, bf16[1,576,4096]{2,1,0:T(8,128)(2,1)} %bitcast.10), custom_call_target="tpu_custom_call" | custom-call | flops 1140850688 | bytes 4718592 | tf_op jit(solution)/shard_map/pallas_call | solution.py:291
  73.4 0.6 collective-permute-done.18.b2
  74.0 3.9 %collective-permute-done.19.b3 = bf16[160,896]{1,0:T(8,128)(2,1)S(1)} collective-permute-done((bf16[160,896]{1,0:T(8,128)(2,1)S(1)}, bf16[160,896]{1,0:T(8,128)(2,1)S(1)}, u32[]{:S(2)}, u32[]{:S(2)}) %collective-permute-start.19) | collective-permute-done | bytes 286752 | tf_op jit(solution)/shard_map/ppermute | solution.py:40
  77.9 0.2 shard_map.118
  78.1 6.6 %collective-permute-start.21 = (bf16[40,896]{1,0:T(8,128)(2,1)S(1)}, bf16[40,896]{1,0:T(8,128)(2,1)S(1)}, u32[]{:S(2)}, u32[]{:S(2)}) collective-permute-start(bf16[40,896]{1,0:T(8,128)(2,1)S(1)} %get-tuple-element.66), channel_id=1, source_target_pairs={{0,0},{1,1},{2,2},{3,3},{4,4},{5,5},{6,6},{7,7},{8,8},{9,9},{10,10... | collective-permute-start | bytes 215048 | tf_op jit(solution)/shard_map/ppermute | solution.py:40
  84.7 1.7 %collective-permute-start.22 = (bf16[40,896]{1,0:T(8,128)(2,1)S(1)}, bf16[40,896]{1,0:T(8,128)(2,1)S(1)}, u32[]{:S(2)}, u32[]{:S(2)}) collective-permute-start(bf16[40,896]{1,0:T(8,128)(2,1)S(1)} %get-tuple-element.67), channel_id=1, source_target_pairs={{0,28},{1,29},{2,30},{3,31},{4,0},{5,1},{6,2},{7,3},{8,4},{9,5},{1... | collective-permute-start | bytes 215048 | tf_op jit(solution)/shard_map/ppermute | solution.py:40
  86.5 3.3 %collective-permute-start.23 = (bf16[40,896]{1,0:T(8,128)(2,1)S(1)}, bf16[40,896]{1,0:T(8,128)(2,1)S(1)}, u32[]{:S(2)}, u32[]{:S(2)}) collective-permute-start(bf16[40,896]{1,0:T(8,128)(2,1)S(1)} %get-tuple-element.68), channel_id=1, source_target_pairs={{0,8},{1,9},{2,10},{3,11},{4,12},{5,13},{6,14},{7,15},{8,16},{9,17... | collective-permute-start | bytes 215048 | tf_op jit(solution)/shard_map/ppermute | solution.py:40
  89.8 3.6 %collective-permute-start.24 = (bf16[40,896]{1,0:T(8,128)(2,1)S(1)}, bf16[40,896]{1,0:T(8,128)(2,1)S(1)}, u32[]{:S(2)}, u32[]{:S(2)}) collective-permute-start(bf16[40,896]{1,0:T(8,128)(2,1)S(1)} %get-tuple-element.69), channel_id=1, source_target_pairs={{0,20},{1,21},{2,22},{3,23},{4,24},{5,25},{6,26},{7,27},{8,28},{9,... | collective-permute-start | bytes 215048 | tf_op jit(solution)/shard_map/ppermute | solution.py:40
  93.4 3.3 %collective-permute-done.23.c = bf16[40,896]{1,0:T(8,128)(2,1)S(1)} collective-permute-done((bf16[40,896]{1,0:T(8,128)(2,1)S(1)}, bf16[40,896]{1,0:T(8,128)(2,1)S(1)}, u32[]{:S(2)}, u32[]{:S(2)}) %collective-permute-start.23) | collective-permute-done | bytes 71712 | tf_op jit(solution)/shard_map/ppermute | solution.py:40
  96.6 3.0 %collective-permute-done.24.d = bf16[40,896]{1,0:T(8,128)(2,1)S(1)} collective-permute-done((bf16[40,896]{1,0:T(8,128)(2,1)S(1)}, bf16[40,896]{1,0:T(8,128)(2,1)S(1)}, u32[]{:S(2)}, u32[]{:S(2)}) %collective-permute-start.24) | collective-permute-done | bytes 71712 | tf_op jit(solution)/shard_map/ppermute | solution.py:40
  99.7 0.3 shard_map.119
  100.0 1.3 %collective-permute-done.25 = bf16[8,7168]{1,0:T(8,128)(2,1)S(1)} collective-permute-done((bf16[8,7168]{1,0:T(8,128)(2,1)S(1)}, bf16[8,7168]{1,0:T(8,128)(2,1)S(1)}, u32[]{:S(2)}, u32[]{:S(2)}) %collective-permute-start.25) | collective-permute-done | bytes 114720 | tf_op jit(solution)/shard_map/ppermute | solution.py:40
  101.5 4.6 %collective-permute-done.26 = bf16[8,7168]{1,0:T(8,128)(2,1)S(1)} collective-permute-done((bf16[8,7168]{1,0:T(8,128)(2,1)S(1)}, bf16[8,7168]{1,0:T(8,128)(2,1)S(1)}, u32[]{:S(2)}, u32[]{:S(2)}) %collective-permute-start.26) | collective-permute-done | bytes 114720 | tf_op jit(solution)/shard_map/ppermute | solution.py:40
  106.1 0.7 add_convert_fusion.2
  (27 shorter events, 0.7 us)
Async XLA Ops:
  0.6 7.0 %collective-permute-start.1 = (bf16[7168,128]{1,0:T(8,128)(2,1)}, bf16[7168,128]{1,0:T(8,128)(2,1)S(1)}, u32[]{:S(2)}, u32[]{:S(2)}) collective-permute-start(bf16[7168,128]{1,0:T(8,128)(2,1)} %bitcast.11), channel_id=1, source_target_pairs={{0,64},{1,65},{2,66},{3,67},{4,68},{5,69},{6,70},{7,71},{8,72},{9,... | collective-permute-start | bytes 5505032 | tf_op jit(solution)/shard_map/ppermute | solution.py:40
  7.6 21.5 %collective-permute-start.5 = (bf16[7168,128]{1,0:T(8,128)(2,1)}, bf16[7168,128]{1,0:T(8,128)(2,1)S(1)}, u32[]{:S(2)}, u32[]{:S(2)}) collective-permute-start(bf16[7168,128]{1,0:T(8,128)(2,1)} %bitcast.13), channel_id=1, source_target_pairs={{0,64},{1,65},{2,66},{3,67},{4,68},{5,69},{6,70},{7,71},{8,72},{9,... | collective-permute-start | bytes 5505032 | tf_op jit(solution)/shard_map/ppermute | solution.py:40
  8.0 15.8 %collective-permute-start = (bf16[40,896]{1,0:T(8,128)(2,1)}, bf16[40,896]{1,0:T(8,128)(2,1)S(1)}, u32[]{:S(2)}, u32[]{:S(2)}) collective-permute-start(bf16[40,896]{1,0:T(8,128)(2,1)} %get-tuple-element.36), channel_id=1, source_target_pairs={{0,0},{1,1},{2,2},{3,3},{4,4},{5,5},{6,6},{7,7},{8,8},{9,9},{10,10... | collective-permute-start | bytes 215048 | tf_op jit(solution)/shard_map/ppermute | solution.py:40
  15.9 7.9 %collective-permute-start.3 = (bf16[40,896]{1,0:T(8,128)(2,1)}, bf16[40,896]{1,0:T(8,128)(2,1)S(1)}, u32[]{:S(2)}, u32[]{:S(2)}) collective-permute-start(bf16[40,896]{1,0:T(8,128)(2,1)} %get-tuple-element.39), channel_id=1, source_target_pairs={{0,24},{1,25},{2,26},{3,27},{4,28},{5,29},{6,30},{7,31},{8,0},{9,1... | collective-permute-start | bytes 215048 | tf_op jit(solution)/shard_map/ppermute | solution.py:40
  17.3 11.8 %copy-start.1 = (bf16[1,128,7168]{2,1,0:T(8,128)(2,1)S(1)}, bf16[1,128,7168]{2,1,0:T(8,128)(2,1)}, u32[]{:S(2)}) copy-start(bf16[1,128,7168]{2,1,0:T(8,128)(2,1)} %param.19) | copy-start | bytes 5505028
  17.3 11.7 %collective-permute-start.4 = (bf16[40,896]{1,0:T(8,128)(2,1)}, bf16[40,896]{1,0:T(8,128)(2,1)S(1)}, u32[]{:S(2)}, u32[]{:S(2)}) collective-permute-start(bf16[40,896]{1,0:T(8,128)(2,1)} %get-tuple-element.40), channel_id=1, source_target_pairs={{0,12},{1,13},{2,14},{3,15},{4,16},{5,17},{6,18},{7,19},{8,20},{9,... | collective-permute-start | bytes 215048 | tf_op jit(solution)/shard_map/ppermute | solution.py:40
  18.9 10.1 %collective-permute-start.2 = (bf16[40,896]{1,0:T(8,128)(2,1)}, bf16[40,896]{1,0:T(8,128)(2,1)S(1)}, u32[]{:S(2)}, u32[]{:S(2)}) collective-permute-start(bf16[40,896]{1,0:T(8,128)(2,1)} %get-tuple-element.38), channel_id=1, source_target_pairs={{0,4},{1,5},{2,6},{3,7},{4,8},{5,9},{6,10},{7,11},{8,12},{9,13},{1... | collective-permute-start | bytes 215048 | tf_op jit(solution)/shard_map/ppermute | solution.py:40
  29.1 9.9 %collective-permute-start.8 = (bf16[128,7168]{1,0:T(8,128)(2,1)S(1)}, bf16[128,7168]{1,0:T(8,128)(2,1)S(1)}, u32[]{:S(2)}, u32[]{:S(2)}) collective-permute-start(bf16[128,7168]{1,0:T(8,128)(2,1)S(1)} %bitcast.15), channel_id=1, source_target_pairs={{0,64},{1,65},{2,66},{3,67},{4,68},{5,69},{6,70},{7,71},{8,72},{9,... | collective-permute-start | bytes 5505032 | tf_op jit(solution)/shard_map/ppermute | solution.py:40
  29.2 8.1 %collective-permute-start.6 = (bf16[160,896]{1,0:T(8,128)(2,1)S(1)}, bf16[160,896]{1,0:T(8,128)(2,1)S(1)}, u32[]{:S(2)}, u32[]{:S(2)}) collective-permute-start(bf16[160,896]{1,0:T(8,128)(2,1)S(1)} %shard_map.114.refs_0_), channel_id=1, source_target_pairs={{0,128},{1,129},{2,130},{3,131},{4,132},{5,133},{6,134},{7,135},{8... | collective-permute-start | bytes 860168 | tf_op jit(solution)/shard_map/ppermute | solution.py:40
  29.3 9.7 %collective-permute-start.7 = (bf16[160,896]{1,0:T(8,128)(2,1)S(1)}, bf16[160,896]{1,0:T(8,128)(2,1)S(1)}, u32[]{:S(2)}, u32[]{:S(2)}) collective-permute-start(bf16[160,896]{1,0:T(8,128)(2,1)S(1)} %shard_map.114.refs_0_), channel_id=1, source_target_pairs={{0,2},{1,3},{2,0},{3,1},{4,6},{5,7},{6,4},{7,5},{8,10},{9,11},{10,... | collective-permute-start | bytes 860168 | tf_op jit(solution)/shard_map/ppermute | solution.py:40
  32.4 13.1 %collective-permute-start.10 = (bf16[160,896]{1,0:T(8,128)(2,1)S(1)}, bf16[160,896]{1,0:T(8,128)(2,1)S(1)}, u32[]{:S(2)}, u32[]{:S(2)}) collective-permute-start(bf16[160,896]{1,0:T(8,128)(2,1)S(1)} %shard_map.114.refs_0_), channel_id=1, source_target_pairs={{0,3},{1,0},{2,1},{3,2},{4,7},{5,4},{6,5},{7,6},{8,11},{9,8},{10,9... | collective-permute-start | bytes 860168 | tf_op jit(solution)/shard_map/ppermute | solution.py:40
  33.3 12.5 %collective-permute-start.9 = (bf16[160,896]{1,0:T(8,128)(2,1)S(1)}, bf16[160,896]{1,0:T(8,128)(2,1)S(1)}, u32[]{:S(2)}, u32[]{:S(2)}) collective-permute-start(bf16[160,896]{1,0:T(8,128)(2,1)S(1)} %shard_map.114.refs_0_), channel_id=1, source_target_pairs={{0,1},{1,2},{2,3},{3,0},{4,5},{5,6},{6,7},{7,4},{8,9},{9,10},{10,1... | collective-permute-start | bytes 860168 | tf_op jit(solution)/shard_map/ppermute | solution.py:40
  39.0 12.9 %collective-permute-start.12 = (bf16[160,896]{1,0:T(8,128)(2,1)S(1)}, bf16[160,896]{1,0:T(8,128)(2,1)S(1)}, u32[]{:S(2)}, u32[]{:S(2)}) collective-permute-start(bf16[160,896]{1,0:T(8,128)(2,1)S(1)} %collective-permute-done.6.refs_1_), channel_id=1, source_target_pairs={{0,1},{1,2},{2,3},{3,0},{4,5},{5,6},{6,7},{7,4},{8,9},{9,10},{10,1... | collective-permute-start | bytes 860168 | tf_op jit(solution)/shard_map/ppermute | solution.py:40
  40.3 11.6 %collective-permute-start.13 = (bf16[160,896]{1,0:T(8,128)(2,1)S(1)}, bf16[160,896]{1,0:T(8,128)(2,1)S(1)}, u32[]{:S(2)}, u32[]{:S(2)}) collective-permute-start(bf16[160,896]{1,0:T(8,128)(2,1)S(1)} %collective-permute-done.6.refs_1_), channel_id=1, source_target_pairs={{0,3},{1,0},{2,1},{3,2},{4,7},{5,4},{6,5},{7,6},{8,11},{9,8},{10,9... | collective-permute-start | bytes 860168 | tf_op jit(solution)/shard_map/ppermute | solution.py:40
  41.8 10.2 %collective-permute-start.14 = (bf16[160,896]{1,0:T(8,128)(2,1)S(1)}, bf16[160,896]{1,0:T(8,128)(2,1)S(1)}, u32[]{:S(2)}, u32[]{:S(2)}) collective-permute-start(bf16[160,896]{1,0:T(8,128)(2,1)S(1)} %collective-permute-done.7.refs_2_), channel_id=1, source_target_pairs={{0,128},{1,129},{2,130},{3,131},{4,132},{5,133},{6,134},{7,135},{8... | collective-permute-start | bytes 860168 | tf_op jit(solution)/shard_map/ppermute | solution.py:40
  54.2 7.6 %collective-permute-start.17 = (bf16[160,896]{1,0:T(8,128)(2,1)S(1)}, bf16[160,896]{1,0:T(8,128)(2,1)S(1)}, u32[]{:S(2)}, u32[]{:S(2)}) collective-permute-start(bf16[160,896]{1,0:T(8,128)(2,1)S(1)} %get-tuple-element.57), channel_id=1, source_target_pairs={{0,128},{1,129},{2,130},{3,131},{4,132},{5,133},{6,134},{7,135},{8... | collective-permute-start | bytes 860168 | tf_op jit(solution)/shard_map/ppermute | solution.py:40
  55.5 8.2 %collective-permute-start.15 = (bf16[160,896]{1,0:T(8,128)(2,1)S(1)}, bf16[160,896]{1,0:T(8,128)(2,1)S(1)}, u32[]{:S(2)}, u32[]{:S(2)}) collective-permute-start(bf16[160,896]{1,0:T(8,128)(2,1)S(1)} %get-tuple-element.54), channel_id=1, source_target_pairs={{0,3},{1,0},{2,1},{3,2},{4,7},{5,4},{6,5},{7,6},{8,11},{9,8},{10,9... | collective-permute-start | bytes 860168 | tf_op jit(solution)/shard_map/ppermute | solution.py:40
  58.3 8.5 %collective-permute-start.16 = (bf16[160,896]{1,0:T(8,128)(2,1)S(1)}, bf16[160,896]{1,0:T(8,128)(2,1)S(1)}, u32[]{:S(2)}, u32[]{:S(2)}) collective-permute-start(bf16[160,896]{1,0:T(8,128)(2,1)S(1)} %get-tuple-element.55), channel_id=1, source_target_pairs={{0,1},{1,2},{2,3},{3,0},{4,5},{5,6},{6,7},{7,4},{8,9},{9,10},{10,1... | collective-permute-start | bytes 860168 | tf_op jit(solution)/shard_map/ppermute | solution.py:40
  58.3 15.1 %collective-permute-start.11 = (bf16[160,896]{1,0:T(8,128)(2,1)S(1)}, bf16[160,896]{1,0:T(8,128)(2,1)S(1)}, u32[]{:S(2)}, u32[]{:S(2)}) collective-permute-start(bf16[160,896]{1,0:T(8,128)(2,1)S(1)} %get-tuple-element.50), channel_id=1, source_target_pairs={{0,3},{1,0},{2,1},{3,2},{4,7},{5,4},{6,5},{7,6},{8,11},{9,8},{10,9... | collective-permute-start | bytes 860168 | tf_op jit(solution)/shard_map/ppermute | solution.py:40
  61.0 13.0 %collective-permute-start.18 = (bf16[160,896]{1,0:T(8,128)(2,1)S(1)}, bf16[160,896]{1,0:T(8,128)(2,1)S(1)}, u32[]{:S(2)}, u32[]{:S(2)}) collective-permute-start(bf16[160,896]{1,0:T(8,128)(2,1)S(1)} %get-tuple-element.63), channel_id=1, source_target_pairs={{0,1},{1,2},{2,3},{3,0},{4,5},{5,6},{6,7},{7,4},{8,9},{9,10},{10,1... | collective-permute-start | bytes 860168 | tf_op jit(solution)/shard_map/ppermute | solution.py:40
  66.8 32.8 %copy-start = (f32[8,256]{1,0:T(8,128)S(1)}, f32[8,256]{1,0:T(8,128)}, u32[]{:S(2)}) copy-start(f32[8,256]{1,0:T(8,128)} %get-tuple-element.60.table_ref) | copy-start | bytes 24580
  66.9 39.1 %copy-start.2 = (bf16[8,7168]{1,0:T(8,128)(2,1)S(1)}, bf16[8,7168]{1,0:T(8,128)(2,1)}, u32[]{:S(2)}) copy-start(bf16[8,7168]{1,0:T(8,128)(2,1)} %refs_0_.1) | copy-start | bytes 344068
  66.9 10.9 %collective-permute-start.19 = (bf16[160,896]{1,0:T(8,128)(2,1)S(1)}, bf16[160,896]{1,0:T(8,128)(2,1)S(1)}, u32[]{:S(2)}, u32[]{:S(2)}) collective-permute-start(bf16[160,896]{1,0:T(8,128)(2,1)S(1)} %add_convert_fusion), channel_id=1, source_target_pairs={{0,2},{1,3},{2,0},{3,1},{4,6},{5,7},{6,4},{7,5},{8,10},{9,11},{10,... | collective-permute-start | bytes 860168 | tf_op jit(solution)/shard_map/ppermute | solution.py:40
  67.0 10.8 %collective-permute-start.20 = (bf16[160,896]{1,0:T(8,128)(2,1)S(1)}, bf16[160,896]{1,0:T(8,128)(2,1)S(1)}, u32[]{:S(2)}, u32[]{:S(2)}) collective-permute-start(bf16[160,896]{1,0:T(8,128)(2,1)S(1)} %add_convert_fusion.1), channel_id=1, source_target_pairs={{0,128},{1,129},{2,130},{3,131},{4,132},{5,133},{6,134},{7,135},{8... | collective-permute-start | bytes 860168 | tf_op jit(solution)/shard_map/ppermute | solution.py:40
  78.1 15.3 %collective-permute-start.21 = (bf16[40,896]{1,0:T(8,128)(2,1)S(1)}, bf16[40,896]{1,0:T(8,128)(2,1)S(1)}, u32[]{:S(2)}, u32[]{:S(2)}) collective-permute-start(bf16[40,896]{1,0:T(8,128)(2,1)S(1)} %get-tuple-element.66), channel_id=1, source_target_pairs={{0,0},{1,1},{2,2},{3,3},{4,4},{5,5},{6,6},{7,7},{8,8},{9,9},{10,10... | collective-permute-start | bytes 215048 | tf_op jit(solution)/shard_map/ppermute | solution.py:40
  84.7 8.6 %collective-permute-start.22 = (bf16[40,896]{1,0:T(8,128)(2,1)S(1)}, bf16[40,896]{1,0:T(8,128)(2,1)S(1)}, u32[]{:S(2)}, u32[]{:S(2)}) collective-permute-start(bf16[40,896]{1,0:T(8,128)(2,1)S(1)} %get-tuple-element.67), channel_id=1, source_target_pairs={{0,28},{1,29},{2,30},{3,31},{4,0},{5,1},{6,2},{7,3},{8,4},{9,5},{1... | collective-permute-start | bytes 215048 | tf_op jit(solution)/shard_map/ppermute | solution.py:40
  86.5 10.1 %collective-permute-start.23 = (bf16[40,896]{1,0:T(8,128)(2,1)S(1)}, bf16[40,896]{1,0:T(8,128)(2,1)S(1)}, u32[]{:S(2)}, u32[]{:S(2)}) collective-permute-start(bf16[40,896]{1,0:T(8,128)(2,1)S(1)} %get-tuple-element.68), channel_id=1, source_target_pairs={{0,8},{1,9},{2,10},{3,11},{4,12},{5,13},{6,14},{7,15},{8,16},{9,17... | collective-permute-start | bytes 215048 | tf_op jit(solution)/shard_map/ppermute | solution.py:40
  89.8 9.9 %collective-permute-start.24 = (bf16[40,896]{1,0:T(8,128)(2,1)S(1)}, bf16[40,896]{1,0:T(8,128)(2,1)S(1)}, u32[]{:S(2)}, u32[]{:S(2)}) collective-permute-start(bf16[40,896]{1,0:T(8,128)(2,1)S(1)} %get-tuple-element.69), channel_id=1, source_target_pairs={{0,20},{1,21},{2,22},{3,23},{4,24},{5,25},{6,26},{7,27},{8,28},{9,... | collective-permute-start | bytes 215048 | tf_op jit(solution)/shard_map/ppermute | solution.py:40
  99.9 1.4 %collective-permute-start.25 = (bf16[8,7168]{1,0:T(8,128)(2,1)S(1)}, bf16[8,7168]{1,0:T(8,128)(2,1)S(1)}, u32[]{:S(2)}, u32[]{:S(2)}) collective-permute-start(bf16[8,7168]{1,0:T(8,128)(2,1)S(1)} %shard_map.119), channel_id=1, source_target_pairs={{0,64},{1,65},{2,66},{3,67},{4,68},{5,69},{6,70},{7,71},{8,72},{9,... | collective-permute-start | bytes 344072 | tf_op jit(solution)/shard_map/ppermute | solution.py:40
  101.4 4.7 %collective-permute-start.26 = (bf16[8,7168]{1,0:T(8,128)(2,1)S(1)}, bf16[8,7168]{1,0:T(8,128)(2,1)S(1)}, u32[]{:S(2)}, u32[]{:S(2)}) collective-permute-start(bf16[8,7168]{1,0:T(8,128)(2,1)S(1)} %add_convert_fusion.3), channel_id=1, source_target_pairs={{0,128},{1,129},{2,130},{3,131},{4,132},{5,133},{6,134},{7,135},{8... | collective-permute-start | bytes 344072 | tf_op jit(solution)/shard_map/ppermute | solution.py:40

commit v4 on v3

--- a/solution.py
+++ b/solution.py
@@ -44,7 +44,7 @@
     return send(value, lambda xl, c, xh, z, y: (xl, 1 - c, xh, z, y))
 
 
-STEPS = ((0, 1, -2, 3), (-1, 2, -3, 4))
+STEPS = ((3, -2, 1, 0), (4, -3, 2, -1))
 
 
 def spread(value, k, sign):
@@ -68,7 +68,16 @@
     return pltpu.CompilerParams(vmem_limit_bytes=mib * 1024 * 1024)
 
 
-def pack_kernel(at_ref, *refs):
+def targets():
+    sec, dev = lax.axis_index("sec"), lax.axis_index("dev")
+    xl, core = sec // 2, sec % 2
+    xh, z = dev // 32, (dev // 4) % 8
+    half = jnp.where(xl == core, xh, 1 - xh) * 8
+    steps = [jnp.where(core == 0, STEPS[0][k], STEPS[1][k]) for k in range(4)]
+    return [half + (z + step + 8) % 8 for step in steps]
+
+
+def pack_kernel(*refs):
     sources, (o0, o1, o2, o3, table_ref) = refs[:4], refs[4:9]
     scratch, sems = refs[9:13], refs[13]
     copies = [
@@ -82,8 +91,8 @@
     lane = lax.broadcasted_iota(jnp.int32, (ROWS, 256), 1)
     target, slot, piece = lane // (CAP * PIECES), (lane // PIECES) % CAP, lane % PIECES
     wanted = jnp.full((ROWS, 256), -1, jnp.int32)
-    for k in range(4):
-        wanted = jnp.where(target == k, at_ref[k], wanted)
+    for k, expert in enumerate(targets()):
+        wanted = jnp.where(target == k, expert, wanted)
     named = jnp.zeros((ROWS, 256), jnp.float32)
     weight = jnp.zeros((ROWS, 256), jnp.float32)
     ids, route = ids_ref[...], route_ref[...]
@@ -113,16 +122,16 @@
         ref[...] = out[k * CAP * PIECES : (k + 1) * CAP * PIECES].astype(jnp.bfloat16)
 
 
-def pack(at, stream, gain, ids, route):
+def pack(stream, gain, ids, route):
     return pl.pallas_call(
         pack_kernel,
         out_shape=(PACKED,) * 4 + (jax.ShapeDtypeStruct((ROWS, 256), jnp.float32),),
-        in_specs=[pl.BlockSpec(memory_space=pltpu.SMEM)] + [pl.BlockSpec(memory_space=pl.ANY)] * 4,
+        in_specs=[pl.BlockSpec(memory_space=pl.ANY)] * 4,
         out_specs=(VMEM,) * 5,
         scratch_shapes=[pltpu.VMEM(v.shape, v.dtype) for v in (stream, gain, ids, route)]
         + [pltpu.SemaphoreType.DMA((4,))],
         compiler_params=limit(60),
-    )(at, stream, gain, ids, route)
+    )(stream, gain, ids, route)
 
 
 def join_kernel(a, b, c, d, out):
@@ -136,9 +145,9 @@
     )(*parts)
 
 
-def split_kernel(b0, b1, b2, b3, b4, o0, o1, o2, o3):
-    total = b0[...].astype(jnp.float32)
-    for ref in (b1, b2, b3, b4):
+def split_kernel(b0, b1, b2, o0, o1, o2, o3):
+    total = b0[...]
+    for ref in (b1, b2):
         total = total + ref[...].astype(jnp.float32)
     for k, ref in enumerate((o0, o1, o2, o3)):
         ref[...] = total[k * CAP * PIECES : (k + 1) * CAP * PIECES].astype(jnp.bfloat16)
@@ -148,7 +157,7 @@
     return pl.pallas_call(
         split_kernel,
         out_shape=(PACKED,) * 4,
-        in_specs=[VMEM] * 5,
+        in_specs=[VMEM] * 3,
         out_specs=(VMEM,) * 4,
         compiler_params=limit(8),
     )(*blocks)
@@ -187,9 +196,9 @@
 
 def expert_kernel(count, rows, *refs):
     blocks = refs[:count]
-    wide = refs[count : count + 3]
-    down = refs[count + 3]
-    outs = refs[count + 4 : -1]
+    wide = refs[count : count + 2]
+    down = refs[count + 2]
+    outs = refs[count + 3 : -1]
     work = refs[-1]
     size = 4 * CAP * PIECES
     lanes = work.shape[0]
@@ -228,7 +237,7 @@
     return pl.pallas_call(
         functools.partial(expert_kernel, count, rows),
         out_shape=(BLOCK,) * count,
-        in_specs=[VMEM] * (count + 4),
+        in_specs=[VMEM] * (count + 3),
         out_specs=(VMEM,) * count,
         scratch_shapes=[pltpu.VMEM((PIECE // 128, rows * PIECES, 128), jnp.float32)],
         cost_estimate=pl.CostEstimate(
@@ -323,23 +332,18 @@
     w_up,
     w_down,
 ):
-    sec = lax.axis_index("sec")
-    dev = lax.axis_index("dev")
-    xl, core = sec // 2, sec % 2
-    xh, z = dev // 32, (dev // 4) % 8
-
-    half = jnp.where(xl == core, xh, 1 - xh) * 8
-    at = [half + (z + jnp.where(core == 0, STEPS[0][k], STEPS[1][k])) % 8 for k in range(4)]
-    at = jnp.stack(at).astype(jnp.int32)
-    *packed, table = pack(at, stream, norm_gain[None, :], expert_ids, route_weights)
-    gate_own, up_own, down_own = w_gate[0], w_up[0], w_down[0]
-    gate_other = swap_core(gate_own)
-    packed[1], up_own, gate_other = lax.optimization_barrier((packed[1], up_own, gate_other))
+    *packed, table = pack(stream, norm_gain[None, :], expert_ids, route_weights)
+    down_own = w_down[0]
+    down_other = swap_core(down_own)
     arrived = [spread(packed[k], k, 1) for k in range(4)]
 
-    up_other = swap_core(up_own)
-    wide_own = jnp.concatenate([gate_own, up_own], axis=1)
+    wide_own = jnp.concatenate([w_gate[0], w_up[0]], axis=1)
     mine = join(arrived)
+    mine, down_own, down_other, wide_own = lax.optimization_barrier(
+        (mine, down_own, down_other, wide_own)
+    )
+    wide_other = swap_core(wide_own)
+    down = jnp.concatenate([down_own, down_other], axis=0)
 
     def over(value):
         return send(value, lambda xl, c, xh, z, y: (1 - xl, c, xh, z, y))
@@ -347,17 +351,12 @@
     def along(value, dy):
         return send(value, lambda xl, c, xh, z, y: (xl, c, xh, z, y + dy))
 
-    mine, down_own, up_other, wide_own = lax.optimization_barrier(
-        (mine, down_own, up_other, wide_own)
-    )
-    down_other = swap_core(down_own)
     x_in = over(mine)
     up_in = along(mine, 1)
     dn_in = along(mine, -1)
     y2_in = along(mine, 2)
-    x_in, y2_in, down_other = lax.optimization_barrier((x_in, y2_in, down_other))
-    down = jnp.concatenate([down_own, down_other], axis=0)
-    weights = (wide_own, gate_other, up_other, down)
+    x_in, y2_in, wide_other, down = lax.optimization_barrier((x_in, y2_in, wide_other, down))
+    weights = (wide_own, wide_other, down)
     x_up_in = along(x_in, 1)
     x_dn_in = along(x_in, -1)
     x_y2_in = over(y2_in)
@@ -371,16 +370,17 @@
     x_y2_back = over(x_y2_out)
 
     def add(*values):
-        return sum(v.astype(jnp.float32) for v in values).astype(jnp.bfloat16)
-
-    x_sum = add(x_out, x_up_back, x_dn_back)
-    y2_sum = add(y2_out, x_y2_back)
-    x_sum, y2_sum, queries = lax.optimization_barrier((x_sum, y2_sum, queries))
+        return sum(v.astype(jnp.float32) for v in values)
+
+    near = add(own, up_back, dn_back)
+    x_sum = add(x_out, x_up_back, x_dn_back).astype(jnp.bfloat16)
+    y2_sum = add(y2_out, x_y2_back).astype(jnp.bfloat16)
+    near, x_sum, y2_sum, queries = lax.optimization_barrier((near, x_sum, y2_sum, queries))
     x_back = over(x_sum)
     y2_back = along(y2_sum, 2)
     context = attend(queries, latent_cache, cache_lengths)
-    up_back, context = lax.optimization_barrier((up_back, context))
-    back = split((own, up_back, dn_back, y2_back, x_back))
+    near, context = lax.optimization_barrier((near, context))
+    back = split((near, y2_back, x_back))
     returned = [spread(back[k], k, -1) for k in range(4)]
     part = weigh(table, returned)
     pair = part.astype(jnp.float32) + swap_core(part).astype(jnp.float32)

time: 107 us -> 98.1 us (0.917)
  waiting for transfers between devices: 39.5 us -> 26.4 us
  starting transfers between devices: 48 us -> 53.3 us
    ppermute x27 -> x26, waiting for transfers between devices: 39.5 us -> 26.4 us  [send(): return lax.ppermute(value, ('sec', 'dev'), pairs(move))]
    ppermute x27 -> x26, starting transfers between devices: 48 us -> 53.3 us  [send(): return lax.ppermute(value, ('sec', 'dev'), pairs(move))]
    concatenate x1 -> x2, other arithmetic: 2.45 us -> 2.82 us  [the longest x1 2.59 us: local(): wide_own = jnp.concatenate([w_gate[0], w_up[0]], axis=1)]
  transfers between devices with their start and end apart: 27 -> 26, of which waited for: 17 -> 11; matrix products, arithmetic and copies ran while one was open for 3% -> 3% of each run, Pallas kernels for 10% -> 13%
where the time goes in v4:
time: 98.1 us; the launch traced here: 97.9 us
  starting transfers between devices  53.3 us (54%)
  waiting for transfers between devices  26.4 us (27%)
  Pallas kernels  12.9 us (13%)
  other arithmetic  3.82 us (4%)
  between operations  1.5 us (2%)
    ppermute x26, starting transfers between devices, send(): return lax.ppermute(value, ('sec', 'dev'), pairs(move))  53.3 us
    ppermute x26, waiting for transfers between devices, send(): return lax.ppermute(value, ('sec', 'dev'), pairs(move))  26.4 us
    pallas_call x1, Pallas kernels, attend(): pl.pallas_call(attend_kernel, out_shape=jax.ShapeDtypeStruct((1, heads, L...  5.52 us
    pallas_call x2, Pallas kernels, experts(): pl.pallas_call(functools.partial(expert_kernel, count, rows), out_shape=(...  4.9 us
    concatenate x1, other arithmetic, local(): wide_own = jnp.concatenate([w_gate[0], w_up[0]], axis=1)  2.59 us
    pallas_call x1, Pallas kernels, pack(): pl.pallas_call(pack_kernel, out_shape=(PACKED,) * 4 + (jax.ShapeDtypeStru...  2.11 us
  transfers between devices with their start and end apart: 26, of which 11 were waited for; matrix products, arithmetic and copies ran while one was open for 3% of the time, Pallas kernels for 13%

profile of v4, /device:TPU:1, one launch (start us, length us, event | category | flops | bytes accessed | tf_op | source)
XLA Modules:
  0.0 97.9 jit_solution(4006637899500314157)
XLA Ops:
  0.6 3.3 %collective-permute-start.4 = (bf16[128,7168]{1,0:T(8,128)(2,1)}, bf16[128,7168]{1,0:T(8,128)(2,1)S(1)}, u32[]{:S(2)}, u32[]{:S(2)}) collective-permute-start(bf16[128,7168]{1,0:T(8,128)(2,1)} %bitcast.9), channel_id=1, source_target_pairs={{0,64},{1,65},{2,66},{3,67},{4,68},{5,69},{6,70},{7,71},{8,72},{9,... | collective-permute-start | bytes 5505032 | tf_op jit(solution)/shard_map/ppermute | solution.py:40
  4.0 2.1 %shard_map.113 = (bf16[40,896]{1,0:T(8,128)(2,1)}, bf16[40,896]{1,0:T(8,128)(2,1)}, bf16[40,896]{1,0:T(8,128)(2,1)}, bf16[40,896]{1,0:T(8,128)(2,1)}, f32[8,256]{1,0:T(8,128)}) custom-call(bf16[8,7168]{1,0:T(8,128)(2,1)} %refs_0_.1, f32[1,7168]{1,0:T(1,128)} %bitcast.12, s32[8,8]{1,0:T(8,128)} %refs_2_.1, f32[8,8]{1,0:T(8,128)} %refs_3_.1), custom_call_target="tpu_custom_call" | custom-call | tf_op jit(solution)/shard_map/pallas_call | solution.py:126
  6.1 7.3 %collective-permute-start = (bf16[40,896]{1,0:T(8,128)(2,1)}, bf16[40,896]{1,0:T(8,128)(2,1)S(1)}, u32[]{:S(2)}, u32[]{:S(2)}) collective-permute-start(bf16[40,896]{1,0:T(8,128)(2,1)} %get-tuple-element.35), channel_id=1, source_target_pairs={{0,12},{1,13},{2,14},{3,15},{4,16},{5,17},{6,18},{7,19},{8,20},{9,... | collective-permute-start | bytes 215048 | tf_op jit(solution)/shard_map/ppermute | solution.py:40
  13.4 4.8 %collective-permute-start.2 = (bf16[40,896]{1,0:T(8,128)(2,1)}, bf16[40,896]{1,0:T(8,128)(2,1)S(1)}, u32[]{:S(2)}, u32[]{:S(2)}) collective-permute-start(bf16[40,896]{1,0:T(8,128)(2,1)} %get-tuple-element.37), channel_id=1, source_target_pairs={{0,4},{1,5},{2,6},{3,7},{4,8},{5,9},{6,10},{7,11},{8,12},{9,13},{1... | collective-permute-start | bytes 215048 | tf_op jit(solution)/shard_map/ppermute | solution.py:40
  18.2 2.2 %collective-permute-start.3 = (bf16[40,896]{1,0:T(8,128)(2,1)}, bf16[40,896]{1,0:T(8,128)(2,1)S(1)}, u32[]{:S(2)}, u32[]{:S(2)}) collective-permute-start(bf16[40,896]{1,0:T(8,128)(2,1)} %get-tuple-element.38), channel_id=1, source_target_pairs={{0,0},{1,1},{2,2},{3,3},{4,4},{5,5},{6,6},{7,7},{8,8},{9,9},{10,10... | collective-permute-start | bytes 215048 | tf_op jit(solution)/shard_map/ppermute | solution.py:40
  20.4 2.6 %pad_maximum_fusion.refs_5_.refs_3_ = bf16[7168,256]{1,0:T(8,128)(2,1)S(1)} fusion(bf16[7168,128]{1,0:T(8,128)(2,1)} %bitcast.7, bf16[7168,128]{1,0:T(8,128)(2,1)} %bitcast.8), kind=kLoop, calls=%fused_computation | loop fusion | flops 7340032 | bytes 7340032 | tf_op jit(solution)/shard_map/concatenate | solution.py:340
  23.0 2.2 %collective-permute-done.3.d = bf16[40,896]{1,0:T(8,128)(2,1)S(1)} collective-permute-done((bf16[40,896]{1,0:T(8,128)(2,1)}, bf16[40,896]{1,0:T(8,128)(2,1)S(1)}, u32[]{:S(2)}, u32[]{:S(2)}) %collective-permute-start.3) | collective-permute-done | bytes 71712 | tf_op jit(solution)/shard_map/ppermute | solution.py:40
  25.3 0.1 collective-permute-start.7
  25.4 0.1 collective-permute-start.5
  25.5 3.0 %collective-permute-start.6 = (bf16[160,896]{1,0:T(8,128)(2,1)S(1)}, bf16[160,896]{1,0:T(8,128)(2,1)S(1)}, u32[]{:S(2)}, u32[]{:S(2)}) collective-permute-start(bf16[160,896]{1,0:T(8,128)(2,1)S(1)} %shard_map.114.refs_0_), channel_id=1, source_target_pairs={{0,2},{1,3},{2,0},{3,1},{4,6},{5,7},{6,4},{7,5},{8,10},{9,11},{10,... | collective-permute-start | bytes 860168 | tf_op jit(solution)/shard_map/ppermute | solution.py:40
  28.5 0.4 collective-permute-start.9
  28.9 2.3 %collective-permute-start.10 = (bf16[160,896]{1,0:T(8,128)(2,1)S(1)}, bf16[160,896]{1,0:T(8,128)(2,1)S(1)}, u32[]{:S(2)}, u32[]{:S(2)}) collective-permute-start(bf16[160,896]{1,0:T(8,128)(2,1)S(1)} %shard_map.114.refs_0_), channel_id=1, source_target_pairs={{0,3},{1,0},{2,1},{3,2},{4,7},{5,4},{6,5},{7,6},{8,11},{9,8},{10,9... | collective-permute-start | bytes 860168 | tf_op jit(solution)/shard_map/ppermute | solution.py:40
  31.2 0.2 pad_maximum_fusion.1.refs_7_.refs_5_
  31.4 2.1 %collective-permute-done.5.refs_1_ = bf16[160,896]{1,0:T(8,128)(2,1)S(1)} collective-permute-done((bf16[160,896]{1,0:T(8,128)(2,1)S(1)}, bf16[160,896]{1,0:T(8,128)(2,1)S(1)}, u32[]{:S(2)}, u32[]{:S(2)}) %collective-permute-start.5) | collective-permute-done | bytes 286752 | tf_op jit(solution)/shard_map/ppermute | solution.py:40
  33.5 1.8 %collective-permute-done.6.refs_2_ = bf16[160,896]{1,0:T(8,128)(2,1)S(1)} collective-permute-done((bf16[160,896]{1,0:T(8,128)(2,1)S(1)}, bf16[160,896]{1,0:T(8,128)(2,1)S(1)}, u32[]{:S(2)}, u32[]{:S(2)}) %collective-permute-start.6) | collective-permute-done | bytes 286752 | tf_op jit(solution)/shard_map/ppermute | solution.py:40
  35.2 1.3 %collective-permute-start.8 = (bf16[160,896]{1,0:T(8,128)(2,1)S(1)}, bf16[160,896]{1,0:T(8,128)(2,1)S(1)}, u32[]{:S(2)}, u32[]{:S(2)}) collective-permute-start(bf16[160,896]{1,0:T(8,128)(2,1)S(1)} %collective-permute-done.5.refs_1_), channel_id=1, source_target_pairs={{0,1},{1,2},{2,3},{3,0},{4,5},{5,6},{6,7},{7,4},{8,9},{9,10},{10,1... | collective-permute-start | bytes 860168 | tf_op jit(solution)/shard_map/ppermute | solution.py:40
  36.5 1.4 %collective-permute-start.13 = (bf16[160,896]{1,0:T(8,128)(2,1)S(1)}, bf16[160,896]{1,0:T(8,128)(2,1)S(1)}, u32[]{:S(2)}, u32[]{:S(2)}) collective-permute-start(bf16[160,896]{1,0:T(8,128)(2,1)S(1)} %collective-permute-done.5.refs_1_), channel_id=1, source_target_pairs={{0,3},{1,0},{2,1},{3,2},{4,7},{5,4},{6,5},{7,6},{8,11},{9,8},{10,9... | collective-permute-start | bytes 860168 | tf_op jit(solution)/shard_map/ppermute | solution.py:40
  38.0 0.9 collective-permute-start.14
  38.9 3.1 %collective-permute-done.9.refs_3_ = bf16[160,896]{1,0:T(8,128)(2,1)S(1)} collective-permute-done((bf16[160,896]{1,0:T(8,128)(2,1)S(1)}, bf16[160,896]{1,0:T(8,128)(2,1)S(1)}, u32[]{:S(2)}, u32[]{:S(2)}) %collective-permute-start.9) | collective-permute-done | bytes 286752 | tf_op jit(solution)/shard_map/ppermute | solution.py:40
  42.0 2.6 %shard_map.115 = (bf16[160,896]{1,0:T(8,128)(2,1)S(1)}, bf16[160,896]{1,0:T(8,128)(2,1)S(1)}, bf16[160,896]{1,0:T(8,128)(2,1)S(1)}, bf16[160,896]{1,0:T(8,128)(2,1)S(1)}, bf16[160,896]{1,0:T(8,128)(2,1)S(1)}) custom-call(bf16[160,896]{1,0:T(8,128)(2,1)S(1)} %shard_map.114.refs_0_, bf16[160,896]{1,0:T(8,128)(2,1)S(1)} %collective-permute-done.5.refs_1_, ...), custom_call_target="tpu_custom_call" | custom-call | flops 1233125376 | bytes 14221312 | tf_op jit(solution)/shard_map/pallas_call | solution.py:237
  44.6 1.5 %collective-permute-start.12 = (bf16[160,896]{1,0:T(8,128)(2,1)S(1)}, bf16[160,896]{1,0:T(8,128)(2,1)S(1)}, u32[]{:S(2)}, u32[]{:S(2)}) collective-permute-start(bf16[160,896]{1,0:T(8,128)(2,1)S(1)} %get-tuple-element.50), channel_id=1, source_target_pairs={{0,1},{1,2},{2,3},{3,0},{4,5},{5,6},{6,7},{7,4},{8,9},{9,10},{10,1... | collective-permute-start | bytes 860168 | tf_op jit(solution)/shard_map/ppermute | solution.py:40
  46.1 1.5 %collective-permute-start.11 = (bf16[160,896]{1,0:T(8,128)(2,1)S(1)}, bf16[160,896]{1,0:T(8,128)(2,1)S(1)}, u32[]{:S(2)}, u32[]{:S(2)}) collective-permute-start(bf16[160,896]{1,0:T(8,128)(2,1)S(1)} %get-tuple-element.49), channel_id=1, source_target_pairs={{0,3},{1,0},{2,1},{3,2},{4,7},{5,4},{6,5},{7,6},{8,11},{9,8},{10,9... | collective-permute-start | bytes 860168 | tf_op jit(solution)/shard_map/ppermute | solution.py:40
  47.7 0.4 collective-permute-done.8.refs_0_
  48.1 2.3 %shard_map.116 = (bf16[160,896]{1,0:T(8,128)(2,1)S(1)}, bf16[160,896]{1,0:T(8,128)(2,1)S(1)}, bf16[160,896]{1,0:T(8,128)(2,1)S(1)}) custom-call(bf16[160,896]{1,0:T(8,128)(2,1)S(1)} %collective-permute-done.8.refs_0_, bf16[160,896]{1,0:T(8,128)(2,1)S(1)} %collective-permute-done.13.refs_1_, bf16[160,896]{1,0:T(8,128)(2,1)S(1)} %collective-permute-done.14.refs_2_, ...), custom_call_target="tpu_custom_call" | custom-call | flops 704643072 | bytes 12845056 | tf_op jit(solution)/shard_map/pallas_call | solution.py:237
  50.4 1.4 %collective-permute-start.17 = (bf16[160,896]{1,0:T(8,128)(2,1)S(1)}, bf16[160,896]{1,0:T(8,128)(2,1)S(1)}, u32[]{:S(2)}, u32[]{:S(2)}) collective-permute-start(bf16[160,896]{1,0:T(8,128)(2,1)S(1)} %get-tuple-element.56), channel_id=1, source_target_pairs={{0,128},{1,129},{2,130},{3,131},{4,132},{5,133},{6,134},{7,135},{8... | collective-permute-start | bytes 860168 | tf_op jit(solution)/shard_map/ppermute | solution.py:40
  51.9 1.2 %collective-permute-start.16 = (bf16[160,896]{1,0:T(8,128)(2,1)S(1)}, bf16[160,896]{1,0:T(8,128)(2,1)S(1)}, u32[]{:S(2)}, u32[]{:S(2)}) collective-permute-start(bf16[160,896]{1,0:T(8,128)(2,1)S(1)} %get-tuple-element.54), channel_id=1, source_target_pairs={{0,1},{1,2},{2,3},{3,0},{4,5},{5,6},{6,7},{7,4},{8,9},{9,10},{10,1... | collective-permute-start | bytes 860168 | tf_op jit(solution)/shard_map/ppermute | solution.py:40
  53.0 1.6 %collective-permute-start.15 = (bf16[160,896]{1,0:T(8,128)(2,1)S(1)}, bf16[160,896]{1,0:T(8,128)(2,1)S(1)}, u32[]{:S(2)}, u32[]{:S(2)}) collective-permute-start(bf16[160,896]{1,0:T(8,128)(2,1)S(1)} %get-tuple-element.53), channel_id=1, source_target_pairs={{0,3},{1,0},{2,1},{3,2},{4,7},{5,4},{6,5},{7,6},{8,11},{9,8},{10,9... | collective-permute-start | bytes 860168 | tf_op jit(solution)/shard_map/ppermute | solution.py:40
  54.6 0.1 convert_add_fusion.b0
  54.7 2.5 %collective-permute-done.17 = bf16[160,896]{1,0:T(8,128)(2,1)S(1)} collective-permute-done((bf16[160,896]{1,0:T(8,128)(2,1)S(1)}, bf16[160,896]{1,0:T(8,128)(2,1)S(1)}, u32[]{:S(2)}, u32[]{:S(2)}) %collective-permute-start.17) | collective-permute-done | bytes 286752 | tf_op jit(solution)/shard_map/ppermute | solution.py:40
  57.2 0.1 add_convert_fusion
  57.3 2.0 %collective-permute-done.16 = bf16[160,896]{1,0:T(8,128)(2,1)S(1)} collective-permute-done((bf16[160,896]{1,0:T(8,128)(2,1)S(1)}, bf16[160,896]{1,0:T(8,128)(2,1)S(1)}, u32[]{:S(2)}, u32[]{:S(2)}) %collective-permute-start.16) | collective-permute-done | bytes 286752 | tf_op jit(solution)/shard_map/ppermute | solution.py:40
  59.2 0.0 collective-permute-done.15
  59.2 0.1 add_convert_fusion.1
  59.4 3.9 %collective-permute-start.18 = (bf16[160,896]{1,0:T(8,128)(2,1)S(1)}, bf16[160,896]{1,0:T(8,128)(2,1)S(1)}, u32[]{:S(2)}, u32[]{:S(2)}) collective-permute-start(bf16[160,896]{1,0:T(8,128)(2,1)S(1)} %add_convert_fusion), channel_id=1, source_target_pairs={{0,2},{1,3},{2,0},{3,1},{4,6},{5,7},{6,4},{7,5},{8,10},{9,11},{10,... | collective-permute-start | bytes 860168 | tf_op jit(solution)/shard_map/ppermute | solution.py:40
  63.3 0.9 collective-permute-start.19
  64.8 5.5 %shard_map.117 = bf16[1,128,512]{2,1,0:T(8,128)(2,1)} custom-call(s32[1]{0:T(128)S(6)} %copy.12.length_ref, bf16[1,576,128]{2,1,0:T(8,128)(2,1)} %bitcast.11, bf16[1,576,4096]{2,1,0:T(8,128)(2,1)} %bitcast.6), custom_call_target="tpu_custom_call" | custom-call | flops 1140850688 | bytes 4718592 | tf_op jit(solution)/shard_map/pallas_call | solution.py:300
  70.4 0.1 shard_map.118
  70.5 6.0 %collective-permute-start.20 = (bf16[40,896]{1,0:T(8,128)(2,1)S(1)}, bf16[40,896]{1,0:T(8,128)(2,1)S(1)}, u32[]{:S(2)}, u32[]{:S(2)}) collective-permute-start(bf16[40,896]{1,0:T(8,128)(2,1)S(1)} %get-tuple-element.64), channel_id=1, source_target_pairs={{0,20},{1,21},{2,22},{3,23},{4,24},{5,25},{6,26},{7,27},{8,28},{9,... | collective-permute-start | bytes 215048 | tf_op jit(solution)/shard_map/ppermute | solution.py:40
  76.4 5.5 %collective-permute-start.22 = (bf16[40,896]{1,0:T(8,128)(2,1)S(1)}, bf16[40,896]{1,0:T(8,128)(2,1)S(1)}, u32[]{:S(2)}, u32[]{:S(2)}) collective-permute-start(bf16[40,896]{1,0:T(8,128)(2,1)S(1)} %get-tuple-element.66), channel_id=1, source_target_pairs={{0,28},{1,29},{2,30},{3,31},{4,0},{5,1},{6,2},{7,3},{8,4},{9,5},{1... | collective-permute-start | bytes 215048 | tf_op jit(solution)/shard_map/ppermute | solution.py:40
  81.9 2.5 %collective-permute-start.23 = (bf16[40,896]{1,0:T(8,128)(2,1)S(1)}, bf16[40,896]{1,0:T(8,128)(2,1)S(1)}, u32[]{:S(2)}, u32[]{:S(2)}) collective-permute-start(bf16[40,896]{1,0:T(8,128)(2,1)S(1)} %get-tuple-element.67), channel_id=1, source_target_pairs={{0,0},{1,1},{2,2},{3,3},{4,4},{5,5},{6,6},{7,7},{8,8},{9,9},{10,10... | collective-permute-start | bytes 215048 | tf_op jit(solution)/shard_map/ppermute | solution.py:40
  84.4 1.8 %collective-permute-done.21.b = bf16[40,896]{1,0:T(8,128)(2,1)S(1)} collective-permute-done((bf16[40,896]{1,0:T(8,128)(2,1)S(1)}, bf16[40,896]{1,0:T(8,128)(2,1)S(1)}, u32[]{:S(2)}, u32[]{:S(2)}) %collective-permute-start.21) | collective-permute-done | bytes 71712 | tf_op jit(solution)/shard_map/ppermute | solution.py:40
  86.2 4.6 %collective-permute-done.23.d = bf16[40,896]{1,0:T(8,128)(2,1)S(1)} collective-permute-done((bf16[40,896]{1,0:T(8,128)(2,1)S(1)}, bf16[40,896]{1,0:T(8,128)(2,1)S(1)}, u32[]{:S(2)}, u32[]{:S(2)}) %collective-permute-start.23) | collective-permute-done | bytes 71712 | tf_op jit(solution)/shard_map/ppermute | solution.py:40
  90.9 0.3 shard_map.119
  91.1 0.1 collective-permute-start.24
  91.2 1.3 %collective-permute-done.24 = bf16[8,7168]{1,0:T(8,128)(2,1)S(1)} collective-permute-done((bf16[8,7168]{1,0:T(8,128)(2,1)S(1)}, bf16[8,7168]{1,0:T(8,128)(2,1)S(1)}, u32[]{:S(2)}, u32[]{:S(2)}) %collective-permute-start.24) | collective-permute-done | bytes 114720 | tf_op jit(solution)/shard_map/ppermute | solution.py:40
  92.6 0.1 collective-permute-start.25
  92.7 4.6 %collective-permute-done.25 = bf16[8,7168]{1,0:T(8,128)(2,1)S(1)} collective-permute-done((bf16[8,7168]{1,0:T(8,128)(2,1)S(1)}, bf16[8,7168]{1,0:T(8,128)(2,1)S(1)}, u32[]{:S(2)}, u32[]{:S(2)}) %collective-permute-start.25) | collective-permute-done | bytes 114720 | tf_op jit(solution)/shard_map/ppermute | solution.py:40
  97.2 0.7 add_convert_fusion.2
  (24 shorter events, 0.1 us)
Async XLA Ops:
  0.6 24.6 %collective-permute-start.4 = (bf16[128,7168]{1,0:T(8,128)(2,1)}, bf16[128,7168]{1,0:T(8,128)(2,1)S(1)}, u32[]{:S(2)}, u32[]{:S(2)}) collective-permute-start(bf16[128,7168]{1,0:T(8,128)(2,1)} %bitcast.9), channel_id=1, source_target_pairs={{0,64},{1,65},{2,66},{3,67},{4,68},{5,69},{6,70},{7,71},{8,72},{9,... | collective-permute-start | bytes 5505032 | tf_op jit(solution)/shard_map/ppermute | solution.py:40
  6.1 16.9 %collective-permute-start = (bf16[40,896]{1,0:T(8,128)(2,1)}, bf16[40,896]{1,0:T(8,128)(2,1)S(1)}, u32[]{:S(2)}, u32[]{:S(2)}) collective-permute-start(bf16[40,896]{1,0:T(8,128)(2,1)} %get-tuple-element.35), channel_id=1, source_target_pairs={{0,12},{1,13},{2,14},{3,15},{4,16},{5,17},{6,18},{7,19},{8,20},{9,... | collective-permute-start | bytes 215048 | tf_op jit(solution)/shard_map/ppermute | solution.py:40
  13.4 9.6 %collective-permute-start.1 = (bf16[40,896]{1,0:T(8,128)(2,1)}, bf16[40,896]{1,0:T(8,128)(2,1)S(1)}, u32[]{:S(2)}, u32[]{:S(2)}) collective-permute-start(bf16[40,896]{1,0:T(8,128)(2,1)} %get-tuple-element.36), channel_id=1, source_target_pairs={{0,24},{1,25},{2,26},{3,27},{4,28},{5,29},{6,30},{7,31},{8,0},{9,1... | collective-permute-start | bytes 215048 | tf_op jit(solution)/shard_map/ppermute | solution.py:40
  13.4 9.6 %collective-permute-start.2 = (bf16[40,896]{1,0:T(8,128)(2,1)}, bf16[40,896]{1,0:T(8,128)(2,1)S(1)}, u32[]{:S(2)}, u32[]{:S(2)}) collective-permute-start(bf16[40,896]{1,0:T(8,128)(2,1)} %get-tuple-element.37), channel_id=1, source_target_pairs={{0,4},{1,5},{2,6},{3,7},{4,8},{5,9},{6,10},{7,11},{8,12},{9,13},{1... | collective-permute-start | bytes 215048 | tf_op jit(solution)/shard_map/ppermute | solution.py:40
  18.2 7.1 %collective-permute-start.3 = (bf16[40,896]{1,0:T(8,128)(2,1)}, bf16[40,896]{1,0:T(8,128)(2,1)S(1)}, u32[]{:S(2)}, u32[]{:S(2)}) collective-permute-start(bf16[40,896]{1,0:T(8,128)(2,1)} %get-tuple-element.38), channel_id=1, source_target_pairs={{0,0},{1,1},{2,2},{3,3},{4,4},{5,5},{6,6},{7,7},{8,8},{9,9},{10,10... | collective-permute-start | bytes 215048 | tf_op jit(solution)/shard_map/ppermute | solution.py:40
  20.4 10.8 %copy-start.1 = (bf16[1,128,7168]{2,1,0:T(8,128)(2,1)S(1)}, bf16[1,128,7168]{2,1,0:T(8,128)(2,1)}, u32[]{:S(2)}) copy-start(bf16[1,128,7168]{2,1,0:T(8,128)(2,1)} %param.19) | copy-start | bytes 5505028
  25.3 10.0 %collective-permute-start.7 = (bf16[7168,256]{1,0:T(8,128)(2,1)S(1)}, bf16[7168,256]{1,0:T(8,128)(2,1)S(1)}, u32[]{:S(2)}, u32[]{:S(2)}) collective-permute-start(bf16[7168,256]{1,0:T(8,128)(2,1)S(1)} %pad_maximum_fusion.refs_5_.refs_3_), channel_id=1, source_target_pairs={{0,64},{1,65},{2,66},{3,67},{4,68},{5,69},{6,70},{7,71},{8,72},{9,... | collective-permute-start | bytes 11010056 | tf_op jit(solution)/shard_map/ppermute | solution.py:40
  25.4 8.1 %collective-permute-start.5 = (bf16[160,896]{1,0:T(8,128)(2,1)S(1)}, bf16[160,896]{1,0:T(8,128)(2,1)S(1)}, u32[]{:S(2)}, u32[]{:S(2)}) collective-permute-start(bf16[160,896]{1,0:T(8,128)(2,1)S(1)} %shard_map.114.refs_0_), channel_id=1, source_target_pairs={{0,128},{1,129},{2,130},{3,131},{4,132},{5,133},{6,134},{7,135},{8... | collective-permute-start | bytes 860168 | tf_op jit(solution)/shard_map/ppermute | solution.py:40
  25.5 9.7 %collective-permute-start.6 = (bf16[160,896]{1,0:T(8,128)(2,1)S(1)}, bf16[160,896]{1,0:T(8,128)(2,1)S(1)}, u32[]{:S(2)}, u32[]{:S(2)}) collective-permute-start(bf16[160,896]{1,0:T(8,128)(2,1)S(1)} %shard_map.114.refs_0_), channel_id=1, source_target_pairs={{0,2},{1,3},{2,0},{3,1},{4,6},{5,7},{6,4},{7,5},{8,10},{9,11},{10,... | collective-permute-start | bytes 860168 | tf_op jit(solution)/shard_map/ppermute | solution.py:40
  28.5 13.5 %collective-permute-start.9 = (bf16[160,896]{1,0:T(8,128)(2,1)S(1)}, bf16[160,896]{1,0:T(8,128)(2,1)S(1)}, u32[]{:S(2)}, u32[]{:S(2)}) collective-permute-start(bf16[160,896]{1,0:T(8,128)(2,1)S(1)} %shard_map.114.refs_0_), channel_id=1, source_target_pairs={{0,1},{1,2},{2,3},{3,0},{4,5},{5,6},{6,7},{7,4},{8,9},{9,10},{10,1... | collective-permute-start | bytes 860168 | tf_op jit(solution)/shard_map/ppermute | solution.py:40
  28.9 13.1 %collective-permute-start.10 = (bf16[160,896]{1,0:T(8,128)(2,1)S(1)}, bf16[160,896]{1,0:T(8,128)(2,1)S(1)}, u32[]{:S(2)}, u32[]{:S(2)}) collective-permute-start(bf16[160,896]{1,0:T(8,128)(2,1)S(1)} %shard_map.114.refs_0_), channel_id=1, source_target_pairs={{0,3},{1,0},{2,1},{3,2},{4,7},{5,4},{6,5},{7,6},{8,11},{9,8},{10,9... | collective-permute-start | bytes 860168 | tf_op jit(solution)/shard_map/ppermute | solution.py:40
  35.2 12.9 %collective-permute-start.8 = (bf16[160,896]{1,0:T(8,128)(2,1)S(1)}, bf16[160,896]{1,0:T(8,128)(2,1)S(1)}, u32[]{:S(2)}, u32[]{:S(2)}) collective-permute-start(bf16[160,896]{1,0:T(8,128)(2,1)S(1)} %collective-permute-done.5.refs_1_), channel_id=1, source_target_pairs={{0,1},{1,2},{2,3},{3,0},{4,5},{5,6},{6,7},{7,4},{8,9},{9,10},{10,1... | collective-permute-start | bytes 860168 | tf_op jit(solution)/shard_map/ppermute | solution.py:40
  36.5 11.6 %collective-permute-start.13 = (bf16[160,896]{1,0:T(8,128)(2,1)S(1)}, bf16[160,896]{1,0:T(8,128)(2,1)S(1)}, u32[]{:S(2)}, u32[]{:S(2)}) collective-permute-start(bf16[160,896]{1,0:T(8,128)(2,1)S(1)} %collective-permute-done.5.refs_1_), channel_id=1, source_target_pairs={{0,3},{1,0},{2,1},{3,2},{4,7},{5,4},{6,5},{7,6},{8,11},{9,8},{10,9... | collective-permute-start | bytes 860168 | tf_op jit(solution)/shard_map/ppermute | solution.py:40
  38.0 10.2 %collective-permute-start.14 = (bf16[160,896]{1,0:T(8,128)(2,1)S(1)}, bf16[160,896]{1,0:T(8,128)(2,1)S(1)}, u32[]{:S(2)}, u32[]{:S(2)}) collective-permute-start(bf16[160,896]{1,0:T(8,128)(2,1)S(1)} %collective-permute-done.6.refs_2_), channel_id=1, source_target_pairs={{0,128},{1,129},{2,130},{3,131},{4,132},{5,133},{6,134},{7,135},{8... | collective-permute-start | bytes 860168 | tf_op jit(solution)/shard_map/ppermute | solution.py:40
  44.6 10.0 %collective-permute-start.12 = (bf16[160,896]{1,0:T(8,128)(2,1)S(1)}, bf16[160,896]{1,0:T(8,128)(2,1)S(1)}, u32[]{:S(2)}, u32[]{:S(2)}) collective-permute-start(bf16[160,896]{1,0:T(8,128)(2,1)S(1)} %get-tuple-element.50), channel_id=1, source_target_pairs={{0,1},{1,2},{2,3},{3,0},{4,5},{5,6},{6,7},{7,4},{8,9},{9,10},{10,1... | collective-permute-start | bytes 860168 | tf_op jit(solution)/shard_map/ppermute | solution.py:40
  46.1 8.5 %collective-permute-start.11 = (bf16[160,896]{1,0:T(8,128)(2,1)S(1)}, bf16[160,896]{1,0:T(8,128)(2,1)S(1)}, u32[]{:S(2)}, u32[]{:S(2)}) collective-permute-start(bf16[160,896]{1,0:T(8,128)(2,1)S(1)} %get-tuple-element.49), channel_id=1, source_target_pairs={{0,3},{1,0},{2,1},{3,2},{4,7},{5,4},{6,5},{7,6},{8,11},{9,8},{10,9... | collective-permute-start | bytes 860168 | tf_op jit(solution)/shard_map/ppermute | solution.py:40
  50.4 6.8 %collective-permute-start.17 = (bf16[160,896]{1,0:T(8,128)(2,1)S(1)}, bf16[160,896]{1,0:T(8,128)(2,1)S(1)}, u32[]{:S(2)}, u32[]{:S(2)}) collective-permute-start(bf16[160,896]{1,0:T(8,128)(2,1)S(1)} %get-tuple-element.56), channel_id=1, source_target_pairs={{0,128},{1,129},{2,130},{3,131},{4,132},{5,133},{6,134},{7,135},{8... | collective-permute-start | bytes 860168 | tf_op jit(solution)/shard_map/ppermute | solution.py:40
  51.9 7.4 %collective-permute-start.16 = (bf16[160,896]{1,0:T(8,128)(2,1)S(1)}, bf16[160,896]{1,0:T(8,128)(2,1)S(1)}, u32[]{:S(2)}, u32[]{:S(2)}) collective-permute-start(bf16[160,896]{1,0:T(8,128)(2,1)S(1)} %get-tuple-element.54), channel_id=1, source_target_pairs={{0,1},{1,2},{2,3},{3,0},{4,5},{5,6},{6,7},{7,4},{8,9},{9,10},{10,1... | collective-permute-start | bytes 860168 | tf_op jit(solution)/shard_map/ppermute | solution.py:40
  53.0 6.2 %collective-permute-start.15 = (bf16[160,896]{1,0:T(8,128)(2,1)S(1)}, bf16[160,896]{1,0:T(8,128)(2,1)S(1)}, u32[]{:S(2)}, u32[]{:S(2)}) collective-permute-start(bf16[160,896]{1,0:T(8,128)(2,1)S(1)} %get-tuple-element.53), channel_id=1, source_target_pairs={{0,3},{1,0},{2,1},{3,2},{4,7},{5,4},{6,5},{7,6},{8,11},{9,8},{10,9... | collective-permute-start | bytes 860168 | tf_op jit(solution)/shard_map/ppermute | solution.py:40
  57.2 33.6 %copy-start = (f32[8,256]{1,0:T(8,128)S(1)}, f32[8,256]{1,0:T(8,128)}, u32[]{:S(2)}) copy-start(f32[8,256]{1,0:T(8,128)} %get-tuple-element.60.table_ref) | copy-start | bytes 24580
  59.4 37.9 %copy-start.2 = (bf16[8,7168]{1,0:T(8,128)(2,1)S(1)}, bf16[8,7168]{1,0:T(8,128)(2,1)}, u32[]{:S(2)}) copy-start(bf16[8,7168]{1,0:T(8,128)(2,1)} %refs_0_.1) | copy-start | bytes 344068
  59.4 11.0 %collective-permute-start.18 = (bf16[160,896]{1,0:T(8,128)(2,1)S(1)}, bf16[160,896]{1,0:T(8,128)(2,1)S(1)}, u32[]{:S(2)}, u32[]{:S(2)}) collective-permute-start(bf16[160,896]{1,0:T(8,128)(2,1)S(1)} %add_convert_fusion), channel_id=1, source_target_pairs={{0,2},{1,3},{2,0},{3,1},{4,6},{5,7},{6,4},{7,5},{8,10},{9,11},{10,... | collective-permute-start | bytes 860168 | tf_op jit(solution)/shard_map/ppermute | solution.py:40
  63.3 7.1 %collective-permute-start.19 = (bf16[160,896]{1,0:T(8,128)(2,1)S(1)}, bf16[160,896]{1,0:T(8,128)(2,1)S(1)}, u32[]{:S(2)}, u32[]{:S(2)}) collective-permute-start(bf16[160,896]{1,0:T(8,128)(2,1)S(1)} %add_convert_fusion.1), channel_id=1, source_target_pairs={{0,128},{1,129},{2,130},{3,131},{4,132},{5,133},{6,134},{7,135},{8... | collective-permute-start | bytes 860168 | tf_op jit(solution)/shard_map/ppermute | solution.py:40
  70.5 13.9 %collective-permute-start.20 = (bf16[40,896]{1,0:T(8,128)(2,1)S(1)}, bf16[40,896]{1,0:T(8,128)(2,1)S(1)}, u32[]{:S(2)}, u32[]{:S(2)}) collective-permute-start(bf16[40,896]{1,0:T(8,128)(2,1)S(1)} %get-tuple-element.64), channel_id=1, source_target_pairs={{0,20},{1,21},{2,22},{3,23},{4,24},{5,25},{6,26},{7,27},{8,28},{9,... | collective-permute-start | bytes 215048 | tf_op jit(solution)/shard_map/ppermute | solution.py:40
  76.4 9.8 %collective-permute-start.21 = (bf16[40,896]{1,0:T(8,128)(2,1)S(1)}, bf16[40,896]{1,0:T(8,128)(2,1)S(1)}, u32[]{:S(2)}, u32[]{:S(2)}) collective-permute-start(bf16[40,896]{1,0:T(8,128)(2,1)S(1)} %get-tuple-element.65), channel_id=1, source_target_pairs={{0,8},{1,9},{2,10},{3,11},{4,12},{5,13},{6,14},{7,15},{8,16},{9,17... | collective-permute-start | bytes 215048 | tf_op jit(solution)/shard_map/ppermute | solution.py:40
  76.4 9.8 %collective-permute-start.22 = (bf16[40,896]{1,0:T(8,128)(2,1)S(1)}, bf16[40,896]{1,0:T(8,128)(2,1)S(1)}, u32[]{:S(2)}, u32[]{:S(2)}) collective-permute-start(bf16[40,896]{1,0:T(8,128)(2,1)S(1)} %get-tuple-element.66), channel_id=1, source_target_pairs={{0,28},{1,29},{2,30},{3,31},{4,0},{5,1},{6,2},{7,3},{8,4},{9,5},{1... | collective-permute-start | bytes 215048 | tf_op jit(solution)/shard_map/ppermute | solution.py:40
  81.9 9.0 %collective-permute-start.23 = (bf16[40,896]{1,0:T(8,128)(2,1)S(1)}, bf16[40,896]{1,0:T(8,128)(2,1)S(1)}, u32[]{:S(2)}, u32[]{:S(2)}) collective-permute-start(bf16[40,896]{1,0:T(8,128)(2,1)S(1)} %get-tuple-element.67), channel_id=1, source_target_pairs={{0,0},{1,1},{2,2},{3,3},{4,4},{5,5},{6,6},{7,7},{8,8},{9,9},{10,10... | collective-permute-start | bytes 215048 | tf_op jit(solution)/shard_map/ppermute | solution.py:40
  91.1 1.4 %collective-permute-start.24 = (bf16[8,7168]{1,0:T(8,128)(2,1)S(1)}, bf16[8,7168]{1,0:T(8,128)(2,1)S(1)}, u32[]{:S(2)}, u32[]{:S(2)}) collective-permute-start(bf16[8,7168]{1,0:T(8,128)(2,1)S(1)} %shard_map.119), channel_id=1, source_target_pairs={{0,64},{1,65},{2,66},{3,67},{4,68},{5,69},{6,70},{7,71},{8,72},{9,... | collective-permute-start | bytes 344072 | tf_op jit(solution)/shard_map/ppermute | solution.py:40
  92.6 4.7 %collective-permute-start.25 = (bf16[8,7168]{1,0:T(8,128)(2,1)S(1)}, bf16[8,7168]{1,0:T(8,128)(2,1)S(1)}, u32[]{:S(2)}, u32[]{:S(2)}) collective-permute-start(bf16[8,7168]{1,0:T(8,128)(2,1)S(1)} %add_convert_fusion.3), channel_id=1, source_target_pairs={{0,128},{1,129},{2,130},{3,131},{4,132},{5,133},{6,134},{7,135},{8... | collective-permute-start | bytes 344072 | tf_op jit(solution)/shard_map/ppermute | solution.py:40

commit v5 on v4

--- a/solution.py
+++ b/solution.py
@@ -44,14 +44,15 @@
     return send(value, lambda xl, c, xh, z, y: (xl, 1 - c, xh, z, y))
 
 
-STEPS = ((3, -2, 1, 0), (4, -3, 2, -1))
+STEPS = ((3, -2, 1, 0), (-3, 4, 2, -1))
 
 
 def spread(value, k, sign):
     def move(xl, c, xh, z, y):
-        if xl == c:
-            return (xl, c, xh, z + sign * STEPS[c][k], y)
-        return (1 - xl, 1 - c, 1 - xh, z + (STEPS[c][k] if sign > 0 else -STEPS[1 - c][k]), y)
+        z = z + sign * STEPS[c][k]
+        if xl == xh:
+            return (xl, c, xh, z, y)
+        return (1 - xl, c, 1 - xh, z, y)
 
     return send(value, move)
 
@@ -72,7 +73,7 @@
     sec, dev = lax.axis_index("sec"), lax.axis_index("dev")
     xl, core = sec // 2, sec % 2
     xh, z = dev // 32, (dev // 4) % 8
-    half = jnp.where(xl == core, xh, 1 - xh) * 8
+    half = jnp.where(xl == xh, xh, 1 - xh) * 8
     steps = [jnp.where(core == 0, STEPS[0][k], STEPS[1][k]) for k in range(4)]
     return [half + (z + step + 8) % 8 for step in steps]
 

time: 98.1 us -> 91.4 us (0.932)
  waiting for transfers between devices: 26.4 us -> 22.6 us
  starting transfers between devices: 53.3 us -> 50.4 us
    ppermute x26, waiting for transfers between devices: 26.4 us -> 22.6 us  [send(): return lax.ppermute(value, ('sec', 'dev'), pairs(move))]
    ppermute x26, starting transfers between devices: 53.3 us -> 50.4 us  [send(): return lax.ppermute(value, ('sec', 'dev'), pairs(move))]
  transfers between devices with their start and end apart: 26 -> 26, of which waited for: 11 -> 12; matrix products, arithmetic and copies ran while one was open for 3% -> 3% of each run, Pallas kernels for 13% -> 14%
where the time goes in v5:
time: 91.4 us; the launch traced here: 91.2 us
  starting transfers between devices  50.4 us (55%)
  waiting for transfers between devices  22.6 us (25%)
  Pallas kernels  12.9 us (14%)
  other arithmetic  3.82 us (4%)
  between operations  1.48 us (2%)
    ppermute x26, starting transfers between devices, send(): return lax.ppermute(value, ('sec', 'dev'), pairs(move))  50.4 us
    ppermute x26, waiting for transfers between devices, send(): return lax.ppermute(value, ('sec', 'dev'), pairs(move))  22.6 us
    pallas_call x1, Pallas kernels, attend(): pl.pallas_call(attend_kernel, out_shape=jax.ShapeDtypeStruct((1, heads, L...  5.52 us
    pallas_call x2, Pallas kernels, experts(): pl.pallas_call(functools.partial(expert_kernel, count, rows), out_shape=(...  4.89 us
    concatenate x1, other arithmetic, local(): wide_own = jnp.concatenate([w_gate[0], w_up[0]], axis=1)  2.59 us
    pallas_call x1, Pallas kernels, pack(): pl.pallas_call(pack_kernel, out_shape=(PACKED,) * 4 + (jax.ShapeDtypeStru...  2.11 us
  transfers between devices with their start and end apart: 26, of which 12 were waited for; matrix products, arithmetic and copies ran while one was open for 3% of the time, Pallas kernels for 14%

profile of v5, /device:TPU:1, one launch (start us, length us, event | category | flops | bytes accessed | tf_op | source)
XLA Modules:
  0.0 91.2 jit_solution(3717862510907600433)
XLA Ops:
  0.6 3.3 %collective-permute-start.4 = (bf16[128,7168]{1,0:T(8,128)(2,1)}, bf16[128,7168]{1,0:T(8,128)(2,1)S(1)}, u32[]{:S(2)}, u32[]{:S(2)}) collective-permute-start(bf16[128,7168]{1,0:T(8,128)(2,1)} %bitcast.9), channel_id=1, source_target_pairs={{0,64},{1,65},{2,66},{3,67},{4,68},{5,69},{6,70},{7,71},{8,72},{9,... | collective-permute-start | bytes 5505032 | tf_op jit(solution)/shard_map/ppermute | solution.py:40
  4.0 2.1 %shard_map.113 = (bf16[40,896]{1,0:T(8,128)(2,1)}, bf16[40,896]{1,0:T(8,128)(2,1)}, bf16[40,896]{1,0:T(8,128)(2,1)}, bf16[40,896]{1,0:T(8,128)(2,1)}, f32[8,256]{1,0:T(8,128)}) custom-call(bf16[8,7168]{1,0:T(8,128)(2,1)} %refs_0_.1, f32[1,7168]{1,0:T(1,128)} %bitcast.12, s32[8,8]{1,0:T(8,128)} %refs_2_.1, f32[8,8]{1,0:T(8,128)} %refs_3_.1), custom_call_target="tpu_custom_call" | custom-call | tf_op jit(solution)/shard_map/pallas_call | solution.py:127
  6.1 4.8 %collective-permute-start = (bf16[40,896]{1,0:T(8,128)(2,1)}, bf16[40,896]{1,0:T(8,128)(2,1)S(1)}, u32[]{:S(2)}, u32[]{:S(2)}) collective-permute-start(bf16[40,896]{1,0:T(8,128)(2,1)} %get-tuple-element.35), channel_id=1, source_target_pairs={{0,12},{1,13},{2,14},{3,15},{4,16},{5,17},{6,18},{7,19},{8,20},{9,... | collective-permute-start | bytes 215048 | tf_op jit(solution)/shard_map/ppermute | solution.py:40
  10.9 0.5 collective-permute-start.1
  11.4 1.8 %collective-permute-start.2 = (bf16[40,896]{1,0:T(8,128)(2,1)}, bf16[40,896]{1,0:T(8,128)(2,1)S(1)}, u32[]{:S(2)}, u32[]{:S(2)}) collective-permute-start(bf16[40,896]{1,0:T(8,128)(2,1)} %get-tuple-element.37), channel_id=1, source_target_pairs={{0,4},{1,5},{2,6},{3,7},{4,8},{5,9},{6,10},{7,11},{8,12},{9,13},{1... | collective-permute-start | bytes 215048 | tf_op jit(solution)/shard_map/ppermute | solution.py:40
  13.2 3.2 %collective-permute-start.3 = (bf16[40,896]{1,0:T(8,128)(2,1)}, bf16[40,896]{1,0:T(8,128)(2,1)S(1)}, u32[]{:S(2)}, u32[]{:S(2)}) collective-permute-start(bf16[40,896]{1,0:T(8,128)(2,1)} %get-tuple-element.38), channel_id=1, source_target_pairs={{0,0},{1,1},{2,2},{3,3},{4,4},{5,5},{6,6},{7,7},{8,8},{9,9},{10,10... | collective-permute-start | bytes 215048 | tf_op jit(solution)/shard_map/ppermute | solution.py:40
  16.5 2.6 %pad_maximum_fusion.refs_5_.refs_3_ = bf16[7168,256]{1,0:T(8,128)(2,1)S(1)} fusion(bf16[7168,128]{1,0:T(8,128)(2,1)} %bitcast.7, bf16[7168,128]{1,0:T(8,128)(2,1)} %bitcast.8), kind=kLoop, calls=%fused_computation | loop fusion | flops 7340032 | bytes 7340032 | tf_op jit(solution)/shard_map/concatenate | solution.py:341
  19.1 0.4 collective-permute-done.2.c
  19.5 0.1 collective-permute-start.7
  19.6 3.6 %collective-permute-start.5 = (bf16[160,896]{1,0:T(8,128)(2,1)S(1)}, bf16[160,896]{1,0:T(8,128)(2,1)S(1)}, u32[]{:S(2)}, u32[]{:S(2)}) collective-permute-start(bf16[160,896]{1,0:T(8,128)(2,1)S(1)} %shard_map.114.refs_0_), channel_id=1, source_target_pairs={{0,128},{1,129},{2,130},{3,131},{4,132},{5,133},{6,134},{7,135},{8... | collective-permute-start | bytes 860168 | tf_op jit(solution)/shard_map/ppermute | solution.py:40
  23.2 2.9 %collective-permute-start.6 = (bf16[160,896]{1,0:T(8,128)(2,1)S(1)}, bf16[160,896]{1,0:T(8,128)(2,1)S(1)}, u32[]{:S(2)}, u32[]{:S(2)}) collective-permute-start(bf16[160,896]{1,0:T(8,128)(2,1)S(1)} %shard_map.114.refs_0_), channel_id=1, source_target_pairs={{0,2},{1,3},{2,0},{3,1},{4,6},{5,7},{6,4},{7,5},{8,10},{9,11},{10,... | collective-permute-start | bytes 860168 | tf_op jit(solution)/shard_map/ppermute | solution.py:40
  26.1 0.4 collective-permute-start.9
  26.5 2.3 %collective-permute-start.10 = (bf16[160,896]{1,0:T(8,128)(2,1)S(1)}, bf16[160,896]{1,0:T(8,128)(2,1)S(1)}, u32[]{:S(2)}, u32[]{:S(2)}) collective-permute-start(bf16[160,896]{1,0:T(8,128)(2,1)S(1)} %shard_map.114.refs_0_), channel_id=1, source_target_pairs={{0,3},{1,0},{2,1},{3,2},{4,7},{5,4},{6,5},{7,6},{8,11},{9,8},{10,9... | collective-permute-start | bytes 860168 | tf_op jit(solution)/shard_map/ppermute | solution.py:40
  28.8 0.2 pad_maximum_fusion.1.refs_7_.refs_5_
  29.0 1.0 %collective-permute-done.5.refs_1_ = bf16[160,896]{1,0:T(8,128)(2,1)S(1)} collective-permute-done((bf16[160,896]{1,0:T(8,128)(2,1)S(1)}, bf16[160,896]{1,0:T(8,128)(2,1)S(1)}, u32[]{:S(2)}, u32[]{:S(2)}) %collective-permute-start.5) | collective-permute-done | bytes 286752 | tf_op jit(solution)/shard_map/ppermute | solution.py:40
  30.1 2.4 %collective-permute-done.6.refs_2_ = bf16[160,896]{1,0:T(8,128)(2,1)S(1)} collective-permute-done((bf16[160,896]{1,0:T(8,128)(2,1)S(1)}, bf16[160,896]{1,0:T(8,128)(2,1)S(1)}, u32[]{:S(2)}, u32[]{:S(2)}) %collective-permute-start.6) | collective-permute-done | bytes 286752 | tf_op jit(solution)/shard_map/ppermute | solution.py:40
  32.4 1.3 %collective-permute-start.8 = (bf16[160,896]{1,0:T(8,128)(2,1)S(1)}, bf16[160,896]{1,0:T(8,128)(2,1)S(1)}, u32[]{:S(2)}, u32[]{:S(2)}) collective-permute-start(bf16[160,896]{1,0:T(8,128)(2,1)S(1)} %collective-permute-done.5.refs_1_), channel_id=1, source_target_pairs={{0,1},{1,2},{2,3},{3,0},{4,5},{5,6},{6,7},{7,4},{8,9},{9,10},{10,1... | collective-permute-start | bytes 860168 | tf_op jit(solution)/shard_map/ppermute | solution.py:40
  33.7 1.4 %collective-permute-start.13 = (bf16[160,896]{1,0:T(8,128)(2,1)S(1)}, bf16[160,896]{1,0:T(8,128)(2,1)S(1)}, u32[]{:S(2)}, u32[]{:S(2)}) collective-permute-start(bf16[160,896]{1,0:T(8,128)(2,1)S(1)} %collective-permute-done.5.refs_1_), channel_id=1, source_target_pairs={{0,3},{1,0},{2,1},{3,2},{4,7},{5,4},{6,5},{7,6},{8,11},{9,8},{10,9... | collective-permute-start | bytes 860168 | tf_op jit(solution)/shard_map/ppermute | solution.py:40
  35.2 0.5 collective-permute-start.14
  35.7 3.9 %collective-permute-done.9.refs_3_ = bf16[160,896]{1,0:T(8,128)(2,1)S(1)} collective-permute-done((bf16[160,896]{1,0:T(8,128)(2,1)S(1)}, bf16[160,896]{1,0:T(8,128)(2,1)S(1)}, u32[]{:S(2)}, u32[]{:S(2)}) %collective-permute-start.9) | collective-permute-done | bytes 286752 | tf_op jit(solution)/shard_map/ppermute | solution.py:40
  39.6 2.6 %shard_map.115 = (bf16[160,896]{1,0:T(8,128)(2,1)S(1)}, bf16[160,896]{1,0:T(8,128)(2,1)S(1)}, bf16[160,896]{1,0:T(8,128)(2,1)S(1)}, bf16[160,896]{1,0:T(8,128)(2,1)S(1)}, bf16[160,896]{1,0:T(8,128)(2,1)S(1)}) custom-call(bf16[160,896]{1,0:T(8,128)(2,1)S(1)} %shard_map.114.refs_0_, bf16[160,896]{1,0:T(8,128)(2,1)S(1)} %collective-permute-done.5.refs_1_, ...), custom_call_target="tpu_custom_call" | custom-call | flops 1233125376 | bytes 14221312 | tf_op jit(solution)/shard_map/pallas_call | solution.py:238
  42.2 1.6 %collective-permute-start.12 = (bf16[160,896]{1,0:T(8,128)(2,1)S(1)}, bf16[160,896]{1,0:T(8,128)(2,1)S(1)}, u32[]{:S(2)}, u32[]{:S(2)}) collective-permute-start(bf16[160,896]{1,0:T(8,128)(2,1)S(1)} %get-tuple-element.50), channel_id=1, source_target_pairs={{0,1},{1,2},{2,3},{3,0},{4,5},{5,6},{6,7},{7,4},{8,9},{9,10},{10,1... | collective-permute-start | bytes 860168 | tf_op jit(solution)/shard_map/ppermute | solution.py:40
  43.8 1.5 %collective-permute-start.11 = (bf16[160,896]{1,0:T(8,128)(2,1)S(1)}, bf16[160,896]{1,0:T(8,128)(2,1)S(1)}, u32[]{:S(2)}, u32[]{:S(2)}) collective-permute-start(bf16[160,896]{1,0:T(8,128)(2,1)S(1)} %get-tuple-element.49), channel_id=1, source_target_pairs={{0,3},{1,0},{2,1},{3,2},{4,7},{5,4},{6,5},{7,6},{8,11},{9,8},{10,9... | collective-permute-start | bytes 860168 | tf_op jit(solution)/shard_map/ppermute | solution.py:40
  45.3 0.4 collective-permute-done.8.refs_0_
  45.7 2.3 %shard_map.116 = (bf16[160,896]{1,0:T(8,128)(2,1)S(1)}, bf16[160,896]{1,0:T(8,128)(2,1)S(1)}, bf16[160,896]{1,0:T(8,128)(2,1)S(1)}) custom-call(bf16[160,896]{1,0:T(8,128)(2,1)S(1)} %collective-permute-done.8.refs_0_, bf16[160,896]{1,0:T(8,128)(2,1)S(1)} %collective-permute-done.13.refs_1_, bf16[160,896]{1,0:T(8,128)(2,1)S(1)} %collective-permute-done.14.refs_2_, ...), custom_call_target="tpu_custom_call" | custom-call | flops 704643072 | bytes 12845056 | tf_op jit(solution)/shard_map/pallas_call | solution.py:238
  48.0 0.2 collective-permute-start.17
  48.2 1.3 %collective-permute-start.16 = (bf16[160,896]{1,0:T(8,128)(2,1)S(1)}, bf16[160,896]{1,0:T(8,128)(2,1)S(1)}, u32[]{:S(2)}, u32[]{:S(2)}) collective-permute-start(bf16[160,896]{1,0:T(8,128)(2,1)S(1)} %get-tuple-element.54), channel_id=1, source_target_pairs={{0,1},{1,2},{2,3},{3,0},{4,5},{5,6},{6,7},{7,4},{8,9},{9,10},{10,1... | collective-permute-start | bytes 860168 | tf_op jit(solution)/shard_map/ppermute | solution.py:40
  49.5 1.5 %collective-permute-start.15 = (bf16[160,896]{1,0:T(8,128)(2,1)S(1)}, bf16[160,896]{1,0:T(8,128)(2,1)S(1)}, u32[]{:S(2)}, u32[]{:S(2)}) collective-permute-start(bf16[160,896]{1,0:T(8,128)(2,1)S(1)} %get-tuple-element.53), channel_id=1, source_target_pairs={{0,3},{1,0},{2,1},{3,2},{4,7},{5,4},{6,5},{7,6},{8,11},{9,8},{10,9... | collective-permute-start | bytes 860168 | tf_op jit(solution)/shard_map/ppermute | solution.py:40
  51.0 0.1 convert_add_fusion.b0
  51.1 3.3 %collective-permute-done.17 = bf16[160,896]{1,0:T(8,128)(2,1)S(1)} collective-permute-done((bf16[160,896]{1,0:T(8,128)(2,1)S(1)}, bf16[160,896]{1,0:T(8,128)(2,1)S(1)}, u32[]{:S(2)}, u32[]{:S(2)}) %collective-permute-start.17) | collective-permute-done | bytes 286752 | tf_op jit(solution)/shard_map/ppermute | solution.py:40
  54.5 2.2 %collective-permute-done.16 = bf16[160,896]{1,0:T(8,128)(2,1)S(1)} collective-permute-done((bf16[160,896]{1,0:T(8,128)(2,1)S(1)}, bf16[160,896]{1,0:T(8,128)(2,1)S(1)}, u32[]{:S(2)}, u32[]{:S(2)}) %collective-permute-start.16) | collective-permute-done | bytes 286752 | tf_op jit(solution)/shard_map/ppermute | solution.py:40
  56.7 0.1 add_convert_fusion.1
  56.8 3.6 %collective-permute-start.18 = (bf16[160,896]{1,0:T(8,128)(2,1)S(1)}, bf16[160,896]{1,0:T(8,128)(2,1)S(1)}, u32[]{:S(2)}, u32[]{:S(2)}) collective-permute-start(bf16[160,896]{1,0:T(8,128)(2,1)S(1)} %add_convert_fusion), channel_id=1, source_target_pairs={{0,2},{1,3},{2,0},{3,1},{4,6},{5,7},{6,4},{7,5},{8,10},{9,11},{10,... | collective-permute-start | bytes 860168 | tf_op jit(solution)/shard_map/ppermute | solution.py:40
  60.4 0.6 collective-permute-start.19
  61.6 5.5 %shard_map.117 = bf16[1,128,512]{2,1,0:T(8,128)(2,1)} custom-call(s32[1]{0:T(128)S(6)} %copy.12.length_ref, bf16[1,576,128]{2,1,0:T(8,128)(2,1)} %bitcast.11, bf16[1,576,4096]{2,1,0:T(8,128)(2,1)} %bitcast.6), custom_call_target="tpu_custom_call" | custom-call | flops 1140850688 | bytes 4718592 | tf_op jit(solution)/shard_map/pallas_call | solution.py:301
  67.2 0.1 shard_map.118
  67.3 4.5 %collective-permute-start.20 = (bf16[40,896]{1,0:T(8,128)(2,1)S(1)}, bf16[40,896]{1,0:T(8,128)(2,1)S(1)}, u32[]{:S(2)}, u32[]{:S(2)}) collective-permute-start(bf16[40,896]{1,0:T(8,128)(2,1)S(1)} %get-tuple-element.64), channel_id=1, source_target_pairs={{0,20},{1,21},{2,22},{3,23},{4,24},{5,25},{6,26},{7,27},{8,28},{9,... | collective-permute-start | bytes 215048 | tf_op jit(solution)/shard_map/ppermute | solution.py:40
  71.8 0.3 collective-permute-start.21
  72.1 3.4 %collective-permute-start.22 = (bf16[40,896]{1,0:T(8,128)(2,1)S(1)}, bf16[40,896]{1,0:T(8,128)(2,1)S(1)}, u32[]{:S(2)}, u32[]{:S(2)}) collective-permute-start(bf16[40,896]{1,0:T(8,128)(2,1)S(1)} %get-tuple-element.66), channel_id=1, source_target_pairs={{0,28},{1,29},{2,30},{3,31},{4,0},{5,1},{6,2},{7,3},{8,4},{9,5},{1... | collective-permute-start | bytes 215048 | tf_op jit(solution)/shard_map/ppermute | solution.py:40
  75.5 1.9 %collective-permute-start.23 = (bf16[40,896]{1,0:T(8,128)(2,1)S(1)}, bf16[40,896]{1,0:T(8,128)(2,1)S(1)}, u32[]{:S(2)}, u32[]{:S(2)}) collective-permute-start(bf16[40,896]{1,0:T(8,128)(2,1)S(1)} %get-tuple-element.67), channel_id=1, source_target_pairs={{0,0},{1,1},{2,2},{3,3},{4,4},{5,5},{6,6},{7,7},{8,8},{9,9},{10,10... | collective-permute-start | bytes 215048 | tf_op jit(solution)/shard_map/ppermute | solution.py:40
  77.4 2.2 %collective-permute-done.21.b = bf16[40,896]{1,0:T(8,128)(2,1)S(1)} collective-permute-done((bf16[40,896]{1,0:T(8,128)(2,1)S(1)}, bf16[40,896]{1,0:T(8,128)(2,1)S(1)}, u32[]{:S(2)}, u32[]{:S(2)}) %collective-permute-start.21) | collective-permute-done | bytes 71712 | tf_op jit(solution)/shard_map/ppermute | solution.py:40
  79.6 1.2 %collective-permute-done.22.c = bf16[40,896]{1,0:T(8,128)(2,1)S(1)} collective-permute-done((bf16[40,896]{1,0:T(8,128)(2,1)S(1)}, bf16[40,896]{1,0:T(8,128)(2,1)S(1)}, u32[]{:S(2)}, u32[]{:S(2)}) %collective-permute-start.22) | collective-permute-done | bytes 71712 | tf_op jit(solution)/shard_map/ppermute | solution.py:40
  80.8 0.9 collective-permute-done.23.d
  81.7 0.3 shard_map.119
  82.1 1.3 %collective-permute-done.24 = bf16[8,7168]{1,0:T(8,128)(2,1)S(1)} collective-permute-done((bf16[8,7168]{1,0:T(8,128)(2,1)S(1)}, bf16[8,7168]{1,0:T(8,128)(2,1)S(1)}, u32[]{:S(2)}, u32[]{:S(2)}) %collective-permute-start.24) | collective-permute-done | bytes 114720 | tf_op jit(solution)/shard_map/ppermute | solution.py:40
  83.4 3.7 %collective-permute-start.25 = (bf16[8,7168]{1,0:T(8,128)(2,1)S(1)}, bf16[8,7168]{1,0:T(8,128)(2,1)S(1)}, u32[]{:S(2)}, u32[]{:S(2)}) collective-permute-start(bf16[8,7168]{1,0:T(8,128)(2,1)S(1)} %add_convert_fusion.3), channel_id=1, source_target_pairs={{0,128},{1,129},{2,130},{3,131},{4,132},{5,133},{6,134},{7,135},{8... | collective-permute-start | bytes 344072 | tf_op jit(solution)/shard_map/ppermute | solution.py:40
  87.2 3.4 %collective-permute-done.25 = bf16[8,7168]{1,0:T(8,128)(2,1)S(1)} collective-permute-done((bf16[8,7168]{1,0:T(8,128)(2,1)S(1)}, bf16[8,7168]{1,0:T(8,128)(2,1)S(1)}, u32[]{:S(2)}, u32[]{:S(2)}) %collective-permute-start.25) | collective-permute-done | bytes 114720 | tf_op jit(solution)/shard_map/ppermute | solution.py:40
  90.5 0.7 add_convert_fusion.2
  (24 shorter events, 0.3 us)
Async XLA Ops:
  0.6 18.8 %collective-permute-start.4 = (bf16[128,7168]{1,0:T(8,128)(2,1)}, bf16[128,7168]{1,0:T(8,128)(2,1)S(1)}, u32[]{:S(2)}, u32[]{:S(2)}) collective-permute-start(bf16[128,7168]{1,0:T(8,128)(2,1)} %bitcast.9), channel_id=1, source_target_pairs={{0,64},{1,65},{2,66},{3,67},{4,68},{5,69},{6,70},{7,71},{8,72},{9,... | collective-permute-start | bytes 5505032 | tf_op jit(solution)/shard_map/ppermute | solution.py:40
  6.1 13.0 %collective-permute-start = (bf16[40,896]{1,0:T(8,128)(2,1)}, bf16[40,896]{1,0:T(8,128)(2,1)S(1)}, u32[]{:S(2)}, u32[]{:S(2)}) collective-permute-start(bf16[40,896]{1,0:T(8,128)(2,1)} %get-tuple-element.35), channel_id=1, source_target_pairs={{0,12},{1,13},{2,14},{3,15},{4,16},{5,17},{6,18},{7,19},{8,20},{9,... | collective-permute-start | bytes 215048 | tf_op jit(solution)/shard_map/ppermute | solution.py:40
  10.9 8.2 %collective-permute-start.1 = (bf16[40,896]{1,0:T(8,128)(2,1)}, bf16[40,896]{1,0:T(8,128)(2,1)S(1)}, u32[]{:S(2)}, u32[]{:S(2)}) collective-permute-start(bf16[40,896]{1,0:T(8,128)(2,1)} %get-tuple-element.36), channel_id=1, source_target_pairs={{0,24},{1,25},{2,26},{3,27},{4,28},{5,29},{6,30},{7,31},{8,0},{9,1... | collective-permute-start | bytes 215048 | tf_op jit(solution)/shard_map/ppermute | solution.py:40
  11.4 8.0 %collective-permute-start.2 = (bf16[40,896]{1,0:T(8,128)(2,1)}, bf16[40,896]{1,0:T(8,128)(2,1)S(1)}, u32[]{:S(2)}, u32[]{:S(2)}) collective-permute-start(bf16[40,896]{1,0:T(8,128)(2,1)} %get-tuple-element.37), channel_id=1, source_target_pairs={{0,4},{1,5},{2,6},{3,7},{4,8},{5,9},{6,10},{7,11},{8,12},{9,13},{1... | collective-permute-start | bytes 215048 | tf_op jit(solution)/shard_map/ppermute | solution.py:40
  13.2 6.2 %collective-permute-start.3 = (bf16[40,896]{1,0:T(8,128)(2,1)}, bf16[40,896]{1,0:T(8,128)(2,1)S(1)}, u32[]{:S(2)}, u32[]{:S(2)}) collective-permute-start(bf16[40,896]{1,0:T(8,128)(2,1)} %get-tuple-element.38), channel_id=1, source_target_pairs={{0,0},{1,1},{2,2},{3,3},{4,4},{5,5},{6,6},{7,7},{8,8},{9,9},{10,10... | collective-permute-start | bytes 215048 | tf_op jit(solution)/shard_map/ppermute | solution.py:40
  16.4 12.3 %copy-start.1 = (bf16[1,128,7168]{2,1,0:T(8,128)(2,1)S(1)}, bf16[1,128,7168]{2,1,0:T(8,128)(2,1)}, u32[]{:S(2)}) copy-start(bf16[1,128,7168]{2,1,0:T(8,128)(2,1)} %param.19) | copy-start | bytes 5505028
  19.5 12.9 %collective-permute-start.7 = (bf16[7168,256]{1,0:T(8,128)(2,1)S(1)}, bf16[7168,256]{1,0:T(8,128)(2,1)S(1)}, u32[]{:S(2)}, u32[]{:S(2)}) collective-permute-start(bf16[7168,256]{1,0:T(8,128)(2,1)S(1)} %pad_maximum_fusion.refs_5_.refs_3_), channel_id=1, source_target_pairs={{0,64},{1,65},{2,66},{3,67},{4,68},{5,69},{6,70},{7,71},{8,72},{9,... | collective-permute-start | bytes 11010056 | tf_op jit(solution)/shard_map/ppermute | solution.py:40
  19.6 10.5 %collective-permute-start.5 = (bf16[160,896]{1,0:T(8,128)(2,1)S(1)}, bf16[160,896]{1,0:T(8,128)(2,1)S(1)}, u32[]{:S(2)}, u32[]{:S(2)}) collective-permute-start(bf16[160,896]{1,0:T(8,128)(2,1)S(1)} %shard_map.114.refs_0_), channel_id=1, source_target_pairs={{0,128},{1,129},{2,130},{3,131},{4,132},{5,133},{6,134},{7,135},{8... | collective-permute-start | bytes 860168 | tf_op jit(solution)/shard_map/ppermute | solution.py:40
  23.2 9.2 %collective-permute-start.6 = (bf16[160,896]{1,0:T(8,128)(2,1)S(1)}, bf16[160,896]{1,0:T(8,128)(2,1)S(1)}, u32[]{:S(2)}, u32[]{:S(2)}) collective-permute-start(bf16[160,896]{1,0:T(8,128)(2,1)S(1)} %shard_map.114.refs_0_), channel_id=1, source_target_pairs={{0,2},{1,3},{2,0},{3,1},{4,6},{5,7},{6,4},{7,5},{8,10},{9,11},{10,... | collective-permute-start | bytes 860168 | tf_op jit(solution)/shard_map/ppermute | solution.py:40
  26.1 13.5 %collective-permute-start.9 = (bf16[160,896]{1,0:T(8,128)(2,1)S(1)}, bf16[160,896]{1,0:T(8,128)(2,1)S(1)}, u32[]{:S(2)}, u32[]{:S(2)}) collective-permute-start(bf16[160,896]{1,0:T(8,128)(2,1)S(1)} %shard_map.114.refs_0_), channel_id=1, source_target_pairs={{0,1},{1,2},{2,3},{3,0},{4,5},{5,6},{6,7},{7,4},{8,9},{9,10},{10,1... | collective-permute-start | bytes 860168 | tf_op jit(solution)/shard_map/ppermute | solution.py:40
  26.5 13.1 %collective-permute-start.10 = (bf16[160,896]{1,0:T(8,128)(2,1)S(1)}, bf16[160,896]{1,0:T(8,128)(2,1)S(1)}, u32[]{:S(2)}, u32[]{:S(2)}) collective-permute-start(bf16[160,896]{1,0:T(8,128)(2,1)S(1)} %shard_map.114.refs_0_), channel_id=1, source_target_pairs={{0,3},{1,0},{2,1},{3,2},{4,7},{5,4},{6,5},{7,6},{8,11},{9,8},{10,9... | collective-permute-start | bytes 860168 | tf_op jit(solution)/shard_map/ppermute | solution.py:40
  32.4 13.3 %collective-permute-start.8 = (bf16[160,896]{1,0:T(8,128)(2,1)S(1)}, bf16[160,896]{1,0:T(8,128)(2,1)S(1)}, u32[]{:S(2)}, u32[]{:S(2)}) collective-permute-start(bf16[160,896]{1,0:T(8,128)(2,1)S(1)} %collective-permute-done.5.refs_1_), channel_id=1, source_target_pairs={{0,1},{1,2},{2,3},{3,0},{4,5},{5,6},{6,7},{7,4},{8,9},{9,10},{10,1... | collective-permute-start | bytes 860168 | tf_op jit(solution)/shard_map/ppermute | solution.py:40
  33.7 12.0 %collective-permute-start.13 = (bf16[160,896]{1,0:T(8,128)(2,1)S(1)}, bf16[160,896]{1,0:T(8,128)(2,1)S(1)}, u32[]{:S(2)}, u32[]{:S(2)}) collective-permute-start(bf16[160,896]{1,0:T(8,128)(2,1)S(1)} %collective-permute-done.5.refs_1_), channel_id=1, source_target_pairs={{0,3},{1,0},{2,1},{3,2},{4,7},{5,4},{6,5},{7,6},{8,11},{9,8},{10,9... | collective-permute-start | bytes 860168 | tf_op jit(solution)/shard_map/ppermute | solution.py:40
  35.2 10.6 %collective-permute-start.14 = (bf16[160,896]{1,0:T(8,128)(2,1)S(1)}, bf16[160,896]{1,0:T(8,128)(2,1)S(1)}, u32[]{:S(2)}, u32[]{:S(2)}) collective-permute-start(bf16[160,896]{1,0:T(8,128)(2,1)S(1)} %collective-permute-done.6.refs_2_), channel_id=1, source_target_pairs={{0,128},{1,129},{2,130},{3,131},{4,132},{5,133},{6,134},{7,135},{8... | collective-permute-start | bytes 860168 | tf_op jit(solution)/shard_map/ppermute | solution.py:40
  42.2 8.8 %collective-permute-start.12 = (bf16[160,896]{1,0:T(8,128)(2,1)S(1)}, bf16[160,896]{1,0:T(8,128)(2,1)S(1)}, u32[]{:S(2)}, u32[]{:S(2)}) collective-permute-start(bf16[160,896]{1,0:T(8,128)(2,1)S(1)} %get-tuple-element.50), channel_id=1, source_target_pairs={{0,1},{1,2},{2,3},{3,0},{4,5},{5,6},{6,7},{7,4},{8,9},{9,10},{10,1... | collective-permute-start | bytes 860168 | tf_op jit(solution)/shard_map/ppermute | solution.py:40
  43.8 7.3 %collective-permute-start.11 = (bf16[160,896]{1,0:T(8,128)(2,1)S(1)}, bf16[160,896]{1,0:T(8,128)(2,1)S(1)}, u32[]{:S(2)}, u32[]{:S(2)}) collective-permute-start(bf16[160,896]{1,0:T(8,128)(2,1)S(1)} %get-tuple-element.49), channel_id=1, source_target_pairs={{0,3},{1,0},{2,1},{3,2},{4,7},{5,4},{6,5},{7,6},{8,11},{9,8},{10,9... | collective-permute-start | bytes 860168 | tf_op jit(solution)/shard_map/ppermute | solution.py:40
  48.0 6.4 %collective-permute-start.17 = (bf16[160,896]{1,0:T(8,128)(2,1)S(1)}, bf16[160,896]{1,0:T(8,128)(2,1)S(1)}, u32[]{:S(2)}, u32[]{:S(2)}) collective-permute-start(bf16[160,896]{1,0:T(8,128)(2,1)S(1)} %get-tuple-element.56), channel_id=1, source_target_pairs={{0,128},{1,129},{2,130},{3,131},{4,132},{5,133},{6,134},{7,135},{8... | collective-permute-start | bytes 860168 | tf_op jit(solution)/shard_map/ppermute | solution.py:40
  48.2 8.4 %collective-permute-start.16 = (bf16[160,896]{1,0:T(8,128)(2,1)S(1)}, bf16[160,896]{1,0:T(8,128)(2,1)S(1)}, u32[]{:S(2)}, u32[]{:S(2)}) collective-permute-start(bf16[160,896]{1,0:T(8,128)(2,1)S(1)} %get-tuple-element.54), channel_id=1, source_target_pairs={{0,1},{1,2},{2,3},{3,0},{4,5},{5,6},{6,7},{7,4},{8,9},{9,10},{10,1... | collective-permute-start | bytes 860168 | tf_op jit(solution)/shard_map/ppermute | solution.py:40
  49.5 7.2 %collective-permute-start.15 = (bf16[160,896]{1,0:T(8,128)(2,1)S(1)}, bf16[160,896]{1,0:T(8,128)(2,1)S(1)}, u32[]{:S(2)}, u32[]{:S(2)}) collective-permute-start(bf16[160,896]{1,0:T(8,128)(2,1)S(1)} %get-tuple-element.53), channel_id=1, source_target_pairs={{0,3},{1,0},{2,1},{3,2},{4,7},{5,4},{6,5},{7,6},{8,11},{9,8},{10,9... | collective-permute-start | bytes 860168 | tf_op jit(solution)/shard_map/ppermute | solution.py:40
  54.5 27.2 %copy-start = (f32[8,256]{1,0:T(8,128)S(1)}, f32[8,256]{1,0:T(8,128)}, u32[]{:S(2)}) copy-start(f32[8,256]{1,0:T(8,128)} %get-tuple-element.60.table_ref) | copy-start | bytes 24580
  56.8 33.7 %copy-start.2 = (bf16[8,7168]{1,0:T(8,128)(2,1)S(1)}, bf16[8,7168]{1,0:T(8,128)(2,1)}, u32[]{:S(2)}) copy-start(bf16[8,7168]{1,0:T(8,128)(2,1)} %refs_0_.1) | copy-start | bytes 344068
  56.8 10.4 %collective-permute-start.18 = (bf16[160,896]{1,0:T(8,128)(2,1)S(1)}, bf16[160,896]{1,0:T(8,128)(2,1)S(1)}, u32[]{:S(2)}, u32[]{:S(2)}) collective-permute-start(bf16[160,896]{1,0:T(8,128)(2,1)S(1)} %add_convert_fusion), channel_id=1, source_target_pairs={{0,2},{1,3},{2,0},{3,1},{4,6},{5,7},{6,4},{7,5},{8,10},{9,11},{10,... | collective-permute-start | bytes 860168 | tf_op jit(solution)/shard_map/ppermute | solution.py:40
  60.4 6.8 %collective-permute-start.19 = (bf16[160,896]{1,0:T(8,128)(2,1)S(1)}, bf16[160,896]{1,0:T(8,128)(2,1)S(1)}, u32[]{:S(2)}, u32[]{:S(2)}) collective-permute-start(bf16[160,896]{1,0:T(8,128)(2,1)S(1)} %add_convert_fusion.1), channel_id=1, source_target_pairs={{0,128},{1,129},{2,130},{3,131},{4,132},{5,133},{6,134},{7,135},{8... | collective-permute-start | bytes 860168 | tf_op jit(solution)/shard_map/ppermute | solution.py:40
  67.3 10.1 %collective-permute-start.20 = (bf16[40,896]{1,0:T(8,128)(2,1)S(1)}, bf16[40,896]{1,0:T(8,128)(2,1)S(1)}, u32[]{:S(2)}, u32[]{:S(2)}) collective-permute-start(bf16[40,896]{1,0:T(8,128)(2,1)S(1)} %get-tuple-element.64), channel_id=1, source_target_pairs={{0,20},{1,21},{2,22},{3,23},{4,24},{5,25},{6,26},{7,27},{8,28},{9,... | collective-permute-start | bytes 215048 | tf_op jit(solution)/shard_map/ppermute | solution.py:40
  71.8 7.8 %collective-permute-start.21 = (bf16[40,896]{1,0:T(8,128)(2,1)S(1)}, bf16[40,896]{1,0:T(8,128)(2,1)S(1)}, u32[]{:S(2)}, u32[]{:S(2)}) collective-permute-start(bf16[40,896]{1,0:T(8,128)(2,1)S(1)} %get-tuple-element.65), channel_id=1, source_target_pairs={{0,8},{1,9},{2,10},{3,11},{4,12},{5,13},{6,14},{7,15},{8,16},{9,17... | collective-permute-start | bytes 215048 | tf_op jit(solution)/shard_map/ppermute | solution.py:40
  72.1 8.8 %collective-permute-start.22 = (bf16[40,896]{1,0:T(8,128)(2,1)S(1)}, bf16[40,896]{1,0:T(8,128)(2,1)S(1)}, u32[]{:S(2)}, u32[]{:S(2)}) collective-permute-start(bf16[40,896]{1,0:T(8,128)(2,1)S(1)} %get-tuple-element.66), channel_id=1, source_target_pairs={{0,28},{1,29},{2,30},{3,31},{4,0},{5,1},{6,2},{7,3},{8,4},{9,5},{1... | collective-permute-start | bytes 215048 | tf_op jit(solution)/shard_map/ppermute | solution.py:40
  75.5 6.3 %collective-permute-start.23 = (bf16[40,896]{1,0:T(8,128)(2,1)S(1)}, bf16[40,896]{1,0:T(8,128)(2,1)S(1)}, u32[]{:S(2)}, u32[]{:S(2)}) collective-permute-start(bf16[40,896]{1,0:T(8,128)(2,1)S(1)} %get-tuple-element.67), channel_id=1, source_target_pairs={{0,0},{1,1},{2,2},{3,3},{4,4},{5,5},{6,6},{7,7},{8,8},{9,9},{10,10... | collective-permute-start | bytes 215048 | tf_op jit(solution)/shard_map/ppermute | solution.py:40
  82.0 1.4 %collective-permute-start.24 = (bf16[8,7168]{1,0:T(8,128)(2,1)S(1)}, bf16[8,7168]{1,0:T(8,128)(2,1)S(1)}, u32[]{:S(2)}, u32[]{:S(2)}) collective-permute-start(bf16[8,7168]{1,0:T(8,128)(2,1)S(1)} %shard_map.119), channel_id=1, source_target_pairs={{0,64},{1,65},{2,66},{3,67},{4,68},{5,69},{6,70},{7,71},{8,72},{9,... | collective-permute-start | bytes 344072 | tf_op jit(solution)/shard_map/ppermute | solution.py:40
  83.4 7.1 %collective-permute-start.25 = (bf16[8,7168]{1,0:T(8,128)(2,1)S(1)}, bf16[8,7168]{1,0:T(8,128)(2,1)S(1)}, u32[]{:S(2)}, u32[]{:S(2)}) collective-permute-start(bf16[8,7168]{1,0:T(8,128)(2,1)S(1)} %add_convert_fusion.3), channel_id=1, source_target_pairs={{0,128},{1,129},{2,130},{3,131},{4,132},{5,133},{6,134},{7,135},{8... | collective-permute-start | bytes 344072 | tf_op jit(solution)/shard_map/ppermute | solution.py:40

commit v6 on v5

--- a/solution.py
+++ b/solution.py
@@ -146,10 +146,8 @@
     )(*parts)
 
 
-def split_kernel(b0, b1, b2, o0, o1, o2, o3):
-    total = b0[...]
-    for ref in (b1, b2):
-        total = total + ref[...].astype(jnp.float32)
+def split_kernel(b0, b1, o0, o1, o2, o3):
+    total = b0[...] + b1[...].astype(jnp.float32)
     for k, ref in enumerate((o0, o1, o2, o3)):
         ref[...] = total[k * CAP * PIECES : (k + 1) * CAP * PIECES].astype(jnp.bfloat16)
 
@@ -158,7 +156,7 @@
     return pl.pallas_call(
         split_kernel,
         out_shape=(PACKED,) * 4,
-        in_specs=[VMEM] * 3,
+        in_specs=[VMEM] * 2,
         out_specs=(VMEM,) * 4,
         compiler_params=limit(8),
     )(*blocks)
@@ -356,7 +354,8 @@
     up_in = along(mine, 1)
     dn_in = along(mine, -1)
     y2_in = along(mine, 2)
-    x_in, y2_in, wide_other, down = lax.optimization_barrier((x_in, y2_in, wide_other, down))
+    x_in, wide_other, down = lax.optimization_barrier((x_in, wide_other, down))
+    y2_in, _ = lax.optimization_barrier((y2_in, x_in))
     weights = (wide_own, wide_other, down)
     x_up_in = along(x_in, 1)
     x_dn_in = along(x_in, -1)
@@ -374,14 +373,16 @@
         return sum(v.astype(jnp.float32) for v in values)
 
     near = add(own, up_back, dn_back)
+    y2_sum = add(y2_out, x_y2_back).astype(jnp.bfloat16)
+    y2_back = along(y2_sum, 2)
+    x_up_back, _ = lax.optimization_barrier((x_up_back, y2_sum))
     x_sum = add(x_out, x_up_back, x_dn_back).astype(jnp.bfloat16)
-    y2_sum = add(y2_out, x_y2_back).astype(jnp.bfloat16)
-    near, x_sum, y2_sum, queries = lax.optimization_barrier((near, x_sum, y2_sum, queries))
+    near, x_sum, queries = lax.optimization_barrier((near, x_sum, queries))
     x_back = over(x_sum)
-    y2_back = along(y2_sum, 2)
     context = attend(queries, latent_cache, cache_lengths)
     near, context = lax.optimization_barrier((near, context))
-    back = split((near, y2_back, x_back))
+    near = add(near, y2_back)
+    back = split((near, x_back))
     returned = [spread(back[k], k, -1) for k in range(4)]
     part = weigh(table, returned)
     pair = part.astype(jnp.float32) + swap_core(part).astype(jnp.float32)

time: 91.4 us -> 89.7 us (0.981)
  waiting for transfers between devices: 22.6 us -> 20.4 us
    ppermute x26, waiting for transfers between devices: 22.6 us -> 20.4 us  [send(): return lax.ppermute(value, ('sec', 'dev'), pairs(move))]
  transfers between devices with their start and end apart: 26 -> 26, of which waited for: 12 -> 13; matrix products, arithmetic and copies ran while one was open for 3% -> 4% of each run, Pallas kernels for 14% -> 14%
where the time goes in v6:
time: 89.7 us; the launch traced here: 89.5 us
  starting transfers between devices  50.9 us (57%)
  waiting for transfers between devices  20.4 us (23%)
  Pallas kernels  12.9 us (14%)
  other arithmetic  3.87 us (4%)
  between operations  1.47 us (2%)
    ppermute x26, starting transfers between devices, send(): return lax.ppermute(value, ('sec', 'dev'), pairs(move))  50.9 us
    ppermute x26, waiting for transfers between devices, send(): return lax.ppermute(value, ('sec', 'dev'), pairs(move))  20.4 us
    pallas_call x1, Pallas kernels, attend(): pl.pallas_call(attend_kernel, out_shape=jax.ShapeDtypeStruct((1, heads, L...  5.55 us
    pallas_call x2, Pallas kernels, experts(): pl.pallas_call(functools.partial(expert_kernel, count, rows), out_shape=(...  4.89 us
    concatenate x1, other arithmetic, local(): wide_own = jnp.concatenate([w_gate[0], w_up[0]], axis=1)  2.59 us
    pallas_call x1, Pallas kernels, pack(): pl.pallas_call(pack_kernel, out_shape=(PACKED,) * 4 + (jax.ShapeDtypeStru...  2.11 us
  transfers between devices with their start and end apart: 26, of which 13 were waited for; matrix products, arithmetic and copies ran while one was open for 4% of the time, Pallas kernels for 14%

profile of v6, /device:TPU:1, one launch (start us, length us, event | category | flops | bytes accessed | tf_op | source)
XLA Modules:
  0.0 89.5 jit_solution(8659088881936807085)
XLA Ops:
  0.6 3.3 %collective-permute-start.4 = (bf16[128,7168]{1,0:T(8,128)(2,1)}, bf16[128,7168]{1,0:T(8,128)(2,1)S(1)}, u32[]{:S(2)}, u32[]{:S(2)}) collective-permute-start(bf16[128,7168]{1,0:T(8,128)(2,1)} %bitcast.9), channel_id=1, source_target_pairs={{0,64},{1,65},{2,66},{3,67},{4,68},{5,69},{6,70},{7,71},{8,72},{9,... | collective-permute-start | bytes 5505032 | tf_op jit(solution)/shard_map/ppermute | solution.py:40
  4.0 2.1 %shard_map.113 = (bf16[40,896]{1,0:T(8,128)(2,1)}, bf16[40,896]{1,0:T(8,128)(2,1)}, bf16[40,896]{1,0:T(8,128)(2,1)}, bf16[40,896]{1,0:T(8,128)(2,1)}, f32[8,256]{1,0:T(8,128)}) custom-call(bf16[8,7168]{1,0:T(8,128)(2,1)} %refs_0_.1, f32[1,7168]{1,0:T(1,128)} %bitcast.12, s32[8,8]{1,0:T(8,128)} %refs_2_.1, f32[8,8]{1,0:T(8,128)} %refs_3_.1), custom_call_target="tpu_custom_call" | custom-call | tf_op jit(solution)/shard_map/pallas_call | solution.py:127
  6.1 4.8 %collective-permute-start = (bf16[40,896]{1,0:T(8,128)(2,1)}, bf16[40,896]{1,0:T(8,128)(2,1)S(1)}, u32[]{:S(2)}, u32[]{:S(2)}) collective-permute-start(bf16[40,896]{1,0:T(8,128)(2,1)} %get-tuple-element.35), channel_id=1, source_target_pairs={{0,12},{1,13},{2,14},{3,15},{4,16},{5,17},{6,18},{7,19},{8,20},{9,... | collective-permute-start | bytes 215048 | tf_op jit(solution)/shard_map/ppermute | solution.py:40
  10.9 0.5 collective-permute-start.1
  11.4 1.8 %collective-permute-start.2 = (bf16[40,896]{1,0:T(8,128)(2,1)}, bf16[40,896]{1,0:T(8,128)(2,1)S(1)}, u32[]{:S(2)}, u32[]{:S(2)}) collective-permute-start(bf16[40,896]{1,0:T(8,128)(2,1)} %get-tuple-element.37), channel_id=1, source_target_pairs={{0,4},{1,5},{2,6},{3,7},{4,8},{5,9},{6,10},{7,11},{8,12},{9,13},{1... | collective-permute-start | bytes 215048 | tf_op jit(solution)/shard_map/ppermute | solution.py:40
  13.2 3.2 %collective-permute-start.3 = (bf16[40,896]{1,0:T(8,128)(2,1)}, bf16[40,896]{1,0:T(8,128)(2,1)S(1)}, u32[]{:S(2)}, u32[]{:S(2)}) collective-permute-start(bf16[40,896]{1,0:T(8,128)(2,1)} %get-tuple-element.38), channel_id=1, source_target_pairs={{0,0},{1,1},{2,2},{3,3},{4,4},{5,5},{6,6},{7,7},{8,8},{9,9},{10,10... | collective-permute-start | bytes 215048 | tf_op jit(solution)/shard_map/ppermute | solution.py:40
  16.5 2.6 %pad_maximum_fusion.refs_5_.refs_3_ = bf16[7168,256]{1,0:T(8,128)(2,1)S(1)} fusion(bf16[7168,128]{1,0:T(8,128)(2,1)} %bitcast.7, bf16[7168,128]{1,0:T(8,128)(2,1)} %bitcast.8), kind=kLoop, calls=%fused_computation | loop fusion | flops 7340032 | bytes 7340032 | tf_op jit(solution)/shard_map/concatenate | solution.py:339
  19.1 0.4 collective-permute-done.2.c
  19.5 0.1 collective-permute-start.6
  19.6 3.6 %collective-permute-start.5 = (bf16[160,896]{1,0:T(8,128)(2,1)S(1)}, bf16[160,896]{1,0:T(8,128)(2,1)S(1)}, u32[]{:S(2)}, u32[]{:S(2)}) collective-permute-start(bf16[160,896]{1,0:T(8,128)(2,1)S(1)} %shard_map.114.refs_0_), channel_id=1, source_target_pairs={{0,128},{1,129},{2,130},{3,131},{4,132},{5,133},{6,134},{7,135},{8... | collective-permute-start | bytes 860168 | tf_op jit(solution)/shard_map/ppermute | solution.py:40
  23.2 2.9 %collective-permute-start.8 = (bf16[160,896]{1,0:T(8,128)(2,1)S(1)}, bf16[160,896]{1,0:T(8,128)(2,1)S(1)}, u32[]{:S(2)}, u32[]{:S(2)}) collective-permute-start(bf16[160,896]{1,0:T(8,128)(2,1)S(1)} %shard_map.114.refs_0_), channel_id=1, source_target_pairs={{0,2},{1,3},{2,0},{3,1},{4,6},{5,7},{6,4},{7,5},{8,10},{9,11},{10,... | collective-permute-start | bytes 860168 | tf_op jit(solution)/shard_map/ppermute | solution.py:40
  26.1 0.4 collective-permute-start.9
  26.5 2.3 %collective-permute-start.10 = (bf16[160,896]{1,0:T(8,128)(2,1)S(1)}, bf16[160,896]{1,0:T(8,128)(2,1)S(1)}, u32[]{:S(2)}, u32[]{:S(2)}) collective-permute-start(bf16[160,896]{1,0:T(8,128)(2,1)S(1)} %shard_map.114.refs_0_), channel_id=1, source_target_pairs={{0,3},{1,0},{2,1},{3,2},{4,7},{5,4},{6,5},{7,6},{8,11},{9,8},{10,9... | collective-permute-start | bytes 860168 | tf_op jit(solution)/shard_map/ppermute | solution.py:40
  28.8 0.2 pad_maximum_fusion.1.refs_7_.refs_5_
  29.0 1.0 %collective-permute-done.5.refs_1_ = bf16[160,896]{1,0:T(8,128)(2,1)S(1)} collective-permute-done((bf16[160,896]{1,0:T(8,128)(2,1)S(1)}, bf16[160,896]{1,0:T(8,128)(2,1)S(1)}, u32[]{:S(2)}, u32[]{:S(2)}) %collective-permute-start.5) | collective-permute-done | bytes 286752 | tf_op jit(solution)/shard_map/ppermute | solution.py:40
  30.1 1.3 %collective-permute-start.7 = (bf16[160,896]{1,0:T(8,128)(2,1)S(1)}, bf16[160,896]{1,0:T(8,128)(2,1)S(1)}, u32[]{:S(2)}, u32[]{:S(2)}) collective-permute-start(bf16[160,896]{1,0:T(8,128)(2,1)S(1)} %collective-permute-done.5.refs_1_), channel_id=1, source_target_pairs={{0,1},{1,2},{2,3},{3,0},{4,5},{5,6},{6,7},{7,4},{8,9},{9,10},{10,1... | collective-permute-start | bytes 860168 | tf_op jit(solution)/shard_map/ppermute | solution.py:40
  31.4 1.4 %collective-permute-start.13 = (bf16[160,896]{1,0:T(8,128)(2,1)S(1)}, bf16[160,896]{1,0:T(8,128)(2,1)S(1)}, u32[]{:S(2)}, u32[]{:S(2)}) collective-permute-start(bf16[160,896]{1,0:T(8,128)(2,1)S(1)} %collective-permute-done.5.refs_1_), channel_id=1, source_target_pairs={{0,3},{1,0},{2,1},{3,2},{4,7},{5,4},{6,5},{7,6},{8,11},{9,8},{10,9... | collective-permute-start | bytes 860168 | tf_op jit(solution)/shard_map/ppermute | solution.py:40
  32.8 1.1 %collective-permute-start.14 = (bf16[160,896]{1,0:T(8,128)(2,1)S(1)}, bf16[160,896]{1,0:T(8,128)(2,1)S(1)}, u32[]{:S(2)}, u32[]{:S(2)}) collective-permute-start(bf16[160,896]{1,0:T(8,128)(2,1)S(1)} %collective-permute-done.8.refs_2_), channel_id=1, source_target_pairs={{0,128},{1,129},{2,130},{3,131},{4,132},{5,133},{6,134},{7,135},{8... | collective-permute-start | bytes 860168 | tf_op jit(solution)/shard_map/ppermute | solution.py:40
  33.9 5.7 %collective-permute-done.9.refs_3_ = bf16[160,896]{1,0:T(8,128)(2,1)S(1)} collective-permute-done((bf16[160,896]{1,0:T(8,128)(2,1)S(1)}, bf16[160,896]{1,0:T(8,128)(2,1)S(1)}, u32[]{:S(2)}, u32[]{:S(2)}) %collective-permute-start.9) | collective-permute-done | bytes 286752 | tf_op jit(solution)/shard_map/ppermute | solution.py:40
  39.6 2.6 %shard_map.115 = (bf16[160,896]{1,0:T(8,128)(2,1)S(1)}, bf16[160,896]{1,0:T(8,128)(2,1)S(1)}, bf16[160,896]{1,0:T(8,128)(2,1)S(1)}, bf16[160,896]{1,0:T(8,128)(2,1)S(1)}, bf16[160,896]{1,0:T(8,128)(2,1)S(1)}) custom-call(bf16[160,896]{1,0:T(8,128)(2,1)S(1)} %shard_map.114.refs_0_, bf16[160,896]{1,0:T(8,128)(2,1)S(1)} %collective-permute-done.5.refs_1_, ...), custom_call_target="tpu_custom_call" | custom-call | flops 1233125376 | bytes 14221312 | tf_op jit(solution)/shard_map/pallas_call | solution.py:236
  42.2 1.6 %collective-permute-start.12 = (bf16[160,896]{1,0:T(8,128)(2,1)S(1)}, bf16[160,896]{1,0:T(8,128)(2,1)S(1)}, u32[]{:S(2)}, u32[]{:S(2)}) collective-permute-start(bf16[160,896]{1,0:T(8,128)(2,1)S(1)} %get-tuple-element.50), channel_id=1, source_target_pairs={{0,1},{1,2},{2,3},{3,0},{4,5},{5,6},{6,7},{7,4},{8,9},{9,10},{10,1... | collective-permute-start | bytes 860168 | tf_op jit(solution)/shard_map/ppermute | solution.py:40
  43.8 1.5 %collective-permute-start.11 = (bf16[160,896]{1,0:T(8,128)(2,1)S(1)}, bf16[160,896]{1,0:T(8,128)(2,1)S(1)}, u32[]{:S(2)}, u32[]{:S(2)}) collective-permute-start(bf16[160,896]{1,0:T(8,128)(2,1)S(1)} %get-tuple-element.49), channel_id=1, source_target_pairs={{0,3},{1,0},{2,1},{3,2},{4,7},{5,4},{6,5},{7,6},{8,11},{9,8},{10,9... | collective-permute-start | bytes 860168 | tf_op jit(solution)/shard_map/ppermute | solution.py:40
  45.3 0.4 collective-permute-done.7.refs_0_
  45.7 2.3 %shard_map.116 = (bf16[160,896]{1,0:T(8,128)(2,1)S(1)}, bf16[160,896]{1,0:T(8,128)(2,1)S(1)}, bf16[160,896]{1,0:T(8,128)(2,1)S(1)}) custom-call(bf16[160,896]{1,0:T(8,128)(2,1)S(1)} %collective-permute-done.7.refs_0_, bf16[160,896]{1,0:T(8,128)(2,1)S(1)} %collective-permute-done.13.refs_1_, bf16[160,896]{1,0:T(8,128)(2,1)S(1)} %collective-permute-done.14.refs_2_, ...), custom_call_target="tpu_custom_call" | custom-call | flops 704643072 | bytes 12845056 | tf_op jit(solution)/shard_map/pallas_call | solution.py:236
  48.0 0.2 collective-permute-start.16
  48.9 1.4 %collective-permute-start.17 = (bf16[160,896]{1,0:T(8,128)(2,1)S(1)}, bf16[160,896]{1,0:T(8,128)(2,1)S(1)}, u32[]{:S(2)}, u32[]{:S(2)}) collective-permute-start(bf16[160,896]{1,0:T(8,128)(2,1)S(1)} %get-tuple-element.57), channel_id=1, source_target_pairs={{0,1},{1,2},{2,3},{3,0},{4,5},{5,6},{6,7},{7,4},{8,9},{9,10},{10,1... | collective-permute-start | bytes 860168 | tf_op jit(solution)/shard_map/ppermute | solution.py:40
  50.2 1.5 %collective-permute-start.15 = (bf16[160,896]{1,0:T(8,128)(2,1)S(1)}, bf16[160,896]{1,0:T(8,128)(2,1)S(1)}, u32[]{:S(2)}, u32[]{:S(2)}) collective-permute-start(bf16[160,896]{1,0:T(8,128)(2,1)S(1)} %get-tuple-element.53), channel_id=1, source_target_pairs={{0,3},{1,0},{2,1},{3,2},{4,7},{5,4},{6,5},{7,6},{8,11},{9,8},{10,9... | collective-permute-start | bytes 860168 | tf_op jit(solution)/shard_map/ppermute | solution.py:40
  51.8 0.1 convert_add_fusion.1
  51.9 2.5 %collective-permute-done.16 = bf16[160,896]{1,0:T(8,128)(2,1)S(1)} collective-permute-done((bf16[160,896]{1,0:T(8,128)(2,1)S(1)}, bf16[160,896]{1,0:T(8,128)(2,1)S(1)}, u32[]{:S(2)}, u32[]{:S(2)}) %collective-permute-start.16) | collective-permute-done | bytes 286752 | tf_op jit(solution)/shard_map/ppermute | solution.py:40
  54.5 1.3 %collective-permute-start.18 = (bf16[160,896]{1,0:T(8,128)(2,1)S(1)}, bf16[160,896]{1,0:T(8,128)(2,1)S(1)}, u32[]{:S(2)}, u32[]{:S(2)}) collective-permute-start(bf16[160,896]{1,0:T(8,128)(2,1)S(1)} %add_convert_fusion.1), channel_id=1, source_target_pairs={{0,2},{1,3},{2,0},{3,1},{4,6},{5,7},{6,4},{7,5},{8,10},{9,11},{10,... | collective-permute-start | bytes 860168 | tf_op jit(solution)/shard_map/ppermute | solution.py:40
  55.8 0.9 collective-permute-done.15
  56.7 0.1 add_convert_fusion
  56.8 1.4 %collective-permute-start.19 = (bf16[160,896]{1,0:T(8,128)(2,1)S(1)}, bf16[160,896]{1,0:T(8,128)(2,1)S(1)}, u32[]{:S(2)}, u32[]{:S(2)}) collective-permute-start(bf16[160,896]{1,0:T(8,128)(2,1)S(1)} %add_convert_fusion), channel_id=1, source_target_pairs={{0,128},{1,129},{2,130},{3,131},{4,132},{5,133},{6,134},{7,135},{8... | collective-permute-start | bytes 860168 | tf_op jit(solution)/shard_map/ppermute | solution.py:40
  58.2 5.5 %shard_map.117 = bf16[1,128,512]{2,1,0:T(8,128)(2,1)} custom-call(s32[1]{0:T(128)S(6)} %copy.12.length_ref, bf16[1,576,128]{2,1,0:T(8,128)(2,1)} %bitcast.11, bf16[1,576,4096]{2,1,0:T(8,128)(2,1)} %bitcast.6), custom_call_target="tpu_custom_call" | custom-call | flops 1140850688 | bytes 4718592 | tf_op jit(solution)/shard_map/pallas_call | solution.py:299
  63.8 0.6 collective-permute-done.18
  64.5 4.5 %collective-permute-start.20 = (bf16[40,896]{1,0:T(8,128)(2,1)S(1)}, bf16[40,896]{1,0:T(8,128)(2,1)S(1)}, u32[]{:S(2)}, u32[]{:S(2)}) collective-permute-start(bf16[40,896]{1,0:T(8,128)(2,1)S(1)} %get-tuple-element.64), channel_id=1, source_target_pairs={{0,20},{1,21},{2,22},{3,23},{4,24},{5,25},{6,26},{7,27},{8,28},{9,... | collective-permute-start | bytes 215048 | tf_op jit(solution)/shard_map/ppermute | solution.py:40
  69.0 0.3 collective-permute-start.21
  69.3 3.2 %collective-permute-start.22 = (bf16[40,896]{1,0:T(8,128)(2,1)S(1)}, bf16[40,896]{1,0:T(8,128)(2,1)S(1)}, u32[]{:S(2)}, u32[]{:S(2)}) collective-permute-start(bf16[40,896]{1,0:T(8,128)(2,1)S(1)} %get-tuple-element.66), channel_id=1, source_target_pairs={{0,28},{1,29},{2,30},{3,31},{4,0},{5,1},{6,2},{7,3},{8,4},{9,5},{1... | collective-permute-start | bytes 215048 | tf_op jit(solution)/shard_map/ppermute | solution.py:40
  72.5 2.1 %collective-permute-start.23 = (bf16[40,896]{1,0:T(8,128)(2,1)S(1)}, bf16[40,896]{1,0:T(8,128)(2,1)S(1)}, u32[]{:S(2)}, u32[]{:S(2)}) collective-permute-start(bf16[40,896]{1,0:T(8,128)(2,1)S(1)} %get-tuple-element.67), channel_id=1, source_target_pairs={{0,0},{1,1},{2,2},{3,3},{4,4},{5,5},{6,6},{7,7},{8,8},{9,9},{10,10... | collective-permute-start | bytes 215048 | tf_op jit(solution)/shard_map/ppermute | solution.py:40
  74.6 2.3 %collective-permute-done.21.b = bf16[40,896]{1,0:T(8,128)(2,1)S(1)} collective-permute-done((bf16[40,896]{1,0:T(8,128)(2,1)S(1)}, bf16[40,896]{1,0:T(8,128)(2,1)S(1)}, u32[]{:S(2)}, u32[]{:S(2)}) %collective-permute-start.21) | collective-permute-done | bytes 71712 | tf_op jit(solution)/shard_map/ppermute | solution.py:40
  76.9 1.1 %collective-permute-done.22.c = bf16[40,896]{1,0:T(8,128)(2,1)S(1)} collective-permute-done((bf16[40,896]{1,0:T(8,128)(2,1)S(1)}, bf16[40,896]{1,0:T(8,128)(2,1)S(1)}, u32[]{:S(2)}, u32[]{:S(2)}) %collective-permute-start.22) | collective-permute-done | bytes 71712 | tf_op jit(solution)/shard_map/ppermute | solution.py:40
  78.1 0.7 collective-permute-done.23.d
  78.8 0.3 shard_map.119
  79.0 0.1 collective-permute-start.24
  79.1 1.3 %collective-permute-done.24 = bf16[8,7168]{1,0:T(8,128)(2,1)S(1)} collective-permute-done((bf16[8,7168]{1,0:T(8,128)(2,1)S(1)}, bf16[8,7168]{1,0:T(8,128)(2,1)S(1)}, u32[]{:S(2)}, u32[]{:S(2)}) %collective-permute-start.24) | collective-permute-done | bytes 114720 | tf_op jit(solution)/shard_map/ppermute | solution.py:40
  80.5 5.0 %collective-permute-start.25 = (bf16[8,7168]{1,0:T(8,128)(2,1)S(1)}, bf16[8,7168]{1,0:T(8,128)(2,1)S(1)}, u32[]{:S(2)}, u32[]{:S(2)}) collective-permute-start(bf16[8,7168]{1,0:T(8,128)(2,1)S(1)} %add_convert_fusion.3), channel_id=1, source_target_pairs={{0,128},{1,129},{2,130},{3,131},{4,132},{5,133},{6,134},{7,135},{8... | collective-permute-start | bytes 344072 | tf_op jit(solution)/shard_map/ppermute | solution.py:40
  85.5 3.4 %collective-permute-done.25 = bf16[8,7168]{1,0:T(8,128)(2,1)S(1)} collective-permute-done((bf16[8,7168]{1,0:T(8,128)(2,1)S(1)}, bf16[8,7168]{1,0:T(8,128)(2,1)S(1)}, u32[]{:S(2)}, u32[]{:S(2)}) %collective-permute-start.25) | collective-permute-done | bytes 114720 | tf_op jit(solution)/shard_map/ppermute | solution.py:40
  88.8 0.7 add_convert_fusion.2
  (25 shorter events, 0.3 us)
Async XLA Ops:
  0.6 18.8 %collective-permute-start.4 = (bf16[128,7168]{1,0:T(8,128)(2,1)}, bf16[128,7168]{1,0:T(8,128)(2,1)S(1)}, u32[]{:S(2)}, u32[]{:S(2)}) collective-permute-start(bf16[128,7168]{1,0:T(8,128)(2,1)} %bitcast.9), channel_id=1, source_target_pairs={{0,64},{1,65},{2,66},{3,67},{4,68},{5,69},{6,70},{7,71},{8,72},{9,... | collective-permute-start | bytes 5505032 | tf_op jit(solution)/shard_map/ppermute | solution.py:40
  6.1 13.0 %collective-permute-start = (bf16[40,896]{1,0:T(8,128)(2,1)}, bf16[40,896]{1,0:T(8,128)(2,1)S(1)}, u32[]{:S(2)}, u32[]{:S(2)}) collective-permute-start(bf16[40,896]{1,0:T(8,128)(2,1)} %get-tuple-element.35), channel_id=1, source_target_pairs={{0,12},{1,13},{2,14},{3,15},{4,16},{5,17},{6,18},{7,19},{8,20},{9,... | collective-permute-start | bytes 215048 | tf_op jit(solution)/shard_map/ppermute | solution.py:40
  10.9 8.2 %collective-permute-start.1 = (bf16[40,896]{1,0:T(8,128)(2,1)}, bf16[40,896]{1,0:T(8,128)(2,1)S(1)}, u32[]{:S(2)}, u32[]{:S(2)}) collective-permute-start(bf16[40,896]{1,0:T(8,128)(2,1)} %get-tuple-element.36), channel_id=1, source_target_pairs={{0,24},{1,25},{2,26},{3,27},{4,28},{5,29},{6,30},{7,31},{8,0},{9,1... | collective-permute-start | bytes 215048 | tf_op jit(solution)/shard_map/ppermute | solution.py:40
  11.4 8.0 %collective-permute-start.2 = (bf16[40,896]{1,0:T(8,128)(2,1)}, bf16[40,896]{1,0:T(8,128)(2,1)S(1)}, u32[]{:S(2)}, u32[]{:S(2)}) collective-permute-start(bf16[40,896]{1,0:T(8,128)(2,1)} %get-tuple-element.37), channel_id=1, source_target_pairs={{0,4},{1,5},{2,6},{3,7},{4,8},{5,9},{6,10},{7,11},{8,12},{9,13},{1... | collective-permute-start | bytes 215048 | tf_op jit(solution)/shard_map/ppermute | solution.py:40
  13.2 6.2 %collective-permute-start.3 = (bf16[40,896]{1,0:T(8,128)(2,1)}, bf16[40,896]{1,0:T(8,128)(2,1)S(1)}, u32[]{:S(2)}, u32[]{:S(2)}) collective-permute-start(bf16[40,896]{1,0:T(8,128)(2,1)} %get-tuple-element.38), channel_id=1, source_target_pairs={{0,0},{1,1},{2,2},{3,3},{4,4},{5,5},{6,6},{7,7},{8,8},{9,9},{10,10... | collective-permute-start | bytes 215048 | tf_op jit(solution)/shard_map/ppermute | solution.py:40
  16.4 12.3 %copy-start.1 = (bf16[1,128,7168]{2,1,0:T(8,128)(2,1)S(1)}, bf16[1,128,7168]{2,1,0:T(8,128)(2,1)}, u32[]{:S(2)}) copy-start(bf16[1,128,7168]{2,1,0:T(8,128)(2,1)} %param.19) | copy-start | bytes 5505028
  19.5 10.6 %collective-permute-start.6 = (bf16[7168,256]{1,0:T(8,128)(2,1)S(1)}, bf16[7168,256]{1,0:T(8,128)(2,1)S(1)}, u32[]{:S(2)}, u32[]{:S(2)}) collective-permute-start(bf16[7168,256]{1,0:T(8,128)(2,1)S(1)} %pad_maximum_fusion.refs_5_.refs_3_), channel_id=1, source_target_pairs={{0,64},{1,65},{2,66},{3,67},{4,68},{5,69},{6,70},{7,71},{8,72},{9,... | collective-permute-start | bytes 11010056 | tf_op jit(solution)/shard_map/ppermute | solution.py:40
  19.6 10.5 %collective-permute-start.5 = (bf16[160,896]{1,0:T(8,128)(2,1)S(1)}, bf16[160,896]{1,0:T(8,128)(2,1)S(1)}, u32[]{:S(2)}, u32[]{:S(2)}) collective-permute-start(bf16[160,896]{1,0:T(8,128)(2,1)S(1)} %shard_map.114.refs_0_), channel_id=1, source_target_pairs={{0,128},{1,129},{2,130},{3,131},{4,132},{5,133},{6,134},{7,135},{8... | collective-permute-start | bytes 860168 | tf_op jit(solution)/shard_map/ppermute | solution.py:40
  23.2 9.6 %collective-permute-start.8 = (bf16[160,896]{1,0:T(8,128)(2,1)S(1)}, bf16[160,896]{1,0:T(8,128)(2,1)S(1)}, u32[]{:S(2)}, u32[]{:S(2)}) collective-permute-start(bf16[160,896]{1,0:T(8,128)(2,1)S(1)} %shard_map.114.refs_0_), channel_id=1, source_target_pairs={{0,2},{1,3},{2,0},{3,1},{4,6},{5,7},{6,4},{7,5},{8,10},{9,11},{10,... | collective-permute-start | bytes 860168 | tf_op jit(solution)/shard_map/ppermute | solution.py:40
  26.1 13.5 %collective-permute-start.9 = (bf16[160,896]{1,0:T(8,128)(2,1)S(1)}, bf16[160,896]{1,0:T(8,128)(2,1)S(1)}, u32[]{:S(2)}, u32[]{:S(2)}) collective-permute-start(bf16[160,896]{1,0:T(8,128)(2,1)S(1)} %shard_map.114.refs_0_), channel_id=1, source_target_pairs={{0,1},{1,2},{2,3},{3,0},{4,5},{5,6},{6,7},{7,4},{8,9},{9,10},{10,1... | collective-permute-start | bytes 860168 | tf_op jit(solution)/shard_map/ppermute | solution.py:40
  26.5 13.1 %collective-permute-start.10 = (bf16[160,896]{1,0:T(8,128)(2,1)S(1)}, bf16[160,896]{1,0:T(8,128)(2,1)S(1)}, u32[]{:S(2)}, u32[]{:S(2)}) collective-permute-start(bf16[160,896]{1,0:T(8,128)(2,1)S(1)} %shard_map.114.refs_0_), channel_id=1, source_target_pairs={{0,3},{1,0},{2,1},{3,2},{4,7},{5,4},{6,5},{7,6},{8,11},{9,8},{10,9... | collective-permute-start | bytes 860168 | tf_op jit(solution)/shard_map/ppermute | solution.py:40
  30.1 15.7 %collective-permute-start.7 = (bf16[160,896]{1,0:T(8,128)(2,1)S(1)}, bf16[160,896]{1,0:T(8,128)(2,1)S(1)}, u32[]{:S(2)}, u32[]{:S(2)}) collective-permute-start(bf16[160,896]{1,0:T(8,128)(2,1)S(1)} %collective-permute-done.5.refs_1_), channel_id=1, source_target_pairs={{0,1},{1,2},{2,3},{3,0},{4,5},{5,6},{6,7},{7,4},{8,9},{9,10},{10,1... | collective-permute-start | bytes 860168 | tf_op jit(solution)/shard_map/ppermute | solution.py:40
  31.4 14.4 %collective-permute-start.13 = (bf16[160,896]{1,0:T(8,128)(2,1)S(1)}, bf16[160,896]{1,0:T(8,128)(2,1)S(1)}, u32[]{:S(2)}, u32[]{:S(2)}) collective-permute-start(bf16[160,896]{1,0:T(8,128)(2,1)S(1)} %collective-permute-done.5.refs_1_), channel_id=1, source_target_pairs={{0,3},{1,0},{2,1},{3,2},{4,7},{5,4},{6,5},{7,6},{8,11},{9,8},{10,9... | collective-permute-start | bytes 860168 | tf_op jit(solution)/shard_map/ppermute | solution.py:40
  32.8 12.9 %collective-permute-start.14 = (bf16[160,896]{1,0:T(8,128)(2,1)S(1)}, bf16[160,896]{1,0:T(8,128)(2,1)S(1)}, u32[]{:S(2)}, u32[]{:S(2)}) collective-permute-start(bf16[160,896]{1,0:T(8,128)(2,1)S(1)} %collective-permute-done.8.refs_2_), channel_id=1, source_target_pairs={{0,128},{1,129},{2,130},{3,131},{4,132},{5,133},{6,134},{7,135},{8... | collective-permute-start | bytes 860168 | tf_op jit(solution)/shard_map/ppermute | solution.py:40
  42.2 9.6 %collective-permute-start.12 = (bf16[160,896]{1,0:T(8,128)(2,1)S(1)}, bf16[160,896]{1,0:T(8,128)(2,1)S(1)}, u32[]{:S(2)}, u32[]{:S(2)}) collective-permute-start(bf16[160,896]{1,0:T(8,128)(2,1)S(1)} %get-tuple-element.50), channel_id=1, source_target_pairs={{0,1},{1,2},{2,3},{3,0},{4,5},{5,6},{6,7},{7,4},{8,9},{9,10},{10,1... | collective-permute-start | bytes 860168 | tf_op jit(solution)/shard_map/ppermute | solution.py:40
  43.8 8.0 %collective-permute-start.11 = (bf16[160,896]{1,0:T(8,128)(2,1)S(1)}, bf16[160,896]{1,0:T(8,128)(2,1)S(1)}, u32[]{:S(2)}, u32[]{:S(2)}) collective-permute-start(bf16[160,896]{1,0:T(8,128)(2,1)S(1)} %get-tuple-element.49), channel_id=1, source_target_pairs={{0,3},{1,0},{2,1},{3,2},{4,7},{5,4},{6,5},{7,6},{8,11},{9,8},{10,9... | collective-permute-start | bytes 860168 | tf_op jit(solution)/shard_map/ppermute | solution.py:40
  48.0 6.4 %collective-permute-start.16 = (bf16[160,896]{1,0:T(8,128)(2,1)S(1)}, bf16[160,896]{1,0:T(8,128)(2,1)S(1)}, u32[]{:S(2)}, u32[]{:S(2)}) collective-permute-start(bf16[160,896]{1,0:T(8,128)(2,1)S(1)} %get-tuple-element.55), channel_id=1, source_target_pairs={{0,128},{1,129},{2,130},{3,131},{4,132},{5,133},{6,134},{7,135},{8... | collective-permute-start | bytes 860168 | tf_op jit(solution)/shard_map/ppermute | solution.py:40
  48.9 7.8 %collective-permute-start.17 = (bf16[160,896]{1,0:T(8,128)(2,1)S(1)}, bf16[160,896]{1,0:T(8,128)(2,1)S(1)}, u32[]{:S(2)}, u32[]{:S(2)}) collective-permute-start(bf16[160,896]{1,0:T(8,128)(2,1)S(1)} %get-tuple-element.57), channel_id=1, source_target_pairs={{0,1},{1,2},{2,3},{3,0},{4,5},{5,6},{6,7},{7,4},{8,9},{9,10},{10,1... | collective-permute-start | bytes 860168 | tf_op jit(solution)/shard_map/ppermute | solution.py:40
  50.2 6.4 %collective-permute-start.15 = (bf16[160,896]{1,0:T(8,128)(2,1)S(1)}, bf16[160,896]{1,0:T(8,128)(2,1)S(1)}, u32[]{:S(2)}, u32[]{:S(2)}) collective-permute-start(bf16[160,896]{1,0:T(8,128)(2,1)S(1)} %get-tuple-element.53), channel_id=1, source_target_pairs={{0,3},{1,0},{2,1},{3,2},{4,7},{5,4},{6,5},{7,6},{8,11},{9,8},{10,9... | collective-permute-start | bytes 860168 | tf_op jit(solution)/shard_map/ppermute | solution.py:40
  54.5 9.9 %collective-permute-start.18 = (bf16[160,896]{1,0:T(8,128)(2,1)S(1)}, bf16[160,896]{1,0:T(8,128)(2,1)S(1)}, u32[]{:S(2)}, u32[]{:S(2)}) collective-permute-start(bf16[160,896]{1,0:T(8,128)(2,1)S(1)} %add_convert_fusion.1), channel_id=1, source_target_pairs={{0,2},{1,3},{2,0},{3,1},{4,6},{5,7},{6,4},{7,5},{8,10},{9,11},{10,... | collective-permute-start | bytes 860168 | tf_op jit(solution)/shard_map/ppermute | solution.py:40
  56.8 22.0 %copy-start = (f32[8,256]{1,0:T(8,128)S(1)}, f32[8,256]{1,0:T(8,128)}, u32[]{:S(2)}) copy-start(f32[8,256]{1,0:T(8,128)} %get-tuple-element.61.table_ref) | copy-start | bytes 24580
  56.8 7.6 %collective-permute-start.19 = (bf16[160,896]{1,0:T(8,128)(2,1)S(1)}, bf16[160,896]{1,0:T(8,128)(2,1)S(1)}, u32[]{:S(2)}, u32[]{:S(2)}) collective-permute-start(bf16[160,896]{1,0:T(8,128)(2,1)S(1)} %add_convert_fusion), channel_id=1, source_target_pairs={{0,128},{1,129},{2,130},{3,131},{4,132},{5,133},{6,134},{7,135},{8... | collective-permute-start | bytes 860168 | tf_op jit(solution)/shard_map/ppermute | solution.py:40
  58.2 30.6 %copy-start.2 = (bf16[8,7168]{1,0:T(8,128)(2,1)S(1)}, bf16[8,7168]{1,0:T(8,128)(2,1)}, u32[]{:S(2)}) copy-start(bf16[8,7168]{1,0:T(8,128)(2,1)} %refs_0_.1) | copy-start | bytes 344068
  64.5 10.1 %collective-permute-start.20 = (bf16[40,896]{1,0:T(8,128)(2,1)S(1)}, bf16[40,896]{1,0:T(8,128)(2,1)S(1)}, u32[]{:S(2)}, u32[]{:S(2)}) collective-permute-start(bf16[40,896]{1,0:T(8,128)(2,1)S(1)} %get-tuple-element.64), channel_id=1, source_target_pairs={{0,20},{1,21},{2,22},{3,23},{4,24},{5,25},{6,26},{7,27},{8,28},{9,... | collective-permute-start | bytes 215048 | tf_op jit(solution)/shard_map/ppermute | solution.py:40
  69.0 7.9 %collective-permute-start.21 = (bf16[40,896]{1,0:T(8,128)(2,1)S(1)}, bf16[40,896]{1,0:T(8,128)(2,1)S(1)}, u32[]{:S(2)}, u32[]{:S(2)}) collective-permute-start(bf16[40,896]{1,0:T(8,128)(2,1)S(1)} %get-tuple-element.65), channel_id=1, source_target_pairs={{0,8},{1,9},{2,10},{3,11},{4,12},{5,13},{6,14},{7,15},{8,16},{9,17... | collective-permute-start | bytes 215048 | tf_op jit(solution)/shard_map/ppermute | solution.py:40
  69.3 8.8 %collective-permute-start.22 = (bf16[40,896]{1,0:T(8,128)(2,1)S(1)}, bf16[40,896]{1,0:T(8,128)(2,1)S(1)}, u32[]{:S(2)}, u32[]{:S(2)}) collective-permute-start(bf16[40,896]{1,0:T(8,128)(2,1)S(1)} %get-tuple-element.66), channel_id=1, source_target_pairs={{0,28},{1,29},{2,30},{3,31},{4,0},{5,1},{6,2},{7,3},{8,4},{9,5},{1... | collective-permute-start | bytes 215048 | tf_op jit(solution)/shard_map/ppermute | solution.py:40
  72.5 6.3 %collective-permute-start.23 = (bf16[40,896]{1,0:T(8,128)(2,1)S(1)}, bf16[40,896]{1,0:T(8,128)(2,1)S(1)}, u32[]{:S(2)}, u32[]{:S(2)}) collective-permute-start(bf16[40,896]{1,0:T(8,128)(2,1)S(1)} %get-tuple-element.67), channel_id=1, source_target_pairs={{0,0},{1,1},{2,2},{3,3},{4,4},{5,5},{6,6},{7,7},{8,8},{9,9},{10,10... | collective-permute-start | bytes 215048 | tf_op jit(solution)/shard_map/ppermute | solution.py:40
  79.0 1.4 %collective-permute-start.24 = (bf16[8,7168]{1,0:T(8,128)(2,1)S(1)}, bf16[8,7168]{1,0:T(8,128)(2,1)S(1)}, u32[]{:S(2)}, u32[]{:S(2)}) collective-permute-start(bf16[8,7168]{1,0:T(8,128)(2,1)S(1)} %shard_map.119), channel_id=1, source_target_pairs={{0,64},{1,65},{2,66},{3,67},{4,68},{5,69},{6,70},{7,71},{8,72},{9,... | collective-permute-start | bytes 344072 | tf_op jit(solution)/shard_map/ppermute | solution.py:40
  80.5 8.4 %collective-permute-start.25 = (bf16[8,7168]{1,0:T(8,128)(2,1)S(1)}, bf16[8,7168]{1,0:T(8,128)(2,1)S(1)}, u32[]{:S(2)}, u32[]{:S(2)}) collective-permute-start(bf16[8,7168]{1,0:T(8,128)(2,1)S(1)} %add_convert_fusion.3), channel_id=1, source_target_pairs={{0,128},{1,129},{2,130},{3,131},{4,132},{5,133},{6,134},{7,135},{8... | collective-permute-start | bytes 344072 | tf_op jit(solution)/shard_map/ppermute | solution.py:40

commit v7 on v6

--- a/solution.py
+++ b/solution.py
@@ -277,7 +277,7 @@
             * score_scale
         )
         at = part * size + lax.broadcasted_iota(jnp.int32, scores.shape, 1)
-        scores = jnp.where(at < length_ref[0], scores, jnp.float32(-1e30))
+        scores = jnp.where(at < length_ref[0:1, 0:1], scores, jnp.float32(-1e30))
         new = jnp.maximum(peak, jnp.max(scores, axis=1, keepdims=True))
         powered = jnp.exp(scores - new)
         fade = jnp.exp(peak - new)
@@ -300,7 +300,7 @@
         attend_kernel,
         out_shape=jax.ShapeDtypeStruct((1, heads, LATENT), jnp.bfloat16),
         in_specs=[
-            pl.BlockSpec(memory_space=pltpu.SMEM),
+            VMEM,
             pl.BlockSpec(memory_space=pltpu.HBM),
             pl.BlockSpec(memory_space=pltpu.HBM),
         ],
@@ -338,8 +338,9 @@
 
     wide_own = jnp.concatenate([w_gate[0], w_up[0]], axis=1)
     mine = join(arrived)
-    mine, down_own, down_other, wide_own = lax.optimization_barrier(
-        (mine, down_own, down_other, wide_own)
+    cache_lengths = jnp.broadcast_to(cache_lengths[:, None], (8, 128))
+    mine, down_own, down_other, wide_own, cache_lengths = lax.optimization_barrier(
+        (mine, down_own, down_other, wide_own, cache_lengths)
     )
     wide_other = swap_core(wide_own)
     down = jnp.concatenate([down_own, down_other], axis=0)

time: 89.7 us -> 89.4 us (level)
  starting transfers between devices: 50.9 us -> 49 us
    ppermute x26, starting transfers between devices: 50.9 us -> 49 us  [send(): return lax.ppermute(value, ('sec', 'dev'), pairs(move))]
  transfers between devices with their start and end apart: 26 -> 26, of which waited for: 13 -> 10; matrix products, arithmetic and copies ran while one was open for 4% -> 4% of each run, Pallas kernels for 14% -> 15%
where the time goes in v7:
time: 89.4 us; the launch traced here: 89.1 us
  starting transfers between devices  49 us (55%)
  waiting for transfers between devices  20.5 us (23%)
  Pallas kernels  13.6 us (15%)
  other arithmetic  3.87 us (4%)
  between operations  1.49 us (2%)
    ppermute x26, starting transfers between devices, send(): return lax.ppermute(value, ('sec', 'dev'), pairs(move))  49 us
    ppermute x26, waiting for transfers between devices, send(): return lax.ppermute(value, ('sec', 'dev'), pairs(move))  20.5 us
    pallas_call x1, Pallas kernels, attend(): pl.pallas_call(attend_kernel, out_shape=jax.ShapeDtypeStruct((1, heads, L...  6.3 us
    pallas_call x2, Pallas kernels, experts(): pl.pallas_call(functools.partial(expert_kernel, count, rows), out_shape=(...  4.89 us
    concatenate x1, other arithmetic, local(): wide_own = jnp.concatenate([w_gate[0], w_up[0]], axis=1)  2.59 us
    pallas_call x1, Pallas kernels, pack(): pl.pallas_call(pack_kernel, out_shape=(PACKED,) * 4 + (jax.ShapeDtypeStru...  2.11 us
  transfers between devices with their start and end apart: 26, of which 10 were waited for; matrix products, arithmetic and copies ran while one was open for 4% of the time, Pallas kernels for 15%

profile of v7, /device:TPU:1, one launch (start us, length us, event | category | flops | bytes accessed | tf_op | source)
XLA Modules:
  0.0 89.1 jit_solution(17556419258084060332)
XLA Ops:
  0.6 3.3 %collective-permute-start.4 = (bf16[128,7168]{1,0:T(8,128)(2,1)}, bf16[128,7168]{1,0:T(8,128)(2,1)S(1)}, u32[]{:S(2)}, u32[]{:S(2)}) collective-permute-start(bf16[128,7168]{1,0:T(8,128)(2,1)} %bitcast.11), channel_id=1, source_target_pairs={{0,64},{1,65},{2,66},{3,67},{4,68},{5,69},{6,70},{7,71},{8,72},{9,... | collective-permute-start | bytes 5505032 | tf_op jit(solution)/shard_map/ppermute | solution.py:40
  4.0 2.1 %shard_map.113 = (bf16[40,896]{1,0:T(8,128)(2,1)}, bf16[40,896]{1,0:T(8,128)(2,1)}, bf16[40,896]{1,0:T(8,128)(2,1)}, bf16[40,896]{1,0:T(8,128)(2,1)}, f32[8,256]{1,0:T(8,128)}) custom-call(bf16[8,7168]{1,0:T(8,128)(2,1)} %refs_0_.1, f32[1,7168]{1,0:T(1,128)} %bitcast.14, s32[8,8]{1,0:T(8,128)} %refs_2_.1, f32[8,8]{1,0:T(8,128)} %refs_3_.1), custom_call_target="tpu_custom_call" | custom-call | tf_op jit(solution)/shard_map/pallas_call | solution.py:127
  6.1 4.8 %collective-permute-start = (bf16[40,896]{1,0:T(8,128)(2,1)}, bf16[40,896]{1,0:T(8,128)(2,1)S(1)}, u32[]{:S(2)}, u32[]{:S(2)}) collective-permute-start(bf16[40,896]{1,0:T(8,128)(2,1)} %get-tuple-element.36), channel_id=1, source_target_pairs={{0,12},{1,13},{2,14},{3,15},{4,16},{5,17},{6,18},{7,19},{8,20},{9,... | collective-permute-start | bytes 215048 | tf_op jit(solution)/shard_map/ppermute | solution.py:40
  10.9 0.5 collective-permute-start.1
  11.4 1.8 %collective-permute-start.2 = (bf16[40,896]{1,0:T(8,128)(2,1)}, bf16[40,896]{1,0:T(8,128)(2,1)S(1)}, u32[]{:S(2)}, u32[]{:S(2)}) collective-permute-start(bf16[40,896]{1,0:T(8,128)(2,1)} %get-tuple-element.38), channel_id=1, source_target_pairs={{0,4},{1,5},{2,6},{3,7},{4,8},{5,9},{6,10},{7,11},{8,12},{9,13},{1... | collective-permute-start | bytes 215048 | tf_op jit(solution)/shard_map/ppermute | solution.py:40
  13.2 3.2 %collective-permute-start.3 = (bf16[40,896]{1,0:T(8,128)(2,1)}, bf16[40,896]{1,0:T(8,128)(2,1)S(1)}, u32[]{:S(2)}, u32[]{:S(2)}) collective-permute-start(bf16[40,896]{1,0:T(8,128)(2,1)} %get-tuple-element.39), channel_id=1, source_target_pairs={{0,0},{1,1},{2,2},{3,3},{4,4},{5,5},{6,6},{7,7},{8,8},{9,9},{10,10... | collective-permute-start | bytes 215048 | tf_op jit(solution)/shard_map/ppermute | solution.py:40
  16.5 2.6 %pad_maximum_fusion.refs_5_.refs_3_ = bf16[7168,256]{1,0:T(8,128)(2,1)S(1)} fusion(bf16[7168,128]{1,0:T(8,128)(2,1)} %bitcast.9, bf16[7168,128]{1,0:T(8,128)(2,1)} %bitcast.10), kind=kLoop, calls=%fused_computation | loop fusion | flops 7340032 | bytes 7340032 | tf_op jit(solution)/shard_map/concatenate | solution.py:339
  19.8 0.6 broadcast_in_dim.13.length_ref
  20.4 3.2 %collective-permute-start.5 = (bf16[160,896]{1,0:T(8,128)(2,1)S(1)}, bf16[160,896]{1,0:T(8,128)(2,1)S(1)}, u32[]{:S(2)}, u32[]{:S(2)}) collective-permute-start(bf16[160,896]{1,0:T(8,128)(2,1)S(1)} %shard_map.114.refs_0_), channel_id=1, source_target_pairs={{0,128},{1,129},{2,130},{3,131},{4,132},{5,133},{6,134},{7,135},{8... | collective-permute-start | bytes 860168 | tf_op jit(solution)/shard_map/ppermute | solution.py:40
  23.6 2.9 %collective-permute-start.8 = (bf16[160,896]{1,0:T(8,128)(2,1)S(1)}, bf16[160,896]{1,0:T(8,128)(2,1)S(1)}, u32[]{:S(2)}, u32[]{:S(2)}) collective-permute-start(bf16[160,896]{1,0:T(8,128)(2,1)S(1)} %shard_map.114.refs_0_), channel_id=1, source_target_pairs={{0,2},{1,3},{2,0},{3,1},{4,6},{5,7},{6,4},{7,5},{8,10},{9,11},{10,... | collective-permute-start | bytes 860168 | tf_op jit(solution)/shard_map/ppermute | solution.py:40
  26.5 0.4 collective-permute-start.9
  26.9 2.3 %collective-permute-start.10 = (bf16[160,896]{1,0:T(8,128)(2,1)S(1)}, bf16[160,896]{1,0:T(8,128)(2,1)S(1)}, u32[]{:S(2)}, u32[]{:S(2)}) collective-permute-start(bf16[160,896]{1,0:T(8,128)(2,1)S(1)} %shard_map.114.refs_0_), channel_id=1, source_target_pairs={{0,3},{1,0},{2,1},{3,2},{4,7},{5,4},{6,5},{7,6},{8,11},{9,8},{10,9... | collective-permute-start | bytes 860168 | tf_op jit(solution)/shard_map/ppermute | solution.py:40
  29.2 0.2 pad_maximum_fusion.1.refs_7_.refs_5_
  29.4 0.9 %collective-permute-done.5.refs_1_ = bf16[160,896]{1,0:T(8,128)(2,1)S(1)} collective-permute-done((bf16[160,896]{1,0:T(8,128)(2,1)S(1)}, bf16[160,896]{1,0:T(8,128)(2,1)S(1)}, u32[]{:S(2)}, u32[]{:S(2)}) %collective-permute-start.5) | collective-permute-done | bytes 286752 | tf_op jit(solution)/shard_map/ppermute | solution.py:40
  30.4 1.3 %collective-permute-start.7 = (bf16[160,896]{1,0:T(8,128)(2,1)S(1)}, bf16[160,896]{1,0:T(8,128)(2,1)S(1)}, u32[]{:S(2)}, u32[]{:S(2)}) collective-permute-start(bf16[160,896]{1,0:T(8,128)(2,1)S(1)} %collective-permute-done.5.refs_1_), channel_id=1, source_target_pairs={{0,1},{1,2},{2,3},{3,0},{4,5},{5,6},{6,7},{7,4},{8,9},{9,10},{10,1... | collective-permute-start | bytes 860168 | tf_op jit(solution)/shard_map/ppermute | solution.py:40
  31.6 1.4 %collective-permute-start.13 = (bf16[160,896]{1,0:T(8,128)(2,1)S(1)}, bf16[160,896]{1,0:T(8,128)(2,1)S(1)}, u32[]{:S(2)}, u32[]{:S(2)}) collective-permute-start(bf16[160,896]{1,0:T(8,128)(2,1)S(1)} %collective-permute-done.5.refs_1_), channel_id=1, source_target_pairs={{0,3},{1,0},{2,1},{3,2},{4,7},{5,4},{6,5},{7,6},{8,11},{9,8},{10,9... | collective-permute-start | bytes 860168 | tf_op jit(solution)/shard_map/ppermute | solution.py:40
  33.1 1.1 %collective-permute-start.14 = (bf16[160,896]{1,0:T(8,128)(2,1)S(1)}, bf16[160,896]{1,0:T(8,128)(2,1)S(1)}, u32[]{:S(2)}, u32[]{:S(2)}) collective-permute-start(bf16[160,896]{1,0:T(8,128)(2,1)S(1)} %collective-permute-done.8.refs_2_), channel_id=1, source_target_pairs={{0,128},{1,129},{2,130},{3,131},{4,132},{5,133},{6,134},{7,135},{8... | collective-permute-start | bytes 860168 | tf_op jit(solution)/shard_map/ppermute | solution.py:40
  34.2 5.8 %collective-permute-done.9.refs_3_ = bf16[160,896]{1,0:T(8,128)(2,1)S(1)} collective-permute-done((bf16[160,896]{1,0:T(8,128)(2,1)S(1)}, bf16[160,896]{1,0:T(8,128)(2,1)S(1)}, u32[]{:S(2)}, u32[]{:S(2)}) %collective-permute-start.9) | collective-permute-done | bytes 286752 | tf_op jit(solution)/shard_map/ppermute | solution.py:40
  40.0 2.6 %shard_map.115 = (bf16[160,896]{1,0:T(8,128)(2,1)S(1)}, bf16[160,896]{1,0:T(8,128)(2,1)S(1)}, bf16[160,896]{1,0:T(8,128)(2,1)S(1)}, bf16[160,896]{1,0:T(8,128)(2,1)S(1)}, bf16[160,896]{1,0:T(8,128)(2,1)S(1)}) custom-call(bf16[160,896]{1,0:T(8,128)(2,1)S(1)} %shard_map.114.refs_0_, bf16[160,896]{1,0:T(8,128)(2,1)S(1)} %collective-permute-done.5.refs_1_, ...), custom_call_target="tpu_custom_call" | custom-call | flops 1233125376 | bytes 14221312 | tf_op jit(solution)/shard_map/pallas_call | solution.py:236
  42.6 1.6 %collective-permute-start.12 = (bf16[160,896]{1,0:T(8,128)(2,1)S(1)}, bf16[160,896]{1,0:T(8,128)(2,1)S(1)}, u32[]{:S(2)}, u32[]{:S(2)}) collective-permute-start(bf16[160,896]{1,0:T(8,128)(2,1)S(1)} %get-tuple-element.51), channel_id=1, source_target_pairs={{0,1},{1,2},{2,3},{3,0},{4,5},{5,6},{6,7},{7,4},{8,9},{9,10},{10,1... | collective-permute-start | bytes 860168 | tf_op jit(solution)/shard_map/ppermute | solution.py:40
  44.2 1.5 %collective-permute-start.11 = (bf16[160,896]{1,0:T(8,128)(2,1)S(1)}, bf16[160,896]{1,0:T(8,128)(2,1)S(1)}, u32[]{:S(2)}, u32[]{:S(2)}) collective-permute-start(bf16[160,896]{1,0:T(8,128)(2,1)S(1)} %get-tuple-element.50), channel_id=1, source_target_pairs={{0,3},{1,0},{2,1},{3,2},{4,7},{5,4},{6,5},{7,6},{8,11},{9,8},{10,9... | collective-permute-start | bytes 860168 | tf_op jit(solution)/shard_map/ppermute | solution.py:40
  45.7 0.4 collective-permute-done.7.refs_0_
  46.2 2.3 %shard_map.116 = (bf16[160,896]{1,0:T(8,128)(2,1)S(1)}, bf16[160,896]{1,0:T(8,128)(2,1)S(1)}, bf16[160,896]{1,0:T(8,128)(2,1)S(1)}) custom-call(bf16[160,896]{1,0:T(8,128)(2,1)S(1)} %collective-permute-done.7.refs_0_, bf16[160,896]{1,0:T(8,128)(2,1)S(1)} %collective-permute-done.13.refs_1_, bf16[160,896]{1,0:T(8,128)(2,1)S(1)} %collective-permute-done.14.refs_2_, ...), custom_call_target="tpu_custom_call" | custom-call | flops 704643072 | bytes 12845056 | tf_op jit(solution)/shard_map/pallas_call | solution.py:236
  48.4 0.1 collective-permute-start.16
  48.5 1.4 %collective-permute-start.17 = (bf16[160,896]{1,0:T(8,128)(2,1)S(1)}, bf16[160,896]{1,0:T(8,128)(2,1)S(1)}, u32[]{:S(2)}, u32[]{:S(2)}) collective-permute-start(bf16[160,896]{1,0:T(8,128)(2,1)S(1)} %get-tuple-element.58), channel_id=1, source_target_pairs={{0,1},{1,2},{2,3},{3,0},{4,5},{5,6},{6,7},{7,4},{8,9},{9,10},{10,1... | collective-permute-start | bytes 860168 | tf_op jit(solution)/shard_map/ppermute | solution.py:40
  49.9 1.5 %collective-permute-start.15 = (bf16[160,896]{1,0:T(8,128)(2,1)S(1)}, bf16[160,896]{1,0:T(8,128)(2,1)S(1)}, u32[]{:S(2)}, u32[]{:S(2)}) collective-permute-start(bf16[160,896]{1,0:T(8,128)(2,1)S(1)} %get-tuple-element.54), channel_id=1, source_target_pairs={{0,3},{1,0},{2,1},{3,2},{4,7},{5,4},{6,5},{7,6},{8,11},{9,8},{10,9... | collective-permute-start | bytes 860168 | tf_op jit(solution)/shard_map/ppermute | solution.py:40
  51.5 0.1 convert_add_fusion.1
  51.6 3.2 %collective-permute-done.16 = bf16[160,896]{1,0:T(8,128)(2,1)S(1)} collective-permute-done((bf16[160,896]{1,0:T(8,128)(2,1)S(1)}, bf16[160,896]{1,0:T(8,128)(2,1)S(1)}, u32[]{:S(2)}, u32[]{:S(2)}) %collective-permute-start.16) | collective-permute-done | bytes 286752 | tf_op jit(solution)/shard_map/ppermute | solution.py:40
  54.7 0.1 add_convert_fusion.1
  54.8 1.3 %collective-permute-start.18 = (bf16[160,896]{1,0:T(8,128)(2,1)S(1)}, bf16[160,896]{1,0:T(8,128)(2,1)S(1)}, u32[]{:S(2)}, u32[]{:S(2)}) collective-permute-start(bf16[160,896]{1,0:T(8,128)(2,1)S(1)} %add_convert_fusion.1), channel_id=1, source_target_pairs={{0,2},{1,3},{2,0},{3,1},{4,6},{5,7},{6,4},{7,5},{8,10},{9,11},{10,... | collective-permute-start | bytes 860168 | tf_op jit(solution)/shard_map/ppermute | solution.py:40
  56.1 1.1 %collective-permute-done.15 = bf16[160,896]{1,0:T(8,128)(2,1)S(1)} collective-permute-done((bf16[160,896]{1,0:T(8,128)(2,1)S(1)}, bf16[160,896]{1,0:T(8,128)(2,1)S(1)}, u32[]{:S(2)}, u32[]{:S(2)}) %collective-permute-start.15) | collective-permute-done | bytes 286752 | tf_op jit(solution)/shard_map/ppermute | solution.py:40
  57.2 0.1 add_convert_fusion
  57.3 0.6 collective-permute-start.19
  57.9 6.3 %shard_map.117 = bf16[1,128,512]{2,1,0:T(8,128)(2,1)} custom-call(s32[8,128]{1,0:T(8,128)} %broadcast_in_dim.13.length_ref, bf16[1,576,128]{2,1,0:T(8,128)(2,1)} %bitcast.13, bf16[1,576,4096]{2,1,0:T(8,128)(2,1)} %bitcast.8), custom_call_target="tpu_custom_call" | custom-call | flops 1140850688 | bytes 4718592 | tf_op jit(solution)/shard_map/pallas_call | solution.py:299
  64.3 0.1 shard_map.118
  64.3 4.5 %collective-permute-start.20 = (bf16[40,896]{1,0:T(8,128)(2,1)S(1)}, bf16[40,896]{1,0:T(8,128)(2,1)S(1)}, u32[]{:S(2)}, u32[]{:S(2)}) collective-permute-start(bf16[40,896]{1,0:T(8,128)(2,1)S(1)} %get-tuple-element.66), channel_id=1, source_target_pairs={{0,20},{1,21},{2,22},{3,23},{4,24},{5,25},{6,26},{7,27},{8,28},{9,... | collective-permute-start | bytes 215048 | tf_op jit(solution)/shard_map/ppermute | solution.py:40
  68.9 0.3 collective-permute-start.21
  69.1 3.6 %collective-permute-start.22 = (bf16[40,896]{1,0:T(8,128)(2,1)S(1)}, bf16[40,896]{1,0:T(8,128)(2,1)S(1)}, u32[]{:S(2)}, u32[]{:S(2)}) collective-permute-start(bf16[40,896]{1,0:T(8,128)(2,1)S(1)} %get-tuple-element.68), channel_id=1, source_target_pairs={{0,28},{1,29},{2,30},{3,31},{4,0},{5,1},{6,2},{7,3},{8,4},{9,5},{1... | collective-permute-start | bytes 215048 | tf_op jit(solution)/shard_map/ppermute | solution.py:40
  72.7 1.9 %collective-permute-start.23 = (bf16[40,896]{1,0:T(8,128)(2,1)S(1)}, bf16[40,896]{1,0:T(8,128)(2,1)S(1)}, u32[]{:S(2)}, u32[]{:S(2)}) collective-permute-start(bf16[40,896]{1,0:T(8,128)(2,1)S(1)} %get-tuple-element.69), channel_id=1, source_target_pairs={{0,0},{1,1},{2,2},{3,3},{4,4},{5,5},{6,6},{7,7},{8,8},{9,9},{10,10... | collective-permute-start | bytes 215048 | tf_op jit(solution)/shard_map/ppermute | solution.py:40
  74.7 2.1 %collective-permute-done.21.b = bf16[40,896]{1,0:T(8,128)(2,1)S(1)} collective-permute-done((bf16[40,896]{1,0:T(8,128)(2,1)S(1)}, bf16[40,896]{1,0:T(8,128)(2,1)S(1)}, u32[]{:S(2)}, u32[]{:S(2)}) %collective-permute-start.21) | collective-permute-done | bytes 71712 | tf_op jit(solution)/shard_map/ppermute | solution.py:40
  76.7 0.4 collective-permute-done.22.c
  77.2 2.0 %collective-permute-done.23.d = bf16[40,896]{1,0:T(8,128)(2,1)S(1)} collective-permute-done((bf16[40,896]{1,0:T(8,128)(2,1)S(1)}, bf16[40,896]{1,0:T(8,128)(2,1)S(1)}, u32[]{:S(2)}, u32[]{:S(2)}) %collective-permute-start.23) | collective-permute-done | bytes 71712 | tf_op jit(solution)/shard_map/ppermute | solution.py:40
  79.1 0.3 shard_map.119
  79.4 0.2 collective-permute-start.24
  79.6 1.2 %collective-permute-done.24 = bf16[8,7168]{1,0:T(8,128)(2,1)S(1)} collective-permute-done((bf16[8,7168]{1,0:T(8,128)(2,1)S(1)}, bf16[8,7168]{1,0:T(8,128)(2,1)S(1)}, u32[]{:S(2)}, u32[]{:S(2)}) %collective-permute-start.24) | collective-permute-done | bytes 114720 | tf_op jit(solution)/shard_map/ppermute | solution.py:40
  80.8 4.2 %collective-permute-start.25 = (bf16[8,7168]{1,0:T(8,128)(2,1)S(1)}, bf16[8,7168]{1,0:T(8,128)(2,1)S(1)}, u32[]{:S(2)}, u32[]{:S(2)}) collective-permute-start(bf16[8,7168]{1,0:T(8,128)(2,1)S(1)} %add_convert_fusion.3), channel_id=1, source_target_pairs={{0,128},{1,129},{2,130},{3,131},{4,132},{5,133},{6,134},{7,135},{8... | collective-permute-start | bytes 344072 | tf_op jit(solution)/shard_map/ppermute | solution.py:40
  85.0 3.4 %collective-permute-done.25 = bf16[8,7168]{1,0:T(8,128)(2,1)S(1)} collective-permute-done((bf16[8,7168]{1,0:T(8,128)(2,1)S(1)}, bf16[8,7168]{1,0:T(8,128)(2,1)S(1)}, u32[]{:S(2)}, u32[]{:S(2)}) %collective-permute-start.25) | collective-permute-done | bytes 114720 | tf_op jit(solution)/shard_map/ppermute | solution.py:40
  88.4 0.7 add_convert_fusion.2
  (26 shorter events, 0.2 us)
Async XLA Ops:
  0.6 19.1 %collective-permute-start.4 = (bf16[128,7168]{1,0:T(8,128)(2,1)}, bf16[128,7168]{1,0:T(8,128)(2,1)S(1)}, u32[]{:S(2)}, u32[]{:S(2)}) collective-permute-start(bf16[128,7168]{1,0:T(8,128)(2,1)} %bitcast.11), channel_id=1, source_target_pairs={{0,64},{1,65},{2,66},{3,67},{4,68},{5,69},{6,70},{7,71},{8,72},{9,... | collective-permute-start | bytes 5505032 | tf_op jit(solution)/shard_map/ppermute | solution.py:40
  6.1 13.6 %collective-permute-start = (bf16[40,896]{1,0:T(8,128)(2,1)}, bf16[40,896]{1,0:T(8,128)(2,1)S(1)}, u32[]{:S(2)}, u32[]{:S(2)}) collective-permute-start(bf16[40,896]{1,0:T(8,128)(2,1)} %get-tuple-element.36), channel_id=1, source_target_pairs={{0,12},{1,13},{2,14},{3,15},{4,16},{5,17},{6,18},{7,19},{8,20},{9,... | collective-permute-start | bytes 215048 | tf_op jit(solution)/shard_map/ppermute | solution.py:40
  10.9 8.8 %collective-permute-start.1 = (bf16[40,896]{1,0:T(8,128)(2,1)}, bf16[40,896]{1,0:T(8,128)(2,1)S(1)}, u32[]{:S(2)}, u32[]{:S(2)}) collective-permute-start(bf16[40,896]{1,0:T(8,128)(2,1)} %get-tuple-element.37), channel_id=1, source_target_pairs={{0,24},{1,25},{2,26},{3,27},{4,28},{5,29},{6,30},{7,31},{8,0},{9,1... | collective-permute-start | bytes 215048 | tf_op jit(solution)/shard_map/ppermute | solution.py:40
  11.4 8.3 %collective-permute-start.2 = (bf16[40,896]{1,0:T(8,128)(2,1)}, bf16[40,896]{1,0:T(8,128)(2,1)S(1)}, u32[]{:S(2)}, u32[]{:S(2)}) collective-permute-start(bf16[40,896]{1,0:T(8,128)(2,1)} %get-tuple-element.38), channel_id=1, source_target_pairs={{0,4},{1,5},{2,6},{3,7},{4,8},{5,9},{6,10},{7,11},{8,12},{9,13},{1... | collective-permute-start | bytes 215048 | tf_op jit(solution)/shard_map/ppermute | solution.py:40
  13.2 6.5 %collective-permute-start.3 = (bf16[40,896]{1,0:T(8,128)(2,1)}, bf16[40,896]{1,0:T(8,128)(2,1)S(1)}, u32[]{:S(2)}, u32[]{:S(2)}) collective-permute-start(bf16[40,896]{1,0:T(8,128)(2,1)} %get-tuple-element.39), channel_id=1, source_target_pairs={{0,0},{1,1},{2,2},{3,3},{4,4},{5,5},{6,6},{7,7},{8,8},{9,9},{10,10... | collective-permute-start | bytes 215048 | tf_op jit(solution)/shard_map/ppermute | solution.py:40
  16.4 12.8 %copy-start.1 = (bf16[1,128,7168]{2,1,0:T(8,128)(2,1)S(1)}, bf16[1,128,7168]{2,1,0:T(8,128)(2,1)}, u32[]{:S(2)}) copy-start(bf16[1,128,7168]{2,1,0:T(8,128)(2,1)} %param.19) | copy-start | bytes 5505028
  20.4 10.0 %collective-permute-start.6 = (bf16[7168,256]{1,0:T(8,128)(2,1)S(1)}, bf16[7168,256]{1,0:T(8,128)(2,1)S(1)}, u32[]{:S(2)}, u32[]{:S(2)}) collective-permute-start(bf16[7168,256]{1,0:T(8,128)(2,1)S(1)} %pad_maximum_fusion.refs_5_.refs_3_), channel_id=1, source_target_pairs={{0,64},{1,65},{2,66},{3,67},{4,68},{5,69},{6,70},{7,71},{8,72},{9,... | collective-permute-start | bytes 11010056 | tf_op jit(solution)/shard_map/ppermute | solution.py:40
  20.4 10.0 %collective-permute-start.5 = (bf16[160,896]{1,0:T(8,128)(2,1)S(1)}, bf16[160,896]{1,0:T(8,128)(2,1)S(1)}, u32[]{:S(2)}, u32[]{:S(2)}) collective-permute-start(bf16[160,896]{1,0:T(8,128)(2,1)S(1)} %shard_map.114.refs_0_), channel_id=1, source_target_pairs={{0,128},{1,129},{2,130},{3,131},{4,132},{5,133},{6,134},{7,135},{8... | collective-permute-start | bytes 860168 | tf_op jit(solution)/shard_map/ppermute | solution.py:40
  23.6 9.5 %collective-permute-start.8 = (bf16[160,896]{1,0:T(8,128)(2,1)S(1)}, bf16[160,896]{1,0:T(8,128)(2,1)S(1)}, u32[]{:S(2)}, u32[]{:S(2)}) collective-permute-start(bf16[160,896]{1,0:T(8,128)(2,1)S(1)} %shard_map.114.refs_0_), channel_id=1, source_target_pairs={{0,2},{1,3},{2,0},{3,1},{4,6},{5,7},{6,4},{7,5},{8,10},{9,11},{10,... | collective-permute-start | bytes 860168 | tf_op jit(solution)/shard_map/ppermute | solution.py:40
  26.5 13.5 %collective-permute-start.9 = (bf16[160,896]{1,0:T(8,128)(2,1)S(1)}, bf16[160,896]{1,0:T(8,128)(2,1)S(1)}, u32[]{:S(2)}, u32[]{:S(2)}) collective-permute-start(bf16[160,896]{1,0:T(8,128)(2,1)S(1)} %shard_map.114.refs_0_), channel_id=1, source_target_pairs={{0,1},{1,2},{2,3},{3,0},{4,5},{5,6},{6,7},{7,4},{8,9},{9,10},{10,1... | collective-permute-start | bytes 860168 | tf_op jit(solution)/shard_map/ppermute | solution.py:40
  26.9 13.1 %collective-permute-start.10 = (bf16[160,896]{1,0:T(8,128)(2,1)S(1)}, bf16[160,896]{1,0:T(8,128)(2,1)S(1)}, u32[]{:S(2)}, u32[]{:S(2)}) collective-permute-start(bf16[160,896]{1,0:T(8,128)(2,1)S(1)} %shard_map.114.refs_0_), channel_id=1, source_target_pairs={{0,3},{1,0},{2,1},{3,2},{4,7},{5,4},{6,5},{7,6},{8,11},{9,8},{10,9... | collective-permute-start | bytes 860168 | tf_op jit(solution)/shard_map/ppermute | solution.py:40
  30.4 15.8 %collective-permute-start.7 = (bf16[160,896]{1,0:T(8,128)(2,1)S(1)}, bf16[160,896]{1,0:T(8,128)(2,1)S(1)}, u32[]{:S(2)}, u32[]{:S(2)}) collective-permute-start(bf16[160,896]{1,0:T(8,128)(2,1)S(1)} %collective-permute-done.5.refs_1_), channel_id=1, source_target_pairs={{0,1},{1,2},{2,3},{3,0},{4,5},{5,6},{6,7},{7,4},{8,9},{9,10},{10,1... | collective-permute-start | bytes 860168 | tf_op jit(solution)/shard_map/ppermute | solution.py:40
  31.6 14.5 %collective-permute-start.13 = (bf16[160,896]{1,0:T(8,128)(2,1)S(1)}, bf16[160,896]{1,0:T(8,128)(2,1)S(1)}, u32[]{:S(2)}, u32[]{:S(2)}) collective-permute-start(bf16[160,896]{1,0:T(8,128)(2,1)S(1)} %collective-permute-done.5.refs_1_), channel_id=1, source_target_pairs={{0,3},{1,0},{2,1},{3,2},{4,7},{5,4},{6,5},{7,6},{8,11},{9,8},{10,9... | collective-permute-start | bytes 860168 | tf_op jit(solution)/shard_map/ppermute | solution.py:40
  33.1 13.1 %collective-permute-start.14 = (bf16[160,896]{1,0:T(8,128)(2,1)S(1)}, bf16[160,896]{1,0:T(8,128)(2,1)S(1)}, u32[]{:S(2)}, u32[]{:S(2)}) collective-permute-start(bf16[160,896]{1,0:T(8,128)(2,1)S(1)} %collective-permute-done.8.refs_2_), channel_id=1, source_target_pairs={{0,128},{1,129},{2,130},{3,131},{4,132},{5,133},{6,134},{7,135},{8... | collective-permute-start | bytes 860168 | tf_op jit(solution)/shard_map/ppermute | solution.py:40
  42.6 8.8 %collective-permute-start.12 = (bf16[160,896]{1,0:T(8,128)(2,1)S(1)}, bf16[160,896]{1,0:T(8,128)(2,1)S(1)}, u32[]{:S(2)}, u32[]{:S(2)}) collective-permute-start(bf16[160,896]{1,0:T(8,128)(2,1)S(1)} %get-tuple-element.51), channel_id=1, source_target_pairs={{0,1},{1,2},{2,3},{3,0},{4,5},{5,6},{6,7},{7,4},{8,9},{9,10},{10,1... | collective-permute-start | bytes 860168 | tf_op jit(solution)/shard_map/ppermute | solution.py:40
  44.2 7.3 %collective-permute-start.11 = (bf16[160,896]{1,0:T(8,128)(2,1)S(1)}, bf16[160,896]{1,0:T(8,128)(2,1)S(1)}, u32[]{:S(2)}, u32[]{:S(2)}) collective-permute-start(bf16[160,896]{1,0:T(8,128)(2,1)S(1)} %get-tuple-element.50), channel_id=1, source_target_pairs={{0,3},{1,0},{2,1},{3,2},{4,7},{5,4},{6,5},{7,6},{8,11},{9,8},{10,9... | collective-permute-start | bytes 860168 | tf_op jit(solution)/shard_map/ppermute | solution.py:40
  48.4 6.3 %collective-permute-start.16 = (bf16[160,896]{1,0:T(8,128)(2,1)S(1)}, bf16[160,896]{1,0:T(8,128)(2,1)S(1)}, u32[]{:S(2)}, u32[]{:S(2)}) collective-permute-start(bf16[160,896]{1,0:T(8,128)(2,1)S(1)} %get-tuple-element.56), channel_id=1, source_target_pairs={{0,128},{1,129},{2,130},{3,131},{4,132},{5,133},{6,134},{7,135},{8... | collective-permute-start | bytes 860168 | tf_op jit(solution)/shard_map/ppermute | solution.py:40
  48.5 8.6 %collective-permute-start.17 = (bf16[160,896]{1,0:T(8,128)(2,1)S(1)}, bf16[160,896]{1,0:T(8,128)(2,1)S(1)}, u32[]{:S(2)}, u32[]{:S(2)}) collective-permute-start(bf16[160,896]{1,0:T(8,128)(2,1)S(1)} %get-tuple-element.58), channel_id=1, source_target_pairs={{0,1},{1,2},{2,3},{3,0},{4,5},{5,6},{6,7},{7,4},{8,9},{9,10},{10,1... | collective-permute-start | bytes 860168 | tf_op jit(solution)/shard_map/ppermute | solution.py:40
  49.9 7.3 %collective-permute-start.15 = (bf16[160,896]{1,0:T(8,128)(2,1)S(1)}, bf16[160,896]{1,0:T(8,128)(2,1)S(1)}, u32[]{:S(2)}, u32[]{:S(2)}) collective-permute-start(bf16[160,896]{1,0:T(8,128)(2,1)S(1)} %get-tuple-element.54), channel_id=1, source_target_pairs={{0,3},{1,0},{2,1},{3,2},{4,7},{5,4},{6,5},{7,6},{8,11},{9,8},{10,9... | collective-permute-start | bytes 860168 | tf_op jit(solution)/shard_map/ppermute | solution.py:40
  54.8 9.4 %collective-permute-start.18 = (bf16[160,896]{1,0:T(8,128)(2,1)S(1)}, bf16[160,896]{1,0:T(8,128)(2,1)S(1)}, u32[]{:S(2)}, u32[]{:S(2)}) collective-permute-start(bf16[160,896]{1,0:T(8,128)(2,1)S(1)} %add_convert_fusion.1), channel_id=1, source_target_pairs={{0,2},{1,3},{2,0},{3,1},{4,6},{5,7},{6,4},{7,5},{8,10},{9,11},{10,... | collective-permute-start | bytes 860168 | tf_op jit(solution)/shard_map/ppermute | solution.py:40
  57.3 21.8 %copy-start = (f32[8,256]{1,0:T(8,128)S(1)}, f32[8,256]{1,0:T(8,128)}, u32[]{:S(2)}) copy-start(f32[8,256]{1,0:T(8,128)} %get-tuple-element.63.table_ref) | copy-start | bytes 24580
  57.3 7.0 %collective-permute-start.19 = (bf16[160,896]{1,0:T(8,128)(2,1)S(1)}, bf16[160,896]{1,0:T(8,128)(2,1)S(1)}, u32[]{:S(2)}, u32[]{:S(2)}) collective-permute-start(bf16[160,896]{1,0:T(8,128)(2,1)S(1)} %add_convert_fusion), channel_id=1, source_target_pairs={{0,128},{1,129},{2,130},{3,131},{4,132},{5,133},{6,134},{7,135},{8... | collective-permute-start | bytes 860168 | tf_op jit(solution)/shard_map/ppermute | solution.py:40
  57.9 30.5 %copy-start.2 = (bf16[8,7168]{1,0:T(8,128)(2,1)S(1)}, bf16[8,7168]{1,0:T(8,128)(2,1)}, u32[]{:S(2)}) copy-start(bf16[8,7168]{1,0:T(8,128)(2,1)} %refs_0_.1) | copy-start | bytes 344068
  64.3 10.3 %collective-permute-start.20 = (bf16[40,896]{1,0:T(8,128)(2,1)S(1)}, bf16[40,896]{1,0:T(8,128)(2,1)S(1)}, u32[]{:S(2)}, u32[]{:S(2)}) collective-permute-start(bf16[40,896]{1,0:T(8,128)(2,1)S(1)} %get-tuple-element.66), channel_id=1, source_target_pairs={{0,20},{1,21},{2,22},{3,23},{4,24},{5,25},{6,26},{7,27},{8,28},{9,... | collective-permute-start | bytes 215048 | tf_op jit(solution)/shard_map/ppermute | solution.py:40
  68.9 7.9 %collective-permute-start.21 = (bf16[40,896]{1,0:T(8,128)(2,1)S(1)}, bf16[40,896]{1,0:T(8,128)(2,1)S(1)}, u32[]{:S(2)}, u32[]{:S(2)}) collective-permute-start(bf16[40,896]{1,0:T(8,128)(2,1)S(1)} %get-tuple-element.67), channel_id=1, source_target_pairs={{0,8},{1,9},{2,10},{3,11},{4,12},{5,13},{6,14},{7,15},{8,16},{9,17... | collective-permute-start | bytes 215048 | tf_op jit(solution)/shard_map/ppermute | solution.py:40
  69.1 8.0 %collective-permute-start.22 = (bf16[40,896]{1,0:T(8,128)(2,1)S(1)}, bf16[40,896]{1,0:T(8,128)(2,1)S(1)}, u32[]{:S(2)}, u32[]{:S(2)}) collective-permute-start(bf16[40,896]{1,0:T(8,128)(2,1)S(1)} %get-tuple-element.68), channel_id=1, source_target_pairs={{0,28},{1,29},{2,30},{3,31},{4,0},{5,1},{6,2},{7,3},{8,4},{9,5},{1... | collective-permute-start | bytes 215048 | tf_op jit(solution)/shard_map/ppermute | solution.py:40
  72.7 6.4 %collective-permute-start.23 = (bf16[40,896]{1,0:T(8,128)(2,1)S(1)}, bf16[40,896]{1,0:T(8,128)(2,1)S(1)}, u32[]{:S(2)}, u32[]{:S(2)}) collective-permute-start(bf16[40,896]{1,0:T(8,128)(2,1)S(1)} %get-tuple-element.69), channel_id=1, source_target_pairs={{0,0},{1,1},{2,2},{3,3},{4,4},{5,5},{6,6},{7,7},{8,8},{9,9},{10,10... | collective-permute-start | bytes 215048 | tf_op jit(solution)/shard_map/ppermute | solution.py:40
  79.4 1.4 %collective-permute-start.24 = (bf16[8,7168]{1,0:T(8,128)(2,1)S(1)}, bf16[8,7168]{1,0:T(8,128)(2,1)S(1)}, u32[]{:S(2)}, u32[]{:S(2)}) collective-permute-start(bf16[8,7168]{1,0:T(8,128)(2,1)S(1)} %shard_map.119), channel_id=1, source_target_pairs={{0,64},{1,65},{2,66},{3,67},{4,68},{5,69},{6,70},{7,71},{8,72},{9,... | collective-permute-start | bytes 344072 | tf_op jit(solution)/shard_map/ppermute | solution.py:40
  80.8 7.6 %collective-permute-start.25 = (bf16[8,7168]{1,0:T(8,128)(2,1)S(1)}, bf16[8,7168]{1,0:T(8,128)(2,1)S(1)}, u32[]{:S(2)}, u32[]{:S(2)}) collective-permute-start(bf16[8,7168]{1,0:T(8,128)(2,1)S(1)} %add_convert_fusion.3), channel_id=1, source_target_pairs={{0,128},{1,129},{2,130},{3,131},{4,132},{5,133},{6,134},{7,135},{8... | collective-permute-start | bytes 344072 | tf_op jit(solution)/shard_map/ppermute | solution.py:40
